TPU v7x, 256 devices: a whole 4x4x8 slice. The times are simulated.
256 devices in a mesh: grp: 4 (over z_hi), seq: 16 (over x, z_lo, core), rep: 4 (over y).
Axes of the slice: x: 4, y: 4, z: 8 (z_hi: 4, z_lo: 2; z = z_hi * 2 + z_lo), core: 2. Of those that a mesh axis runs over, the one named last changes fastest.
Arguments:
- hidden: bfloat16 [4, 4, 2048, 3072], P('rep', 'grp', 'seq'), may hold values from -6 to 6
- queries_keys: bfloat16 [4, 4, 2048, 2, 2048], P('rep', 'grp', 'seq'), may hold values from -10 to 10
- values: bfloat16 [4, 4, 2048, 2048], P('rep', 'grp', 'seq'), may hold values from -6 to 6
- text_len: int32 [4, 4], P('rep', 'grp'), may hold values from 64 to 256
- timestep: int32 [4, 4], P('rep', 'grp'), may hold values from 0 to 63
- gate_table: float32 [64, 3072], replicated, may hold values from 0.5 to 1.5
- w_out: bfloat16 [2, 2048, 3072], P(None, 'seq', 'rep'), may hold values from -0.125 to 0.125
- w_zero: bfloat16 [3072, 3072], P('seq', 'grp'), may hold values from -0.109375 to 0.109375
- cotangent: bfloat16 [4, 4, 2048, 3072], P('rep', 'grp', 'seq'), may hold values from -6 to 6
Outputs:
- final: bfloat16 [4, 4, 2048, 3072], P('rep', 'grp', 'seq')
- ctrl_grad: bfloat16 [4, 2048, 3072], P('rep', 'seq', 'grp')
- grad_zero: float32 [3072, 3072], P(('seq', 'rep'), 'grp')
All inputs are finite; a program needn't handle non-finite values.
Results may differ from a plain program's by a relative error of at most 0.019.
Values may be sent and summed in bfloat16 or wider, within the bound.
No kernel may reach another device: no remote copies, remote signals or barrier semaphores. Data moves between devices by JAX's collectives and lax.ppermute only.
A program may use at most 128 MiB of HBM per device.

v0:
```python
import math

import jax
import jax.numpy as jnp
from jax import lax
from jax.sharding import PartitionSpec as P

H = 16
HEAD = 128


def broadcast(value, axis, source):
    kept = jnp.where(lax.axis_index(axis) == source, value, 0).astype(value.dtype)
    return lax.psum(kept, axis)


def shards(hidden, queries_keys, values, text_len, timestep, gate_table, w_out, w_zero, cotangent):
    is_control = lax.axis_index("grp") == 0
    tok_rows = hidden.shape[2]
    seq_count = lax.axis_size("seq")
    length = tok_rows * seq_count
    group_heads = H // seq_count
    text_slots = length // 8
    tlen = text_len[0, 0]
    pair = queries_keys[0, 0].reshape(tok_rows, 2, seq_count, group_heads, HEAD)
    vals = values[0, 0].reshape(tok_rows, 1, seq_count, group_heads, HEAD)
    position = jnp.arange(length)
    valid = (position >= text_slots) | (position < tlen)
    qk_all = lax.all_to_all(pair, "seq", split_axis=2, concat_axis=0, tiled=True)
    v_all = lax.all_to_all(vals, "seq", split_axis=2, concat_axis=0, tiled=True)
    count = qk_all.shape[3]
    keys = qk_all[:, 1, 0]
    vv = v_all[:, 0, 0]
    block = math.gcd(length, 512)
    blocks = qk_all[:, 0, 0].reshape(length // block, block, count, HEAD)

    def one_block(q_block):
        scores = jnp.einsum(
            "bhe,khe->hbk", q_block, keys, preferred_element_type=jnp.float32
        ) * HEAD ** (-0.5)
        scores = jnp.where(valid[None, None, :], scores, -jnp.inf)
        weights = jax.nn.softmax(scores, axis=-1).astype(jnp.bfloat16)
        result = jnp.einsum("hbk,khe->bhe", weights, vv, preferred_element_type=jnp.float32)
        return result.astype(jnp.bfloat16)

    attn_heads = lax.map(one_block, blocks).reshape(length, 1, count, HEAD)
    attn_tok = lax.all_to_all(attn_heads, "seq", split_axis=0, concat_axis=1, tiled=True).reshape(
        tok_rows, H * HEAD
    )
    w_sel = jnp.where(is_control, w_out[0], w_out[1])
    w_cols = lax.all_gather(w_sel, "rep", axis=1, tiled=True)
    columns = attn_tok
    proj = jnp.dot(
        columns,
        lax.all_gather(w_cols, "seq", axis=0, tiled=True),
        preferred_element_type=jnp.float32,
    )
    steps_count = gate_table.shape[0]
    chosen = (jnp.arange(steps_count) == timestep[0, 0])[:, None]
    gate = jnp.sum(jnp.where(chosen, gate_table, 0.0), axis=0)
    out = (hidden[0, 0].astype(jnp.float32) + gate * proj).astype(jnp.bfloat16)
    control = broadcast(out, "grp", 0)
    zero_block = lax.all_gather(w_zero, "seq", axis=0, tiled=True)
    resid_part = jnp.dot(control, zero_block, preferred_element_type=jnp.float32).astype(
        jnp.bfloat16
    )
    resid = lax.all_gather(resid_part, "grp", axis=1, tiled=True)
    final = jnp.where(
        is_control, out, (out.astype(jnp.float32) + resid.astype(jnp.float32)).astype(jnp.bfloat16)
    )
    own_cot = cotangent[0, 0].astype(jnp.float32)
    main_cot = jnp.where(is_control, 0.0, own_cot)
    csum = lax.psum_scatter(main_cot.astype(jnp.bfloat16), "grp", scatter_dimension=1, tiled=True)
    term = jnp.einsum("tc,dc->td", csum, zero_block, preferred_element_type=jnp.float32)
    term = jnp.where(is_control, term + own_cot, term)
    rounded = lax.optimization_barrier(term.astype(jnp.bfloat16))
    ctrl_grad = lax.psum_scatter(
        rounded.astype(jnp.float32).astype(jnp.bfloat16), "grp", scatter_dimension=1, tiled=True
    )
    columns = control
    grad_zero = lax.psum_scatter(
        jnp.einsum("tr,tc->rc", columns, csum, preferred_element_type=jnp.float32),
        ("seq", "rep"),
        scatter_dimension=0,
        tiled=True,
    )
    return (final[None, None], ctrl_grad[None], grad_zero)


def solution(mesh):
    placed = (
        P("rep", "grp", "seq", None),
        P("rep", "grp", "seq", None, None),
        P("rep", "grp", "seq", None),
        P("rep", "grp"),
        P("rep", "grp"),
        P(),
        P(None, "seq", "rep"),
        P("seq", "grp"),
        P("rep", "grp", "seq", None),
    )
    return jax.shard_map(
        shards,
        mesh=mesh,
        in_specs=placed,
        out_specs=(P("rep", "grp", "seq", None), P("rep", "seq", "grp"), P(("seq", "rep"), "grp")),
        check_vma=False,
    )
```

profile of v0, /device:TPU:193, one launch (start us, length us, event | category | flops | bytes accessed | tf_op | source)
XLA Modules:
  0.0 551.1 jit_solution(13238737243371526114)
XLA Ops:
  8.0 0.0 all-gather.7.cloned.1.call-start
  8.1 1.1 slice_select_fusion
  9.2 12.7 %all-gather = bf16[1,128,3072]{2,1,0:T(8,128)(2,1)} all-gather(bf16[1,128,768]{2,1,0:T(8,128)(2,1)S(1)} %slice_select_fusion), channel_id=2, replica_groups=mesh['grp'=4,'seq'=16,'rep'=4] {'rep'}, dimensions={2}, use_global_device_ids=true | all-gather | bytes 983040 | tf_op jit(solution)/shard_map/all_gather | solution.py:51
  21.9 0.0 all-gather.7.cloned.1.call-update
  22.0 0.0 copy-start.1
  22.0 2.1 copy.30
  24.1 7.3 %all-to-all-start.1 = ((bf16[128,1,16,1,128]{0,4,3,1,2:T(8,128)(2,1)}), bf16[128,1,16,1,128]{0,4,3,1,2:T(8,128)(2,1)S(1)}, u32[]{:S(2)}, u32[]{:S(2)}) async-start(bf16[128,1,16,1,128]{0,4,3,1,2:T(8,128)(2,1)} %bitcast.10), calls=%async_computation.1 | async-start | bytes 1048576 | tf_op jit(solution)/shard_map/all_to_all | solution.py:30
  31.4 1.0 copy.27
  32.4 1.3 copy.28
  33.7 8.8 %all-to-all-done.1 = bf16[128,1,16,1,128]{0,4,3,1,2:T(8,128)(2,1)S(1)} async-done(((bf16[128,1,16,1,128]{0,4,3,1,2:T(8,128)(2,1)}), bf16[128,1,16,1,128]{0,4,3,1,2:T(8,128)(2,1)S(1)}, u32[]{:S(2)}, u32[]{:S(2)}) %all-to-all-start.1) | async-done | bytes 524320 | tf_op jit(solution)/shard_map/all_to_all | solution.py:30
  42.5 5.6 %all-to-all-start = ((bf16[128,2,16,1,128]{4,0,1,3,2:T(8,128)(2,1)}), bf16[128,2,16,1,128]{4,0,1,3,2:T(8,128)(2,1)S(1)}, u32[]{:S(2)}, u32[]{:S(2)}) async-start(bf16[128,2,16,1,128]{4,0,1,3,2:T(8,128)(2,1)} %copy.28), calls=%async_computation | async-start | bytes 2097152 | tf_op jit(solution)/shard_map/all_to_all | solution.py:29
  48.1 0.0 reduce-scatter.4.cloned.1.call-start
  48.1 1.0 fusion.28
  49.2 0.0 reduce-scatter.4.cloned.1.call-update
  49.2 0.0 all-gather.5.cloned.1.call-start
  49.3 0.7 all-gather.5.cloned.1.call-update
  50.0 1.0 copy.32
  51.0 26.5 %all-to-all-done = bf16[128,2,16,1,128]{4,0,1,3,2:T(8,128)(2,1)S(1)} async-done(((bf16[128,2,16,1,128]{4,0,1,3,2:T(8,128)(2,1)}), bf16[128,2,16,1,128]{4,0,1,3,2:T(8,128)(2,1)S(1)}, u32[]{:S(2)}, u32[]{:S(2)}) %all-to-all-start) | async-done | bytes 1048608 | tf_op jit(solution)/shard_map/all_to_all | solution.py:29
  77.5 0.1 copy.29
  77.6 0.1 slice_bitcast_fusion
  77.7 16.9 %while.11 = (s32[]{:T(128)}, bf16[4,512,1,128]{3,1,2,0:T(8,128)(2,1)}, bf16[4,512,1,128]{3,1,2,0:T(8,128)(2,1)S(1)}, bf16[2048,1,128]{2,0,1:T(8,128)(2,1)S(1)}, ...) while((s32[]{:T(128)}, bf16[4,512,1,128]{3,1,2,0:T(8,128)(2,1)}, ...), condition=%wide.region_4.5_spmd.clone, body=%wide.region_1.4_spmd.clone.sunk | while | flops 549524480 | bytes 13912161 | solution.py:46
  77.7 0.7 fusion.46
  78.4 0.8 fusion.47
  79.3 0.9 fusion.48
  80.2 1.8 fusion.49
  82.0 0.7 fusion.46
  82.6 0.8 fusion.47
  83.5 0.9 fusion.48
  84.4 1.8 fusion.49
  86.2 0.7 fusion.46
  86.9 0.8 fusion.47
  87.7 0.9 fusion.48
  88.6 1.8 fusion.49
  90.4 0.7 fusion.46
  91.1 0.8 fusion.47
  91.9 0.9 fusion.48
  92.8 1.8 fusion.49
  94.6 0.5 broadcast.33
  95.1 2.1 reduce.4
  97.3 0.9 reshape.68
  98.2 4.3 all-to-all-start.2
  102.4 0.0 all-reduce.2.cloned.1.call-start
  103.2 0.1 select_reduce_fusion
  103.3 15.2 %all-to-all-done.2 = bf16[16,2,8192]{2,1,0:T(2,128)(2,1)S(1)} async-done(((bf16[16,2,8192]{2,1,0:T(2,128)(2,1)}), bf16[16,2,8192]{2,1,0:T(2,128)(2,1)S(1)}, u32[]{:S(2)}, u32[]{:S(2)}) %all-to-all-start.2) | async-done | bytes 524320 | tf_op jit(solution)/shard_map/all_to_all | solution.py:47
  118.5 0.5 reshape.69
  119.0 0.1 copy.36
  119.1 0.3 copy.35
  119.4 10.9 %all-gather.7.cloned.1.call-done = bf16[1,2048,3072]{2,1,0:T(8,128)(2,1)} async-done(((bf16[1,128,3072]{2,1,0:T(8,128)(2,1)}), bf16[1,2048,3072]{2,1,0:T(8,128)(2,1)}) %all-gather.7.cloned.1.call-update) | async-done | bytes 12582928 | tf_op jit(solution)/shard_map/all_gather | solution.py:55
  130.3 7.4 %broadcast_select_fusion = (bf16[128,3072]{1,0:T(8,128)(2,1)}, bf16[128,3072]{1,0:T(8,128)(2,1)S(1)}) fusion(pred[]{:T(512)S(6)} %eq.14, bf16[128,2048]{0,1:T(8,128)(2,1)S(1)} %bitcast.88, bf16[1,2048,3072]{2,1,0:T(8,128)(2,1)} %all-gather.7.cloned.1.call-done, f32[3072]{0:T(1024)S(1)} %select_reduce_fusion, bf16[1,1,128,3072]{3,2,1,0:T(8,128)(2,1)S(1)} %copy-done.3), kind=kOutput, calls=%fused_computation.35 | convolution fusion | flops 1612578816 | bytes 15478785 | tf_op jit(solution)/shard_map/dot_general | solution.py:53
  137.7 0.0 all-reduce.2.cloned.1.call-update
  137.7 0.0 reduce-scatter.6.cloned.1.call-start
  137.8 0.0 reduce-scatter.4.cloned.1.call-done
  137.8 46.0 %all-gather.5.cloned.1.call-done = bf16[3072,768]{1,0:T(8,128)(2,1)} async-done(((bf16[192,768]{1,0:T(8,128)(2,1)}), bf16[3072,768]{1,0:T(8,128)(2,1)}) %all-gather.5.cloned.1.call-update) | async-done | bytes 4718608 | tf_op jit(solution)/shard_map/all_gather | solution.py:63
  183.8 5.1 fusion.29
  188.9 0.0 reduce-scatter.6.cloned.1.call-update
  188.9 0.0 reduce-scatter.8.cloned.1.call-start
  189.0 12.7 %all-reduce.2.cloned.1.call-done = bf16[128,3072]{1,0:T(8,128)(2,1)} async-done(((bf16[128,3072]{1,0:T(8,128)(2,1)}), bf16[128,3072]{1,0:T(8,128)(2,1)}) %all-reduce.2.cloned.1.call-update) | async-done | bytes 786448 | tf_op jit(solution)/shard_map/psum | solution.py:14
  201.7 6.2 %fusion.32 = f32[3072,768]{1,0:T(8,128)} fusion(bf16[128,3072]{1,0:T(8,128)(2,1)} %all-reduce.2.cloned.1.call-done, bf16[128,768]{1,0:T(8,128)(2,1)S(1)} %copy-done.4), kind=kOutput, calls=%fused_computation.39 | convolution fusion | flops 603979776 | bytes 10420224 | tf_op jit(solution)/shard_map/tr,tc->rc/dot_general | solution.py:82
  207.9 0.0 reduce-scatter.8.cloned.1.call-update
  207.9 1.1 copy-done
  209.0 3.1 convolution_convert_fusion
  212.1 29.8 %all_gather.15 = bf16[128,3072]{1,0:T(8,128)(2,1)S(1)} all-gather(bf16[128,768]{1,0:T(8,128)(2,1)S(1)} %convolution_convert_fusion), channel_id=1, replica_groups=mesh['grp'=4,'seq'=16,'rep'=4] {'grp'}, dimensions={1}, use_global_device_ids=true | all-gather | bytes 983040 | tf_op jit(solution)/shard_map/all_gather | solution.py:67
  241.9 1.1 fusion.31
  243.0 300.5 %reduce-scatter.8.cloned.1.call-done = f32[48,768]{1,0:T(8,128)} async-done(((f32[3072,768]{1,0:T(8,128)}), f32[48,768]{1,0:T(8,128)}) %reduce-scatter.8.cloned.1.call-update) | async-done | bytes 147472 | tf_op jit(solution)/shard_map/reduce_scatter | solution.py:81
  (15 shorter events, 0.0 us)
Async XLA Ops:
  8.0 23.4 %copy-start.2 = (bf16[1,1,128,2,2048]{4,3,2,1,0:T(2,128)(2,1)S(1)}, bf16[1,1,128,2,2048]{4,3,2,1,0:T(2,128)(2,1)}, u32[]{:S(2)}) copy-start(bf16[1,1,128,2,2048]{4,3,2,1,0:T(2,128)(2,1)} %param.12) | copy-start | bytes 3145732
  8.0 122.3 %all-gather.7.cloned.1.call-start = ((), (), s32[]{:S(2)}) async-start(), calls=%async_computation.11 | async-start | bytes 13369344 | tf_op jit(solution)/shard_map/all_gather | solution.py:55
  22.0 26.2 %copy-start.1 = (bf16[1,1,128,3072]{3,2,1,0:T(8,128)(2,1)S(1)}, bf16[1,1,128,3072]{3,2,1,0:T(8,128)(2,1)}, u32[]{:S(2)}) copy-start(bf16[1,1,128,3072]{3,2,1,0:T(8,128)(2,1)} %param.19) | copy-start | bytes 2359300
  24.1 18.5 %all-to-all-start.1 = ((bf16[128,1,16,1,128]{0,4,3,1,2:T(8,128)(2,1)}), bf16[128,1,16,1,128]{0,4,3,1,2:T(8,128)(2,1)S(1)}, u32[]{:S(2)}, u32[]{:S(2)}) async-start(bf16[128,1,16,1,128]{0,4,3,1,2:T(8,128)(2,1)} %bitcast.10), calls=%async_computation.1 | async-start | bytes 1048576 | tf_op jit(solution)/shard_map/all_to_all | solution.py:30
  42.5 34.9 %all-to-all-start = ((bf16[128,2,16,1,128]{4,0,1,3,2:T(8,128)(2,1)}), bf16[128,2,16,1,128]{4,0,1,3,2:T(8,128)(2,1)S(1)}, u32[]{:S(2)}, u32[]{:S(2)}) async-start(bf16[128,2,16,1,128]{4,0,1,3,2:T(8,128)(2,1)} %copy.28), calls=%async_computation | async-start | bytes 2097152 | tf_op jit(solution)/shard_map/all_to_all | solution.py:29
  48.1 89.7 %reduce-scatter.4.cloned.1.call-start = ((), (), s32[]{:S(2)}) async-start(), calls=%async_computation.8 | async-start | bytes 983040 | tf_op jit(solution)/shard_map/reduce_scatter | solution.py:73
  49.2 134.6 %all-gather.5.cloned.1.call-start = ((), (), s32[]{:S(2)}) async-start(), calls=%async_computation.7 | async-start | bytes 5013504 | tf_op jit(solution)/shard_map/all_gather | solution.py:63
  51.0 26.7 %copy-start.6 = (bf16[128,1,16,1,128]{4,0,2,3,1:T(8,128)(2,1)S(1)}, bf16[128,1,16,1,128]{4,0,2,3,1:T(8,128)(2,1)}, u32[]{:S(2)}) copy-start(bf16[128,1,16,1,128]{4,0,2,3,1:T(8,128)(2,1)} %copy.32) | copy-start | bytes 1572868
  77.7 25.5 %copy-start.5 = (f32[64,3072]{1,0:T(8,128)S(1)}, f32[64,3072]{1,0:T(8,128)}, u32[]{:S(2)}) copy-start(f32[64,3072]{1,0:T(8,128)} %param.16) | copy-start | bytes 2359300
  94.6 35.6 %copy-start.3 = (bf16[1,1,128,3072]{3,2,1,0:T(8,128)(2,1)S(1)}, bf16[1,1,128,3072]{3,2,1,0:T(8,128)(2,1)}, u32[]{:S(2)}) copy-start(bf16[1,1,128,3072]{3,2,1,0:T(8,128)(2,1)} %param.11) | copy-start | bytes 2359300
  98.2 20.3 %all-to-all-start.2 = ((bf16[16,2,8192]{2,1,0:T(2,128)(2,1)}), bf16[16,2,8192]{2,1,0:T(2,128)(2,1)S(1)}, u32[]{:S(2)}, u32[]{:S(2)}) async-start(bf16[16,2,8192]{2,1,0:T(2,128)(2,1)} %reshape.68), calls=%async_computation.2 | async-start | bytes 1048576 | tf_op jit(solution)/shard_map/all_to_all | solution.py:47
  102.4 99.2 %all-reduce.2.cloned.1.call-start = ((), (), s32[]{:S(2)}) async-start(), calls=%async_computation.6 | async-start | bytes 1572864 | tf_op jit(solution)/shard_map/psum | solution.py:14
  137.7 105.3 %reduce-scatter.6.cloned.1.call-start = ((), (), s32[]{:S(2)}) async-start(), calls=%async_computation.9 | async-start | bytes 983040 | tf_op jit(solution)/shard_map/reduce_scatter | solution.py:77
  137.8 63.8 %copy-start.4 = (bf16[128,768]{1,0:T(8,128)(2,1)S(1)}, bf16[128,768]{1,0:T(8,128)(2,1)}, u32[]{:S(2)}) copy-start(bf16[128,768]{1,0:T(8,128)(2,1)} %reduce-scatter.4.cloned.1.call-done) | copy-start | bytes 589828
  188.9 354.6 %reduce-scatter.8.cloned.1.call-start = ((), (), s32[]{:S(2)}) async-start(), calls=%async_computation.10 | async-start | bytes 9584640 | tf_op jit(solution)/shard_map/reduce_scatter | solution.py:81
  207.8 1.1 copy-start
Sparse Core Ops, SparseCore 0:
  22.1 108.1 all-gather.6
  132.1 51.6 all-gather.4
Sparse Core Ops, SparseCore 1:
  51.1 49.3 reduce-scatter.3
  137.8 63.8 all-reduce.1
  204.7 38.1 reduce-scatter.5
  246.0 297.5 reduce-scatter.7
where the time goes:
time: 559 us; the launch traced here: 551 us
  waiting for transfers between devices  421 us (75%)
  blocking collectives  42.5 us (8%)
  matrix products  32.3 us (6%)
  starting transfers between devices  17.3 us (3%)
  between operations  16.5 us (3%)
  other arithmetic  12 us (2%)
  local copies, waits for them, and re-layouts  9.14 us (2%)
    reduce_scatter x1, waiting for transfers between devices, shards(): lax.psum_scatter(jnp.einsum('tr,tc->rc', columns, csum, preferred_element...  301 us
    all_gather x1, waiting for transfers between devices, shards(): zero_block = lax.all_gather(w_zero, 'seq', axis=0, tiled=True)  46 us
    all_gather x1, blocking collectives, shards(): resid = lax.all_gather(resid_part, 'grp', axis=1, tiled=True)  29.8 us
    all_to_all x1, waiting for transfers between devices, shards(): lax.all_to_all(pair, 'seq', split_axis=2, concat_axis=0, tiled=True)  26.5 us
    all_to_all x1, waiting for transfers between devices, shards(): lax.all_to_all(attn_heads, 'seq', split_axis=0, concat_axis=1, tiled=True)  15.2 us
    all_gather x1, blocking collectives, shards(): w_cols = lax.all_gather(w_sel, 'rep', axis=1, tiled=True)  12.7 us
    psum x1, waiting for transfers between devices, broadcast(): return lax.psum(kept, axis)  12.7 us
  transfers between devices with their start and end apart: 9, of which 7 were waited for; matrix products, arithmetic and copies ran while one was open for 9% of the time, Pallas kernels for 0%

commit v1 on v0

v1 whole, which is shorter than its diff:
```python
import functools
import math

import jax
import jax.numpy as jnp
from jax import lax
from jax.experimental import pallas as pl
from jax.experimental.pallas import tpu as pltpu
from jax.sharding import Mesh, PartitionSpec as P

H = 16
HEAD = 128
SIZES = {"grp": 4, "x": 4, "zl": 2, "core": 2, "rep": 4}
SEQ = ("x", "zl", "core")
BF = jnp.bfloat16
F32 = jnp.float32
MIB = 1 << 20


def send(value, axis, pairs):
    return lax.ppermute(value, axis, pairs)


def shift(value, axis, step):
    n = SIZES[axis]
    return lax.ppermute(value, axis, [(i, (i + step) % n) for i in range(n)])


def attend_kernel(tlen_ref, q_ref, k_ref, v_ref, o_ref, wide_ref, *, text_slots, scale):
    @pl.when(pl.program_id(0) == 0)
    def _():
        length = wide_ref.shape[0]
        wide_ref[:, :HEAD] = v_ref[...].reshape(length, HEAD)
        wide_ref[:, HEAD:] = jnp.ones((length, HEAD), BF)

    rows = o_ref.shape[0]
    q = q_ref[...].reshape(rows, HEAD)
    length = wide_ref.shape[0]
    k = k_ref[...].reshape(length, HEAD)
    s = lax.dot_general(q, k, (((1,), (1,)), ((), ())), preferred_element_type=F32)
    place = lax.broadcasted_iota(jnp.int32, (rows, text_slots), 1)
    head = jnp.where(place < tlen_ref[0, 0], s[:, :text_slots], -jnp.inf)
    tail = s[:, text_slots:]
    top = jnp.maximum(
        jnp.max(head, axis=1, keepdims=True), jnp.max(tail, axis=1, keepdims=True)
    )
    factor = scale * math.log2(math.e)
    p_head = jnp.exp2((head - top) * factor).astype(BF)
    p_tail = jnp.exp2((tail - top) * factor).astype(BF)
    both = jnp.dot(p_head, wide_ref[:text_slots, :], preferred_element_type=F32) + jnp.dot(
        p_tail, wide_ref[text_slots:, :], preferred_element_type=F32
    )
    o_ref[...] = (both[:, :HEAD] / both[:, HEAD:]).astype(BF)


def attend(qkv, tlen):
    blocks, _, per, _ = qkv.shape
    length = blocks * per
    q_blocks = 2
    rows = q_blocks * per
    whole = lambda part: pl.BlockSpec((blocks, None, per, HEAD), lambda i: (0, part, 0, 0))
    return pl.pallas_call(
        functools.partial(attend_kernel, text_slots=length // 8, scale=HEAD ** -0.5),
        grid=(length // rows,),
        in_specs=[
            pl.BlockSpec(memory_space=pltpu.SMEM),
            pl.BlockSpec((q_blocks, None, per, HEAD), lambda i: (i, 0, 0, 0)),
            whole(1),
            whole(2),
        ],
        out_specs=pl.BlockSpec((rows, HEAD), lambda i: (i, 0)),
        out_shape=jax.ShapeDtypeStruct((length, HEAD), BF),
        scratch_shapes=[pltpu.VMEM((length, 2 * HEAD), BF)],
        compiler_params=pltpu.CompilerParams(vmem_limit_bytes=40 * MIB),
        cost_estimate=pl.CostEstimate(
            flops=6 * length * length * HEAD,
            bytes_accessed=8 * length * HEAD,
            transcendentals=length * length,
        ),
        name="attend",
    )(tlen, qkv, qkv, qkv)


def project_kernel(place_ref, a_ref, y0, y1, y3, y2a, y2b, x0, x1, x3, x2a, x2b, own_ref, other_ref, wide_ref):
    half = own_ref.shape[0]
    x, zl, core, rep = place_ref[0], place_ref[1], place_ref[2], place_ref[3]
    mine = pl.multiple_of(core * half, half)
    theirs = pl.multiple_of((1 - core) * half, half)
    for at, step in enumerate((0, 1, 3, 2)):
        for other_zl in range(2):
            head = lax.rem(x + 4 - step, 4) * 2 + (1 - zl if other_zl else zl)
            lanes = slice((2 * at + other_zl) * HEAD, (2 * at + other_zl + 1) * HEAD)
            wide_ref[:half, lanes] = a_ref[head, pl.ds(mine, half), :]
            wide_ref[half:, lanes] = a_ref[head, pl.ds(theirs, half), :]
    wide_y, wide_x, depth = y0.shape[1], x0.shape[2], x0.shape[1]
    block = wide_y + wide_x

    def times(lanes, w):
        return jnp.dot(wide_ref[:, lanes], w, preferred_element_type=F32)

    for at, step in enumerate((0, 1, 3, 2)):
        start = lax.rem(rep + 4 - step, 4) * block
        if step == 2:
            deep = y2a.shape[0]
            total = times(slice(0, deep), y2a[...]) + times(slice(deep, 2 * deep), y2b[...])
        else:
            total = times(slice(None), (y0, y1, None, y3)[step][...])
        place = pl.ds(pl.multiple_of(start, HEAD), wide_y)
        own_ref[:, place] = total[:half]
        other_ref[:, place] = total[half:].astype(BF)
        total = 0.0
        for k, piece in enumerate((x0, x1, x3)):
            total = total + times(slice(k * depth, (k + 1) * depth), piece[at])
        far = x2a[at] if at < 2 else x2b[at - 2]
        total = total + times(slice(3 * depth, 4 * depth), far)
        place = pl.ds(pl.multiple_of(start + wide_y, HEAD), wide_x)
        own_ref[:, place] = total[:half]
        other_ref[:, place] = total[half:].astype(BF)


def project(place, attn, by_y, by_x):
    heads, rows, _ = attn.shape
    half = rows // 2
    columns = 4 * (by_y[0].shape[1] + by_x[0].shape[2])
    vmem = pl.BlockSpec(memory_space=pltpu.VMEM)
    return pl.pallas_call(
        project_kernel,
        in_specs=[pl.BlockSpec(memory_space=pltpu.SMEM)] + [vmem] * 11,
        out_specs=[vmem, vmem],
        out_shape=[
            jax.ShapeDtypeStruct((half, columns), F32),
            jax.ShapeDtypeStruct((half, columns), BF),
        ],
        scratch_shapes=[pltpu.VMEM((rows, heads * HEAD), BF)],
        compiler_params=pltpu.CompilerParams(vmem_limit_bytes=40 * MIB),
        cost_estimate=pl.CostEstimate(
            flops=2 * rows * heads * HEAD * columns,
            bytes_accessed=2 * heads * HEAD * columns,
            transcendentals=0,
        ),
        name="project",
    )(place, attn, *by_y, *by_x)


def ring_gather(value, axis, split):
    below, above = shift(value, axis, 1), shift(value, axis, -1)
    far_a = shift(below[:split], axis, 1)
    far_b = shift(above[split:], axis, -1)
    return value, below, above, far_a, far_b


def gate(*values):
    return lax.optimization_barrier(values)


def grad_kernel(c0, c1, c2, c3, s0, s1, s2, s3, o_ref, ctl_ref, sum_ref):
    rows = c0.shape[0]
    for at, (c, s) in enumerate(((c0, s0), (c1, s1), (c2, s2), (c3, s3))):
        ctl_ref[at * rows : (at + 1) * rows, :] = c[...]
        sum_ref[at * rows : (at + 1) * rows, :] = s[...]
    o_ref[...] = lax.dot_general(
        ctl_ref[...], sum_ref[...], (((0,), (0,)), ((), ())), preferred_element_type=F32
    ).astype(BF)


def grad_partial(ctl, csum):
    rows, width = ctl[0].shape
    vmem = pl.BlockSpec(memory_space=pltpu.VMEM)
    return pl.pallas_call(
        grad_kernel,
        in_specs=[vmem] * 8,
        out_specs=vmem,
        out_shape=jax.ShapeDtypeStruct((width, width), BF),
        scratch_shapes=[pltpu.VMEM((4 * rows, width), BF)] * 2,
        compiler_params=pltpu.CompilerParams(vmem_limit_bytes=40 * MIB),
        cost_estimate=pl.CostEstimate(
            flops=8 * rows * width * width, bytes_accessed=18 * rows * width, transcendentals=0
        ),
        name="grad_partial",
    )(*ctl, *csum)


def pick(blocks, index):
    return lax.dynamic_index_in_dim(blocks, index, 0, keepdims=False)


def shards(hidden, queries_keys, values, text_len, timestep, gate_table, w_out, w_zero, cotangent):
    g = lax.axis_index("grp")
    x = lax.axis_index("x")
    core = lax.axis_index("core")
    rep = lax.axis_index("rep")
    zl = lax.axis_index("zl")
    is_control = g == 0
    n_grp, n_x, n_rep = SIZES["grp"], SIZES["x"], SIZES["rep"]
    tok, width = hidden.shape[2], w_zero.shape[1]

    w_sel = jnp.where(is_control, w_out[0], w_out[1])
    pair = queries_keys[0, 0].reshape(tok, 2, H, HEAD).transpose(2, 1, 0, 3)
    vals = values[0, 0].reshape(tok, 1, H, HEAD).transpose(2, 1, 0, 3)
    qkv, w_pair = gate(
        jnp.concatenate([pair, vals], axis=1), jnp.concatenate([w_sel, shift(w_sel, "zl", 1)])
    )

    wide = 512
    first, second = w_pair[:, :wide], w_pair[:, wide:]
    qkv = lax.all_to_all(qkv, SEQ, split_axis=0, concat_axis=0, tiled=True)
    over_x = [first] + [shift(first, "x", step) for step in (1, 3, 2)]
    over_y = [second] + [shift(second, "rep", step) for step in (1, 3, 2)]
    qkv, over_x, over_y, cot, zero_own = gate(qkv, over_x, over_y, cotangent[0, 0], w_zero)

    zero_block = lax.all_gather(zero_own, SEQ, axis=0, tiled=True)
    over_x, over_y = jnp.concatenate(over_x), jnp.stack(over_y)
    by_y = ring_gather(over_x, "rep", over_x.shape[0] // 2)
    by_x = ring_gather(over_y, "x", over_y.shape[0] // 2)

    def cot_block(index):
        return lax.dynamic_slice_in_dim(cot, index * width, width, axis=1)

    csum = jnp.where(is_control, 0.0, cot_block(g).astype(F32))
    for step in range(1, n_grp):
        pairs = [(i, (i + step) % n_grp) for i in range(1, n_grp)]
        got = send(cot_block((g + step) % n_grp), "grp", pairs)
        csum = csum + got.astype(F32)
    attn, csum = gate(attend(qkv, text_len), csum.astype(BF))

    heads = lax.all_to_all(
        attn.reshape(8, 2 * tok, HEAD), ("x", "zl"), split_axis=0, concat_axis=0, tiled=True
    )
    own, other = project(jnp.stack([x, zl, core, rep]), heads, by_y, by_x)
    other = shift(other, "core", 1)
    level = lax.dynamic_slice_in_dim(gate_table, timestep[0, 0], 1, axis=0)
    out = (hidden[0, 0].astype(F32) + level * (own + other.astype(F32))).astype(BF)

    out, csum = gate(out, csum)
    top, low = out[: tok // 2], out[tok // 2 :]
    csum_x = [csum] + [shift(csum, "x", step) for step in range(1, n_x)]
    right = send(top, "grp", [(0, 1)])
    left = send(low, "grp", [(0, 3)])
    right, left, top, low = gate(right, left, top, low)
    low_far = send(jnp.where(is_control, low, left), "grp", [(0, 1), (3, 2)])
    top_far = send(jnp.where(is_control, top, right), "grp", [(0, 3), (1, 2)])
    low_far, top_far, csum_x, zero_block = gate(low_far, top_far, csum_x, zero_block)
    control = jnp.concatenate(
        [
            jnp.where(is_control, top, jnp.where(g == 1, right, top_far)),
            jnp.where(is_control, low, jnp.where(g == 3, left, low_far)),
        ]
    )

    resid = jnp.dot(control, zero_block, preferred_element_type=F32).astype(BF)
    resid, control = gate(resid, control)
    parts = [resid] + [
        send(resid, "grp", [(i, (i + step) % n_grp) for i in range(n_grp) if (i + step) % n_grp])
        for step in range(1, n_grp)
    ]
    columns = []
    for j in range(n_grp):
        block = parts[0]
        for step in range(1, n_grp):
            block = jnp.where((g - step) % n_grp == j, parts[step], block)
        columns.append(block)
    resid_all = jnp.concatenate(columns, axis=1)
    final = jnp.where(is_control, out, (out.astype(F32) + resid_all.astype(F32)).astype(BF))

    def ctl_block(index):
        return lax.dynamic_slice_in_dim(control, index * width, width, axis=1)

    ctl_x = [ctl_block(x)] + [
        shift(ctl_block((x + step) % n_x), "x", step) for step in range(1, n_x)
    ]
    partial = grad_partial(ctl_x, csum_x)
    partial, csum = gate(partial, csum)
    term = lax.dot_general(csum, zero_block, (((1,), (1,)), ((), ())), preferred_element_type=F32)
    term = jnp.where(is_control, term + cotangent[0, 0].astype(F32), term).astype(BF)

    def term_block(index):
        return lax.dynamic_slice_in_dim(term, index * width, width, axis=1)

    ctrl = term_block(g).astype(F32)
    for step in range(1, n_grp):
        ctrl = ctrl + shift(term_block((g + step) % n_grp), "grp", step).astype(F32)
    ctrl_grad = ctrl.astype(BF)

    rows = width // 16
    partial = partial.reshape(2, 2, n_rep * rows, width).transpose(1, 0, 2, 3)
    mine = pick(partial, core).astype(F32)
    got = shift(pick(partial, 1 - core), "core", 1)
    over_rep = (mine + got.astype(F32)).reshape(2, n_rep, rows, width).transpose(1, 0, 2, 3)
    grad = pick(over_rep, rep)
    for step in range(1, n_rep):
        got = shift(pick(over_rep, (rep + step) % n_rep).astype(BF), "rep", step)
        grad = grad + got.astype(F32)
    mine = pick(grad, zl)
    got = shift(pick(grad, 1 - zl).astype(BF), "zl", 1)
    grad_zero = mine + got.astype(F32)
    return (final[None, None], ctrl_grad[None], grad_zero)


def solution(mesh):
    split = Mesh(mesh.devices.reshape(4, 4, 2, 2, 4), ("grp", "x", "zl", "core", "rep"))
    placed = (
        P("rep", "grp", SEQ, None),
        P("rep", "grp", SEQ, None, None),
        P("rep", "grp", SEQ, None),
        P("rep", "grp"),
        P("rep", "grp"),
        P(),
        P(None, SEQ, "rep"),
        P(SEQ, "grp"),
        P("rep", "grp", SEQ, None),
    )
    return jax.shard_map(
        shards,
        mesh=split,
        in_specs=placed,
        out_specs=(P("rep", "grp", SEQ, None), P("rep", SEQ, "grp"), P((*SEQ, "rep"), "grp")),
        check_vma=False,
    )
```

time: 559 us -> 258 us (0.46)
  the two profiles are of different devices: /device:TPU:193 before, /device:TPU:112 now
where the time goes in v1:
time: 258 us; the launch traced here: 257 us
  waiting for transfers between devices  119 us (46%)
  starting transfers between devices  66.7 us (26%)
  local copies, waits for them, and re-layouts  21.2 us (8%)
  Pallas kernels  16.7 us (6%)
  between operations  15.9 us (6%)
  other arithmetic  13.3 us (5%)
  matrix products  4.77 us (2%)
    ppermute x30, waiting for transfers between devices, shift(): return lax.ppermute(value, axis, [(i, (i + step) % n) for i in range(n)])  70.5 us
    ppermute x10, waiting for transfers between devices, send(): return lax.ppermute(value, axis, pairs)  48.1 us
    ppermute x30, starting transfers between devices, shift(): return lax.ppermute(value, axis, [(i, (i + step) % n) for i in range(n)])  36.1 us
    ppermute x10, starting transfers between devices, send(): return lax.ppermute(value, axis, pairs)  21.2 us
    unnamed x43, local copies, waits for them, and re-layouts  13 us
    pallas_call x1, Pallas kernels, attend(): pl.pallas_call(functools.partial(attend_kernel, text_slots=length // 8, s...  11.6 us
    all_to_all x1, starting transfers between devices, shards(): qkv = lax.all_to_all(qkv, SEQ, split_axis=0, concat_axis=0, tiled=True)  5.88 us
  transfers between devices with their start and end apart: 43, of which 20 were waited for; matrix products, arithmetic and copies ran while one was open for 11% of the time, Pallas kernels for 7%

profile of v1, /device:TPU:112, one launch (start us, length us, event | category | flops | bytes accessed | tf_op | source)
XLA Modules:
  0.0 257.2 jit_solution(11401222795273787193)
XLA Ops:
  7.2 1.1 select_bitcast_fusion
  8.5 2.5 copy.12
  11.7 1.3 copy.14
  13.3 1.3 pad_maximum_fusion
  15.1 5.9 %all-to-all-start = ((bf16[16,3,128,128]{3,2,1,0:T(8,128)(2,1)}), bf16[16,3,128,128]{3,2,1,0:T(8,128)(2,1)S(1)}, u32[]{:S(2)}, u32[]{:S(2)}) async-start(bf16[16,3,128,128]{3,2,1,0:T(8,128)(2,1)} %pad_maximum_fusion), calls=%async_computation | async-start | bytes 3145728 | tf_op jit(solution)/shard_map/all_to_all | solution.py:206
  21.0 1.4 collective-permute-start.4
  22.4 1.5 collective-permute-start.1
  23.9 1.8 collective-permute-start.2
  25.7 1.8 collective-permute-start.3
  28.2 1.5 collective-permute-start.6
  29.8 3.5 %collective-permute-done.5 = bf16[256,256]{1,0:T(8,128)(2,1)S(1)} collective-permute-done((bf16[256,256]{1,0:T(8,128)(2,1)S(1)}, bf16[256,256]{1,0:T(8,128)(2,1)S(1)}, u32[]{:S(2)}, u32[]{:S(2)}) %collective-permute-start.5) | collective-permute-done | bytes 131104 | tf_op jit(solution)/shard_map/ppermute | solution.py:26
  33.3 1.4 collective-permute-done.6
  34.7 12.6 %collective-permute-done.1 = bf16[256,512]{1,0:T(8,128)(2,1)S(1)} collective-permute-done((bf16[256,512]{1,0:T(8,128)(2,1)S(1)}, bf16[256,512]{1,0:T(8,128)(2,1)S(1)}, u32[]{:S(2)}, u32[]{:S(2)}) %collective-permute-start.1) | collective-permute-done | bytes 262176 | tf_op jit(solution)/shard_map/ppermute | solution.py:26
  47.3 6.1 %collective-permute-done.3 = bf16[256,512]{1,0:T(8,128)(2,1)} collective-permute-done((bf16[256,512]{1,0:T(8,128)(2,1)S(1)}, bf16[256,512]{1,0:T(8,128)(2,1)}, u32[]{:S(2)}, u32[]{:S(2)}) %collective-permute-start.3) | collective-permute-done | bytes 262176 | tf_op jit(solution)/shard_map/ppermute | solution.py:26
  56.3 1.7 constant_dynamic-update-slice_fusion.y0
  58.0 1.3 collective-permute-start.10
  60.0 1.2 constant_dynamic-slice_fusion.9
  61.2 5.9 %collective-permute-start.7 = (bf16[128,768]{1,0:T(8,128)(2,1)S(1)}, bf16[128,768]{1,0:T(8,128)(2,1)S(1)}, u32[]{:S(2)}, u32[]{:S(2)}) collective-permute-start(bf16[128,768]{1,0:T(8,128)(2,1)S(1)} %get-tuple-element.87), channel_id=1, source_target_pairs={{64,128},{128,192},{192,0},{65,129},{129,193},{193,1},{66,130},{13... | collective-permute-start | bytes 589832 | tf_op jit(solution)/shard_map/ppermute | solution.py:21
  67.1 2.8 %collective-permute-start.8 = (bf16[128,768]{1,0:T(8,128)(2,1)S(1)}, bf16[128,768]{1,0:T(8,128)(2,1)S(1)}, u32[]{:S(2)}, u32[]{:S(2)}) collective-permute-start(bf16[128,768]{1,0:T(8,128)(2,1)S(1)} %get-tuple-element.89), channel_id=1, source_target_pairs={{64,192},{128,0},{192,64},{65,193},{129,1},{193,65},{66,194},{130,... | collective-permute-start | bytes 589832 | tf_op jit(solution)/shard_map/ppermute | solution.py:21
  70.0 1.9 collective-permute-start.9
  71.9 1.4 copy-done.5
  73.3 11.6 %attend.1 = bf16[2048,128]{1,0:T(8,128)(2,1)S(1)} custom-call(s32[1,1]{1,0:T(1,128)S(6)} %copy.25.tlen_ref, bf16[16,3,128,128]{3,2,1,0:T(8,128)(2,1)S(1)} %copy-done.5, bf16[16,3,128,128]{3,2,1,0:T(8,128)(2,1)S(1)} %copy-done.5, bf16[16,3,128,128]{3,2,1,0:T(8,128)(2,1)S(1)} %copy-done.5), custom_call_target="tpu_custom_call" | custom-call | flops 3221225472 | bytes 2097152 | tf_op jit(solution)/shard_map/attend/pallas_call | solution.py:62
  84.9 1.3 collective-permute-done.8
  86.2 9.9 %collective-permute-done.9 = bf16[128,768]{1,0:T(8,128)(2,1)S(1)} collective-permute-done((bf16[128,768]{1,0:T(8,128)(2,1)S(1)}, bf16[128,768]{1,0:T(8,128)(2,1)S(1)}, u32[]{:S(2)}, u32[]{:S(2)}) %collective-permute-start.9) | collective-permute-done | bytes 196640 | tf_op jit(solution)/shard_map/ppermute | solution.py:21
  96.1 1.7 add_convert_fusion.2.s0
  97.9 3.5 %all-to-all-start.1 = ((bf16[8,256,128]{2,1,0:T(8,128)(2,1)}), bf16[8,256,128]{2,1,0:T(8,128)(2,1)S(1)}, u32[]{:S(2)}, u32[]{:S(2)}) async-start(bf16[8,256,128]{2,1,0:T(8,128)(2,1)} %bitcast.67), calls=%async_computation.1 | async-start | bytes 1048576 | tf_op jit(solution)/shard_map/all_to_all | solution.py:226
  101.3 1.1 pad_maximum_fusion.2.x0
  102.5 1.5 collective-permute-start.14
  103.9 1.8 collective-permute-start.15
  106.7 1.3 collective-permute-start.12
  109.6 11.7 %collective-permute-done.14.x1 = bf16[4,256,256]{2,1,0:T(8,128)(2,1)S(1)} collective-permute-done((bf16[4,256,256]{2,1,0:T(8,128)(2,1)S(1)}, bf16[4,256,256]{2,1,0:T(8,128)(2,1)S(1)}, u32[]{:S(2)}, u32[]{:S(2)}) %collective-permute-start.14) | collective-permute-done | bytes 524320 | tf_op jit(solution)/shard_map/ppermute | solution.py:26
  122.0 2.5 collective-permute-start.16
  126.2 5.0 %collective-permute-done.16.x2a = bf16[2,256,256]{2,1,0:T(8,128)(2,1)} collective-permute-done((bf16[2,256,256]{2,1,0:T(8,128)(2,1)}, bf16[2,256,256]{2,1,0:T(8,128)(2,1)}, u32[]{:S(2)}, u32[]{:S(2)}) %collective-permute-start.16) | collective-permute-done | bytes 262176 | tf_op jit(solution)/shard_map/ppermute | solution.py:26
  131.2 1.9 collective-permute-done.17.x2b
  133.1 1.0 copy-done.2
  134.1 1.0 copy-done.8
  135.2 1.0 copy-done.10
  136.2 4.4 %project.1 = (f32[128,3072]{1,0:T(8,128)S(1)}, bf16[128,3072]{1,0:T(8,128)(2,1)}) custom-call(s32[4]{0:T(128)S(1)} %pad_add_fusion.place_ref, bf16[8,256,128]{2,1,0:T(8,128)(2,1)S(1)} %all-to-all-done.1.a_ref, bf16[1024,512]{1,0:T(8,128)(2,1)} %constant_dynamic-update-slice_fusion.y0, bf16[1024,512]{1,0:T(8,128)(2,1)S(1)} %collective-permute-done.10.y1, ...), custom_call_target="tpu_custom_call" | custom-call | flops 1610612736 | bytes 6291456 | tf_op jit(solution)/shard_map/project/pallas_call | solution.py:126
  140.6 1.2 copy-done.6
  142.4 1.8 collective-permute-done.18
  144.2 1.9 fusion.1
  146.2 1.4 collective-permute-start.19
  148.3 20.5 %collective-permute-done.19 = bf16[64,3072]{1,0:T(8,128)(2,1)S(1)} collective-permute-done((bf16[64,3072]{1,0:T(8,128)(2,1)S(1)}, bf16[64,3072]{1,0:T(8,128)(2,1)S(1)}, u32[]{:S(2)}, u32[]{:S(2)}) %collective-permute-start.19) | collective-permute-done | bytes 393248 | tf_op jit(solution)/shard_map/ppermute | solution.py:21
  169.7 2.0 collective-permute-start.22
  172.6 1.3 collective-permute-start.21
  174.3 3.0 %collective-permute-start.24 = (bf16[128,768]{1,0:T(8,128)(2,1)S(1)}, bf16[128,768]{1,0:T(8,128)(2,1)S(1)}, u32[]{:S(2)}, u32[]{:S(2)}) collective-permute-start(bf16[128,768]{1,0:T(8,128)(2,1)S(1)} %copy-done.3), channel_id=1, source_target_pairs={{0,32},{16,48},{32,0},{48,16},{1,33},{17,49},{33,1},{49,17},{2,34}... | collective-permute-start | bytes 589832 | tf_op jit(solution)/shard_map/ppermute | solution.py:26
  177.5 8.3 %collective-permute-done.23.s1 = bf16[128,768]{1,0:T(8,128)(2,1)S(1)} collective-permute-done((bf16[128,768]{1,0:T(8,128)(2,1)S(1)}, bf16[128,768]{1,0:T(8,128)(2,1)S(1)}, u32[]{:S(2)}, u32[]{:S(2)}) %collective-permute-start.23) | collective-permute-done | bytes 196640 | tf_op jit(solution)/shard_map/ppermute | solution.py:26
  186.4 8.3 %collective-permute-done.21 = bf16[64,3072]{1,0:T(8,128)(2,1)} collective-permute-done((bf16[64,3072]{1,0:T(8,128)(2,1)}, bf16[64,3072]{1,0:T(8,128)(2,1)}, u32[]{:S(2)}, u32[]{:S(2)}) %collective-permute-start.21) | collective-permute-done | bytes 393248 | tf_op jit(solution)/shard_map/ppermute | solution.py:21
  194.7 1.4 select_select_fusion
  196.1 1.1 copy-done.12
  199.0 3.0 %collective-permute-start.30 = (bf16[128,768]{1,0:T(8,128)(2,1)}, bf16[128,768]{1,0:T(8,128)(2,1)S(1)}, u32[]{:S(2)}, u32[]{:S(2)}) collective-permute-start(bf16[128,768]{1,0:T(8,128)(2,1)} %get-tuple-element.78), channel_id=1, source_target_pairs={{0,32},{16,48},{32,0},{48,16},{1,33},{17,49},{33,1},{49,17},{2,34}... | collective-permute-start | bytes 589832 | tf_op jit(solution)/shard_map/ppermute | solution.py:26
  202.2 1.3 collective-permute-start.26
  203.5 1.9 collective-permute-start.27
  205.4 4.6 %collective-permute-done.29.c1 = bf16[128,768]{1,0:T(8,128)(2,1)S(1)} collective-permute-done((bf16[128,768]{1,0:T(8,128)(2,1)}, bf16[128,768]{1,0:T(8,128)(2,1)S(1)}, u32[]{:S(2)}, u32[]{:S(2)}) %collective-permute-start.29) | collective-permute-done | bytes 196640 | tf_op jit(solution)/shard_map/ppermute | solution.py:26
  210.0 1.9 collective-permute-start.28
  213.2 4.0 %fusion = bf16[128,3072]{1,0:T(8,128)(2,1)S(1)} fusion(pred[]{:T(512)S(6)} %eq.70, bf16[1,1,128,3072]{3,2,1,0:T(8,128)(2,1)S(1)} %copy-done.13, bf16[128,768]{1,0:T(8,128)(2,1)S(1)} %copy-done.3, bf16[3072,768]{1,0:T(8,128)(2,1)} %all-gather.2.cloned.1.call-done), kind=kOutput, calls=%fused_computation.1 | convolution fusion | flops 605552640 | bytes 6488065 | tf_op jit(solution)/shard_map/dot_general | solution.py:273
  217.2 1.9 collective-permute-start.32
  219.2 4.6 %collective-permute-start.33 = (bf16[128,768]{1,0:T(8,128)(2,1)S(1)}, bf16[128,768]{1,0:T(8,128)(2,1)S(1)}, u32[]{:S(2)}, u32[]{:S(2)}) collective-permute-start(bf16[128,768]{1,0:T(8,128)(2,1)S(1)} %get-tuple-element.76), channel_id=1, source_target_pairs={{0,128},{64,192},{128,0},{192,64},{1,129},{65,193},{129,1},{193,65... | collective-permute-start | bytes 589832 | tf_op jit(solution)/shard_map/ppermute | solution.py:26
  223.8 8.1 %collective-permute-done.28 = bf16[128,768]{1,0:T(8,128)(2,1)S(1)} collective-permute-done((bf16[128,768]{1,0:T(8,128)(2,1)S(1)}, bf16[128,768]{1,0:T(8,128)(2,1)S(1)}, u32[]{:S(2)}, u32[]{:S(2)}) %collective-permute-start.28) | collective-permute-done | bytes 196640 | tf_op jit(solution)/shard_map/ppermute | solution.py:21
  232.9 1.1 collective-permute-start.37
  235.0 1.1 fusion.3
  236.1 5.1 %collective-permute-done.36 = bf16[2,48,768]{2,1,0:T(8,128)(2,1)S(1)} collective-permute-done((bf16[2,48,768]{2,1,0:T(8,128)(2,1)S(1)}, bf16[2,48,768]{2,1,0:T(8,128)(2,1)S(1)}, u32[]{:S(2)}, u32[]{:S(2)}) %collective-permute-start.36) | collective-permute-done | bytes 147488 | tf_op jit(solution)/shard_map/ppermute | solution.py:26
  241.1 1.8 collective-permute-done.38
  243.2 5.7 %collective-permute-done.34 = bf16[128,768]{1,0:T(8,128)(2,1)S(1)} collective-permute-done((bf16[128,768]{1,0:T(8,128)(2,1)S(1)}, bf16[128,768]{1,0:T(8,128)(2,1)S(1)}, u32[]{:S(2)}, u32[]{:S(2)}) %collective-permute-start.34) | collective-permute-done | bytes 196640 | tf_op jit(solution)/shard_map/ppermute | solution.py:26
  (105 shorter events, 20.6 us)
Async XLA Ops:
  7.2 135.2 %copy-start = (f32[64,3072]{1,0:T(8,128)S(1)}, f32[64,3072]{1,0:T(8,128)}, u32[]{:S(2)}) copy-start(f32[64,3072]{1,0:T(8,128)} %param.14) | copy-start | bytes 2359300
  8.3 6.7 %collective-permute-start = (bf16[128,768]{1,0:T(8,128)(2,1)S(1)}, bf16[128,768]{1,0:T(8,128)(2,1)S(1)}, u32[]{:S(2)}, u32[]{:S(2)}) collective-permute-start(bf16[128,768]{1,0:T(8,128)(2,1)S(1)} %select_bitcast_fusion), channel_id=1, source_target_pairs={{0,8},{8,0},{1,9},{9,1},{2,10},{10,2},{3,11},{11,3},{4,12},{12,4},... | collective-permute-start | bytes 589832 | tf_op jit(solution)/shard_map/ppermute | solution.py:26
  15.1 38.3 %all-to-all-start = ((bf16[16,3,128,128]{3,2,1,0:T(8,128)(2,1)}), bf16[16,3,128,128]{3,2,1,0:T(8,128)(2,1)S(1)}, u32[]{:S(2)}, u32[]{:S(2)}) async-start(bf16[16,3,128,128]{3,2,1,0:T(8,128)(2,1)} %pad_maximum_fusion), calls=%async_computation | async-start | bytes 3145728 | tf_op jit(solution)/shard_map/all_to_all | solution.py:206
  20.9 173.7 %all-gather.2.cloned.1.call-start = ((), (), s32[]{:S(2)}) async-start(), calls=%async_computation.2 | async-start | bytes 5013504 | tf_op jit(solution)/shard_map/all_gather | solution.py:211
  21.0 7.2 %collective-permute-start.4 = (bf16[256,256]{1,0:T(8,128)(2,1)S(1)}, bf16[256,256]{1,0:T(8,128)(2,1)S(1)}, u32[]{:S(2)}, u32[]{:S(2)}) collective-permute-start(bf16[256,256]{1,0:T(8,128)(2,1)S(1)} %slice.33), channel_id=1, source_target_pairs={{0,1},{1,2},{2,3},{3,0},{4,5},{5,6},{6,7},{7,4},{8,9},{9,10},{10,1... | collective-permute-start | bytes 393224 | tf_op jit(solution)/shard_map/ppermute | solution.py:26
  22.4 24.9 %collective-permute-start.1 = (bf16[256,512]{1,0:T(8,128)(2,1)S(1)}, bf16[256,512]{1,0:T(8,128)(2,1)S(1)}, u32[]{:S(2)}, u32[]{:S(2)}) collective-permute-start(bf16[256,512]{1,0:T(8,128)(2,1)S(1)} %slice.32), channel_id=1, source_target_pairs={{0,16},{16,32},{32,48},{48,0},{1,17},{17,33},{33,49},{49,1},{2,18}... | collective-permute-start | bytes 786440 | tf_op jit(solution)/shard_map/ppermute | solution.py:26
  23.9 23.4 %collective-permute-start.2 = (bf16[256,512]{1,0:T(8,128)(2,1)S(1)}, bf16[256,512]{1,0:T(8,128)(2,1)S(1)}, u32[]{:S(2)}, u32[]{:S(2)}) collective-permute-start(bf16[256,512]{1,0:T(8,128)(2,1)S(1)} %slice.32), channel_id=1, source_target_pairs={{0,48},{16,0},{32,16},{48,32},{1,49},{17,1},{33,17},{49,33},{2,50}... | collective-permute-start | bytes 786440 | tf_op jit(solution)/shard_map/ppermute | solution.py:26
  25.7 27.7 %collective-permute-start.3 = (bf16[256,512]{1,0:T(8,128)(2,1)S(1)}, bf16[256,512]{1,0:T(8,128)(2,1)}, u32[]{:S(2)}, u32[]{:S(2)}) collective-permute-start(bf16[256,512]{1,0:T(8,128)(2,1)S(1)} %slice.32), channel_id=1, source_target_pairs={{0,32},{16,48},{32,0},{48,16},{1,33},{17,49},{33,1},{49,17},{2,34}... | collective-permute-start | bytes 786440 | tf_op jit(solution)/shard_map/ppermute | solution.py:26
  27.5 5.8 %collective-permute-start.5 = (bf16[256,256]{1,0:T(8,128)(2,1)S(1)}, bf16[256,256]{1,0:T(8,128)(2,1)S(1)}, u32[]{:S(2)}, u32[]{:S(2)}) collective-permute-start(bf16[256,256]{1,0:T(8,128)(2,1)S(1)} %slice.33), channel_id=1, source_target_pairs={{0,3},{1,0},{2,1},{3,2},{4,7},{5,4},{6,5},{7,6},{8,11},{9,8},{10,9... | collective-permute-start | bytes 393224 | tf_op jit(solution)/shard_map/ppermute | solution.py:26
  28.2 33.0 %copy-start.16 = (bf16[256,256]{1,0:T(8,128)(2,1)}, bf16[256,256]{1,0:T(8,128)(2,1)S(1)}, u32[]{:S(2)}) copy-start(bf16[256,256]{1,0:T(8,128)(2,1)S(1)} %collective-permute-done.4) | copy-start | bytes 393220
  28.2 6.5 %collective-permute-start.6 = (bf16[256,256]{1,0:T(8,128)(2,1)S(1)}, bf16[256,256]{1,0:T(8,128)(2,1)S(1)}, u32[]{:S(2)}, u32[]{:S(2)}) collective-permute-start(bf16[256,256]{1,0:T(8,128)(2,1)S(1)} %slice.33), channel_id=1, source_target_pairs={{0,2},{1,3},{2,0},{3,1},{4,6},{5,7},{6,4},{7,5},{8,10},{9,11},{10,... | collective-permute-start | bytes 393224 | tf_op jit(solution)/shard_map/ppermute | solution.py:26
  33.3 24.7 %copy-start.17 = (bf16[256,256]{1,0:T(8,128)(2,1)}, bf16[256,256]{1,0:T(8,128)(2,1)S(1)}, u32[]{:S(2)}) copy-start(bf16[256,256]{1,0:T(8,128)(2,1)S(1)} %collective-permute-done.5) | copy-start | bytes 393220
  34.7 12.6 %copy-start.18 = (bf16[256,256]{1,0:T(8,128)(2,1)}, bf16[256,256]{1,0:T(8,128)(2,1)S(1)}, u32[]{:S(2)}) copy-start(bf16[256,256]{1,0:T(8,128)(2,1)S(1)} %collective-permute-done.6) | copy-start | bytes 393220
  53.4 2.9 %copy-start.4 = (bf16[16,3,128,128]{3,2,1,0:T(8,128)(2,1)}, bf16[16,3,128,128]{3,2,1,0:T(8,128)(2,1)S(1)}, u32[]{:S(2)}) copy-start(bf16[16,3,128,128]{3,2,1,0:T(8,128)(2,1)S(1)} %all-to-all-done.q_ref.k_ref.v_ref) | copy-start | bytes 4718596
  58.0 47.8 %collective-permute-start.10 = (bf16[1024,512]{1,0:T(8,128)(2,1)}, bf16[1024,512]{1,0:T(8,128)(2,1)S(1)}, u32[]{:S(2)}, u32[]{:S(2)}) collective-permute-start(bf16[1024,512]{1,0:T(8,128)(2,1)} %constant_dynamic-update-slice_fusion.y0), channel_id=1, source_target_pairs={{0,1},{1,2},{2,3},{3,0},{4,5},{5,6},{6,7},{7,4},{8,9},{9,10},{10,1... | collective-permute-start | bytes 3145736 | tf_op jit(solution)/shard_map/ppermute | solution.py:26
  59.3 48.6 %collective-permute-start.11 = (bf16[1024,512]{1,0:T(8,128)(2,1)}, bf16[1024,512]{1,0:T(8,128)(2,1)S(1)}, u32[]{:S(2)}, u32[]{:S(2)}) collective-permute-start(bf16[1024,512]{1,0:T(8,128)(2,1)} %constant_dynamic-update-slice_fusion.y0), channel_id=1, source_target_pairs={{0,3},{1,0},{2,1},{3,2},{4,7},{5,4},{6,5},{7,6},{8,11},{9,8},{10,9... | collective-permute-start | bytes 3145736 | tf_op jit(solution)/shard_map/ppermute | solution.py:26
  61.2 23.7 %collective-permute-start.7 = (bf16[128,768]{1,0:T(8,128)(2,1)S(1)}, bf16[128,768]{1,0:T(8,128)(2,1)S(1)}, u32[]{:S(2)}, u32[]{:S(2)}) collective-permute-start(bf16[128,768]{1,0:T(8,128)(2,1)S(1)} %get-tuple-element.87), channel_id=1, source_target_pairs={{64,128},{128,192},{192,0},{65,129},{129,193},{193,1},{66,130},{13... | collective-permute-start | bytes 589832 | tf_op jit(solution)/shard_map/ppermute | solution.py:21
  67.1 19.1 %collective-permute-start.8 = (bf16[128,768]{1,0:T(8,128)(2,1)S(1)}, bf16[128,768]{1,0:T(8,128)(2,1)S(1)}, u32[]{:S(2)}, u32[]{:S(2)}) collective-permute-start(bf16[128,768]{1,0:T(8,128)(2,1)S(1)} %get-tuple-element.89), channel_id=1, source_target_pairs={{64,192},{128,0},{192,64},{65,193},{129,1},{193,65},{66,194},{130,... | collective-permute-start | bytes 589832 | tf_op jit(solution)/shard_map/ppermute | solution.py:21
  70.0 26.2 %collective-permute-start.9 = (bf16[128,768]{1,0:T(8,128)(2,1)S(1)}, bf16[128,768]{1,0:T(8,128)(2,1)S(1)}, u32[]{:S(2)}, u32[]{:S(2)}) collective-permute-start(bf16[128,768]{1,0:T(8,128)(2,1)S(1)} %get-tuple-element.88), channel_id=1, source_target_pairs={{64,0},{128,64},{192,128},{65,1},{129,65},{193,129},{66,2},{130,66... | collective-permute-start | bytes 589832 | tf_op jit(solution)/shard_map/ppermute | solution.py:21
  71.9 1.4 copy-start.5
  84.9 13.0 %copy-start.11 = (bf16[2048,128]{1,0:T(8,128)(2,1)}, bf16[2048,128]{1,0:T(8,128)(2,1)S(1)}, u32[]{:S(2)}) copy-start(bf16[2048,128]{1,0:T(8,128)(2,1)S(1)} %attend.1) | copy-start | bytes 1572868
  97.9 35.2 %all-to-all-start.1 = ((bf16[8,256,128]{2,1,0:T(8,128)(2,1)}), bf16[8,256,128]{2,1,0:T(8,128)(2,1)S(1)}, u32[]{:S(2)}, u32[]{:S(2)}) async-start(bf16[8,256,128]{2,1,0:T(8,128)(2,1)} %bitcast.67), calls=%async_computation.1 | async-start | bytes 1048576 | tf_op jit(solution)/shard_map/all_to_all | solution.py:226
  102.5 22.8 %copy-start.1 = (bf16[4,256,256]{2,1,0:T(8,128)(2,1)}, bf16[4,256,256]{2,1,0:T(8,128)(2,1)S(1)}, u32[]{:S(2)}) copy-start(bf16[4,256,256]{2,1,0:T(8,128)(2,1)S(1)} %pad_maximum_fusion.2.x0) | copy-start | bytes 1572868
  102.5 18.8 %collective-permute-start.14 = (bf16[4,256,256]{2,1,0:T(8,128)(2,1)S(1)}, bf16[4,256,256]{2,1,0:T(8,128)(2,1)S(1)}, u32[]{:S(2)}, u32[]{:S(2)}) collective-permute-start(bf16[4,256,256]{2,1,0:T(8,128)(2,1)S(1)} %pad_maximum_fusion.2.x0), channel_id=1, source_target_pairs={{0,16},{16,32},{32,48},{48,0},{1,17},{17,33},{33,49},{49,1},{2,18}... | collective-permute-start | bytes 1572872 | tf_op jit(solution)/shard_map/ppermute | solution.py:26
  103.9 20.5 %collective-permute-start.15 = (bf16[4,256,256]{2,1,0:T(8,128)(2,1)S(1)}, bf16[4,256,256]{2,1,0:T(8,128)(2,1)S(1)}, u32[]{:S(2)}, u32[]{:S(2)}) collective-permute-start(bf16[4,256,256]{2,1,0:T(8,128)(2,1)S(1)} %pad_maximum_fusion.2.x0), channel_id=1, source_target_pairs={{0,48},{16,0},{32,16},{48,32},{1,49},{17,1},{33,17},{49,33},{2,50}... | collective-permute-start | bytes 1572872 | tf_op jit(solution)/shard_map/ppermute | solution.py:26
  106.7 26.4 %collective-permute-start.12 = (bf16[512,512]{1,0:T(8,128)(2,1)}, bf16[512,512]{1,0:T(8,128)(2,1)}, u32[]{:S(2)}, u32[]{:S(2)}) collective-permute-start(bf16[512,512]{1,0:T(8,128)(2,1)} %slice.40), channel_id=1, source_target_pairs={{0,1},{1,2},{2,3},{3,0},{4,5},{5,6},{6,7},{7,4},{8,9},{9,10},{10,1... | collective-permute-start | bytes 1572872 | tf_op jit(solution)/shard_map/ppermute | solution.py:26
  108.8 24.3 %collective-permute-start.13 = (bf16[512,512]{1,0:T(8,128)(2,1)}, bf16[512,512]{1,0:T(8,128)(2,1)}, u32[]{:S(2)}, u32[]{:S(2)}) collective-permute-start(bf16[512,512]{1,0:T(8,128)(2,1)} %slice.41), channel_id=1, source_target_pairs={{0,3},{1,0},{2,1},{3,2},{4,7},{5,4},{6,5},{7,6},{8,11},{9,8},{10,9... | collective-permute-start | bytes 1572872 | tf_op jit(solution)/shard_map/ppermute | solution.py:26
  121.2 3.3 %copy-start.7 = (bf16[4,256,256]{2,1,0:T(8,128)(2,1)}, bf16[4,256,256]{2,1,0:T(8,128)(2,1)S(1)}, u32[]{:S(2)}) copy-start(bf16[4,256,256]{2,1,0:T(8,128)(2,1)S(1)} %collective-permute-done.14.x1) | copy-start | bytes 1572868
  122.0 9.2 %collective-permute-start.16 = (bf16[2,256,256]{2,1,0:T(8,128)(2,1)}, bf16[2,256,256]{2,1,0:T(8,128)(2,1)}, u32[]{:S(2)}, u32[]{:S(2)}) collective-permute-start(bf16[2,256,256]{2,1,0:T(8,128)(2,1)} %slice.42), channel_id=1, source_target_pairs={{0,16},{16,32},{32,48},{48,0},{1,17},{17,33},{33,49},{49,1},{2,18}... | collective-permute-start | bytes 786440 | tf_op jit(solution)/shard_map/ppermute | solution.py:26
  124.5 0.9 copy-start.9
  125.3 7.7 %collective-permute-start.17 = (bf16[2,256,256]{2,1,0:T(8,128)(2,1)}, bf16[2,256,256]{2,1,0:T(8,128)(2,1)}, u32[]{:S(2)}, u32[]{:S(2)}) collective-permute-start(bf16[2,256,256]{2,1,0:T(8,128)(2,1)} %slice.43), channel_id=1, source_target_pairs={{0,48},{16,0},{32,16},{48,32},{1,49},{17,1},{33,17},{49,33},{2,50}... | collective-permute-start | bytes 786440 | tf_op jit(solution)/shard_map/ppermute | solution.py:26
  133.1 1.0 copy-start.2
  134.1 1.0 copy-start.8
  135.2 1.0 copy-start.10
  140.6 1.2 copy-start.6
  141.7 2.5 collective-permute-start.18
  146.2 27.7 %copy-start.3 = (bf16[128,768]{1,0:T(8,128)(2,1)S(1)}, bf16[128,768]{1,0:T(8,128)(2,1)}, u32[]{:S(2)}) copy-start(bf16[128,768]{1,0:T(8,128)(2,1)} %add_convert_fusion.2.s0) | copy-start | bytes 589828
  146.2 22.6 %collective-permute-start.19 = (bf16[64,3072]{1,0:T(8,128)(2,1)S(1)}, bf16[64,3072]{1,0:T(8,128)(2,1)S(1)}, u32[]{:S(2)}, u32[]{:S(2)}) collective-permute-start(bf16[64,3072]{1,0:T(8,128)(2,1)S(1)} %get-tuple-element.54), channel_id=1, source_target_pairs={{0,64},{1,65},{2,66},{3,67},{4,68},{5,69},{6,70},{7,71},{8,72},{9,... | collective-permute-start | bytes 1179656 | tf_op jit(solution)/shard_map/ppermute | solution.py:21
  147.7 21.2 %collective-permute-start.20 = (bf16[64,3072]{1,0:T(8,128)(2,1)S(1)}, bf16[64,3072]{1,0:T(8,128)(2,1)S(1)}, u32[]{:S(2)}, u32[]{:S(2)}) collective-permute-start(bf16[64,3072]{1,0:T(8,128)(2,1)S(1)} %get-tuple-element.56), channel_id=1, source_target_pairs={{0,192},{1,193},{2,194},{3,195},{4,196},{5,197},{6,198},{7,199},{8... | collective-permute-start | bytes 1179656 | tf_op jit(solution)/shard_map/ppermute | solution.py:21
  168.8 3.7 %copy-start.14 = (bf16[64,3072]{1,0:T(8,128)(2,1)}, bf16[64,3072]{1,0:T(8,128)(2,1)S(1)}, u32[]{:S(2)}) copy-start(bf16[64,3072]{1,0:T(8,128)(2,1)S(1)} %collective-permute-done.19) | copy-start | bytes 1179652
  168.8 5.0 %copy-start.15 = (bf16[64,3072]{1,0:T(8,128)(2,1)}, bf16[64,3072]{1,0:T(8,128)(2,1)S(1)}, u32[]{:S(2)}) copy-start(bf16[64,3072]{1,0:T(8,128)(2,1)S(1)} %collective-permute-done.20) | copy-start | bytes 1179652
  169.7 16.6 %collective-permute-start.22 = (bf16[64,3072]{1,0:T(8,128)(2,1)}, bf16[64,3072]{1,0:T(8,128)(2,1)}, u32[]{:S(2)}, u32[]{:S(2)}) collective-permute-start(bf16[64,3072]{1,0:T(8,128)(2,1)} %broadcast_select_fusion), channel_id=1, source_target_pairs={{0,192},{64,128},{1,193},{65,129},{2,194},{66,130},{3,195},{67,131... | collective-permute-start | bytes 1179656 | tf_op jit(solution)/shard_map/ppermute | solution.py:21
  172.6 22.1 %collective-permute-start.21 = (bf16[64,3072]{1,0:T(8,128)(2,1)}, bf16[64,3072]{1,0:T(8,128)(2,1)}, u32[]{:S(2)}, u32[]{:S(2)}) collective-permute-start(bf16[64,3072]{1,0:T(8,128)(2,1)} %broadcast_select_fusion.1), channel_id=1, source_target_pairs={{0,64},{192,128},{1,65},{193,129},{2,66},{194,130},{3,67},{195,131... | collective-permute-start | bytes 1179656 | tf_op jit(solution)/shard_map/ppermute | solution.py:21
  173.9 11.9 %collective-permute-start.23 = (bf16[128,768]{1,0:T(8,128)(2,1)S(1)}, bf16[128,768]{1,0:T(8,128)(2,1)S(1)}, u32[]{:S(2)}, u32[]{:S(2)}) collective-permute-start(bf16[128,768]{1,0:T(8,128)(2,1)S(1)} %copy-done.3), channel_id=1, source_target_pairs={{0,16},{16,32},{32,48},{48,0},{1,17},{17,33},{33,49},{49,1},{2,18}... | collective-permute-start | bytes 589832 | tf_op jit(solution)/shard_map/ppermute | solution.py:26
  174.3 11.4 %collective-permute-start.24 = (bf16[128,768]{1,0:T(8,128)(2,1)S(1)}, bf16[128,768]{1,0:T(8,128)(2,1)S(1)}, u32[]{:S(2)}, u32[]{:S(2)}) collective-permute-start(bf16[128,768]{1,0:T(8,128)(2,1)S(1)} %copy-done.3), channel_id=1, source_target_pairs={{0,32},{16,48},{32,0},{48,16},{1,33},{17,49},{33,1},{49,17},{2,34}... | collective-permute-start | bytes 589832 | tf_op jit(solution)/shard_map/ppermute | solution.py:26
  177.4 9.0 %collective-permute-start.25 = (bf16[128,768]{1,0:T(8,128)(2,1)S(1)}, bf16[128,768]{1,0:T(8,128)(2,1)S(1)}, u32[]{:S(2)}, u32[]{:S(2)}) collective-permute-start(bf16[128,768]{1,0:T(8,128)(2,1)S(1)} %copy-done.3), channel_id=1, source_target_pairs={{0,48},{16,0},{32,16},{48,32},{1,49},{17,1},{33,17},{49,33},{2,50}... | collective-permute-start | bytes 589832 | tf_op jit(solution)/shard_map/ppermute | solution.py:26
  194.7 2.6 %copy-start.12 = (bf16[3072,768]{1,0:T(8,128)(2,1)S(1)}, bf16[3072,768]{1,0:T(8,128)(2,1)}, u32[]{:S(2)}) copy-start(bf16[3072,768]{1,0:T(8,128)(2,1)} %all-gather.2.cloned.1.call-done) | copy-start | bytes 14155780
  198.9 11.1 %collective-permute-start.29 = (bf16[128,768]{1,0:T(8,128)(2,1)}, bf16[128,768]{1,0:T(8,128)(2,1)S(1)}, u32[]{:S(2)}, u32[]{:S(2)}) collective-permute-start(bf16[128,768]{1,0:T(8,128)(2,1)} %get-tuple-element.79), channel_id=1, source_target_pairs={{0,16},{16,32},{32,48},{48,0},{1,17},{17,33},{33,49},{49,1},{2,18}... | collective-permute-start | bytes 589832 | tf_op jit(solution)/shard_map/ppermute | solution.py:26
  199.0 12.9 %collective-permute-start.30 = (bf16[128,768]{1,0:T(8,128)(2,1)}, bf16[128,768]{1,0:T(8,128)(2,1)S(1)}, u32[]{:S(2)}, u32[]{:S(2)}) collective-permute-start(bf16[128,768]{1,0:T(8,128)(2,1)} %get-tuple-element.78), channel_id=1, source_target_pairs={{0,32},{16,48},{32,0},{48,16},{1,33},{17,49},{33,1},{49,17},{2,34}... | collective-permute-start | bytes 589832 | tf_op jit(solution)/shard_map/ppermute | solution.py:26
  202.0 9.9 %collective-permute-start.31 = (bf16[128,768]{1,0:T(8,128)(2,1)S(1)}, bf16[128,768]{1,0:T(8,128)(2,1)S(1)}, u32[]{:S(2)}, u32[]{:S(2)}) collective-permute-start(bf16[128,768]{1,0:T(8,128)(2,1)S(1)} %get-tuple-element.77), channel_id=1, source_target_pairs={{0,48},{16,0},{32,16},{48,32},{1,49},{17,1},{33,17},{49,33},{2,50}... | collective-permute-start | bytes 589832 | tf_op jit(solution)/shard_map/ppermute | solution.py:26
  202.2 17.0 %collective-permute-start.26 = (bf16[128,768]{1,0:T(8,128)(2,1)S(1)}, bf16[128,768]{1,0:T(8,128)(2,1)S(1)}, u32[]{:S(2)}, u32[]{:S(2)}) collective-permute-start(bf16[128,768]{1,0:T(8,128)(2,1)S(1)} %convolution_convert_fusion), channel_id=1, source_target_pairs={{0,192},{128,64},{192,128},{1,193},{129,65},{193,129},{2,194},{130... | collective-permute-start | bytes 589832 | tf_op jit(solution)/shard_map/ppermute | solution.py:21
  203.5 20.4 %collective-permute-start.27 = (bf16[128,768]{1,0:T(8,128)(2,1)S(1)}, bf16[128,768]{1,0:T(8,128)(2,1)S(1)}, u32[]{:S(2)}, u32[]{:S(2)}) collective-permute-start(bf16[128,768]{1,0:T(8,128)(2,1)S(1)} %convolution_convert_fusion), channel_id=1, source_target_pairs={{0,128},{64,192},{192,64},{1,129},{65,193},{193,65},{2,130},{66,19... | collective-permute-start | bytes 589832 | tf_op jit(solution)/shard_map/ppermute | solution.py:21
  210.0 21.9 %collective-permute-start.28 = (bf16[128,768]{1,0:T(8,128)(2,1)S(1)}, bf16[128,768]{1,0:T(8,128)(2,1)S(1)}, u32[]{:S(2)}, u32[]{:S(2)}) collective-permute-start(bf16[128,768]{1,0:T(8,128)(2,1)S(1)} %convolution_convert_fusion), channel_id=1, source_target_pairs={{0,64},{64,128},{128,192},{1,65},{65,129},{129,193},{2,66},{66,130... | collective-permute-start | bytes 589832 | tf_op jit(solution)/shard_map/ppermute | solution.py:21
  212.0 1.2 copy-start.13
  212.9 19.1 %collective-permute-start.35 = (bf16[2,192,768]{2,1,0:T(8,128)(2,1)S(1)}, bf16[2,192,768]{2,1,0:T(8,128)(2,1)S(1)}, u32[]{:S(2)}, u32[]{:S(2)}) collective-permute-start(bf16[2,192,768]{2,1,0:T(8,128)(2,1)S(1)} %dynamic-slice_bitcast_fusion), channel_id=1, source_target_pairs={{0,4},{4,0},{1,5},{5,1},{2,6},{6,2},{3,7},{7,3},{8,12},{12,8},{9,1... | collective-permute-start | bytes 1769480 | tf_op jit(solution)/shard_map/ppermute | solution.py:26
  217.2 25.9 %collective-permute-start.32 = (bf16[128,768]{1,0:T(8,128)(2,1)S(1)}, bf16[128,768]{1,0:T(8,128)(2,1)S(1)}, u32[]{:S(2)}, u32[]{:S(2)}) collective-permute-start(bf16[128,768]{1,0:T(8,128)(2,1)S(1)} %get-tuple-element.74), channel_id=1, source_target_pairs={{0,64},{64,128},{128,192},{192,0},{1,65},{65,129},{129,193},{193,1... | collective-permute-start | bytes 589832 | tf_op jit(solution)/shard_map/ppermute | solution.py:26
  219.2 24.0 %collective-permute-start.33 = (bf16[128,768]{1,0:T(8,128)(2,1)S(1)}, bf16[128,768]{1,0:T(8,128)(2,1)S(1)}, u32[]{:S(2)}, u32[]{:S(2)}) collective-permute-start(bf16[128,768]{1,0:T(8,128)(2,1)S(1)} %get-tuple-element.76), channel_id=1, source_target_pairs={{0,128},{64,192},{128,0},{192,64},{1,129},{65,193},{129,1},{193,65... | collective-permute-start | bytes 589832 | tf_op jit(solution)/shard_map/ppermute | solution.py:26
  232.2 8.9 %collective-permute-start.36 = (bf16[2,48,768]{2,1,0:T(8,128)(2,1)S(1)}, bf16[2,48,768]{2,1,0:T(8,128)(2,1)S(1)}, u32[]{:S(2)}, u32[]{:S(2)}) collective-permute-start(bf16[2,48,768]{2,1,0:T(8,128)(2,1)S(1)} %get-tuple-element.71), channel_id=1, source_target_pairs={{0,1},{1,2},{2,3},{3,0},{4,5},{5,6},{6,7},{7,4},{8,9},{9,10},{10,1... | collective-permute-start | bytes 442376 | tf_op jit(solution)/shard_map/ppermute | solution.py:26
  232.9 8.3 %collective-permute-start.37 = (bf16[2,48,768]{2,1,0:T(8,128)(2,1)S(1)}, bf16[2,48,768]{2,1,0:T(8,128)(2,1)S(1)}, u32[]{:S(2)}, u32[]{:S(2)}) collective-permute-start(bf16[2,48,768]{2,1,0:T(8,128)(2,1)S(1)} %get-tuple-element.73), channel_id=1, source_target_pairs={{0,2},{1,3},{2,0},{3,1},{4,6},{5,7},{6,4},{7,5},{8,10},{9,11},{10,... | collective-permute-start | bytes 442376 | tf_op jit(solution)/shard_map/ppermute | solution.py:26
  234.0 9.0 %collective-permute-start.38 = (bf16[2,48,768]{2,1,0:T(8,128)(2,1)S(1)}, bf16[2,48,768]{2,1,0:T(8,128)(2,1)S(1)}, u32[]{:S(2)}, u32[]{:S(2)}) collective-permute-start(bf16[2,48,768]{2,1,0:T(8,128)(2,1)S(1)} %get-tuple-element.72), channel_id=1, source_target_pairs={{0,3},{1,0},{2,1},{3,2},{4,7},{5,4},{6,5},{7,6},{8,11},{9,8},{10,9... | collective-permute-start | bytes 442376 | tf_op jit(solution)/shard_map/ppermute | solution.py:26
  241.1 7.8 %collective-permute-start.34 = (bf16[128,768]{1,0:T(8,128)(2,1)S(1)}, bf16[128,768]{1,0:T(8,128)(2,1)S(1)}, u32[]{:S(2)}, u32[]{:S(2)}) collective-permute-start(bf16[128,768]{1,0:T(8,128)(2,1)S(1)} %get-tuple-element.75), channel_id=1, source_target_pairs={{0,192},{64,0},{128,64},{192,128},{1,193},{65,1},{129,65},{193,129... | collective-permute-start | bytes 589832 | tf_op jit(solution)/shard_map/ppermute | solution.py:26
  243.0 6.6 %collective-permute-start.39 = (bf16[48,768]{1,0:T(8,128)(2,1)S(1)}, bf16[48,768]{1,0:T(8,128)(2,1)S(1)}, u32[]{:S(2)}, u32[]{:S(2)}) collective-permute-start(bf16[48,768]{1,0:T(8,128)(2,1)S(1)} %fusion.10), channel_id=1, source_target_pairs={{0,8},{8,0},{1,9},{9,1},{2,10},{10,2},{3,11},{11,3},{4,12},{12,4},... | collective-permute-start | bytes 221192 | tf_op jit(solution)/shard_map/ppermute | solution.py:26
Sparse Core Ops, SparseCore 0:
  53.5 59.4 all-gather.1

commit v2 on v1

v2 whole, which is shorter than its diff:
```python
import functools
import math

import jax
import jax.numpy as jnp
from jax import lax
from jax.experimental import pallas as pl
from jax.experimental.pallas import tpu as pltpu
from jax.sharding import Mesh, PartitionSpec as P

H = 16
HEAD = 128
SIZES = {"grp": 4, "x": 4, "zl": 2, "core": 2, "rep": 4}
SEQ = ("x", "zl", "core")
BF = jnp.bfloat16
F32 = jnp.float32
MIB = 1 << 20


def send(value, axis, pairs):
    return lax.ppermute(value, axis, pairs)


def shift(value, axis, step):
    n = SIZES[axis]
    return lax.ppermute(value, axis, [(i, (i + step) % n) for i in range(n)])


def attend_kernel(tlen_ref, q_ref, k_ref, v_ref, o_ref, wide_ref, *, text_slots, scale):
    @pl.when(pl.program_id(0) == 0)
    def _():
        length = wide_ref.shape[0]
        wide_ref[:, :HEAD] = v_ref[...].reshape(length, HEAD)
        wide_ref[:, HEAD:] = jnp.ones((length, HEAD), BF)

    rows = o_ref.shape[0]
    q = q_ref[...].reshape(rows, HEAD)
    length = wide_ref.shape[0]
    k = k_ref[...].reshape(length, HEAD)
    s = lax.dot_general(q, k, (((1,), (1,)), ((), ())), preferred_element_type=F32)
    place = lax.broadcasted_iota(jnp.int32, (rows, text_slots), 1)
    head = jnp.where(place < tlen_ref[0, 0], s[:, :text_slots], -jnp.inf)
    tail = s[:, text_slots:]
    top = jnp.maximum(
        jnp.max(head, axis=1, keepdims=True), jnp.max(tail, axis=1, keepdims=True)
    )
    factor = scale * math.log2(math.e)
    p_head = jnp.exp2((head - top) * factor).astype(BF)
    p_tail = jnp.exp2((tail - top) * factor).astype(BF)
    both = jnp.dot(p_head, wide_ref[:text_slots, :], preferred_element_type=F32) + jnp.dot(
        p_tail, wide_ref[text_slots:, :], preferred_element_type=F32
    )
    o_ref[...] = (both[:, :HEAD] / both[:, HEAD:]).astype(BF)


def attend(qkv, tlen):
    blocks, _, per, _ = qkv.shape
    length = blocks * per
    q_blocks = 2
    rows = q_blocks * per
    whole = lambda part: pl.BlockSpec((blocks, None, per, HEAD), lambda i: (0, part, 0, 0))
    return pl.pallas_call(
        functools.partial(attend_kernel, text_slots=length // 8, scale=HEAD ** -0.5),
        grid=(length // rows,),
        in_specs=[
            pl.BlockSpec(memory_space=pltpu.SMEM),
            pl.BlockSpec((q_blocks, None, per, HEAD), lambda i: (i, 0, 0, 0)),
            whole(1),
            whole(2),
        ],
        out_specs=pl.BlockSpec((rows, HEAD), lambda i: (i, 0)),
        out_shape=jax.ShapeDtypeStruct((length, HEAD), BF),
        scratch_shapes=[pltpu.VMEM((length, 2 * HEAD), BF)],
        compiler_params=pltpu.CompilerParams(vmem_limit_bytes=40 * MIB),
        cost_estimate=pl.CostEstimate(
            flops=6 * length * length * HEAD,
            bytes_accessed=8 * length * HEAD,
            transcendentals=length * length,
        ),
        name="attend",
    )(tlen, qkv, qkv, qkv)


def project_kernel(zl_ref, a_ref, w_ref, own_ref, other_ref, a_held, wide_ref, held, sems, *, first):
    heads, half = held.shape[0], own_ref.shape[0]
    count, _, width = held.shape[1:]
    load = pltpu.make_async_copy(a_ref, a_held, sems.at[heads])
    load.start()
    copies = [
        pltpu.make_async_copy(w_ref.at[h, pl.ds(first, count)], held.at[h], sems.at[h])
        for h in range(heads)
    ]
    for copy in copies:
        copy.start()
    mine = pl.multiple_of(zl_ref[0] * half, half)
    theirs = pl.multiple_of((1 - zl_ref[0]) * half, half)
    load.wait()
    for h in range(heads):
        lanes = slice(h * HEAD, (h + 1) * HEAD)
        wide_ref[:half, lanes] = a_held[h, pl.ds(mine, half), :]
        wide_ref[half:, lanes] = a_held[h, pl.ds(theirs, half), :]
    for copy in copies:
        copy.wait()
    for j in range(count):
        w = held[:, j].reshape(heads * HEAD, width)
        total = jnp.dot(wide_ref[...], w, preferred_element_type=F32)
        lanes = slice(j * width, (j + 1) * width)
        own_ref[:, lanes] = total[:half]
        other_ref[:, lanes] = total[half:].astype(BF)


def project(zl, attn, weight, first, count):
    heads, rows, _ = attn.shape
    _, _, depth, width = weight.shape
    half = rows // 2
    vmem, anywhere = pl.BlockSpec(memory_space=pltpu.VMEM), pl.BlockSpec(memory_space=pl.ANY)
    return pl.pallas_call(
        functools.partial(project_kernel, first=first),
        in_specs=[pl.BlockSpec(memory_space=pltpu.SMEM), anywhere, anywhere],
        out_specs=[vmem, vmem],
        out_shape=[
            jax.ShapeDtypeStruct((half, count * width), F32),
            jax.ShapeDtypeStruct((half, count * width), BF),
        ],
        scratch_shapes=[
            pltpu.VMEM(attn.shape, BF),
            pltpu.VMEM((rows, heads * HEAD), BF),
            pltpu.VMEM((heads, count, depth, width), BF),
            pltpu.SemaphoreType.DMA((heads + 1,)),
        ],
        compiler_params=pltpu.CompilerParams(vmem_limit_bytes=60 * MIB),
        cost_estimate=pl.CostEstimate(
            flops=2 * rows * heads * HEAD * count * width,
            bytes_accessed=2 * heads * HEAD * count * width,
            transcendentals=0,
        ),
        name="project",
    )(zl, attn, weight)


def ring_gather(value, axis):
    return [value] + [shift(value, axis, step) for step in range(1, 4)]


def gate(*values):
    return lax.optimization_barrier(values)


def fetch_zero(zero_ref, held, sems):
    copies = []
    for x in range(4):
        for core in range(2):
            for rep in range(4):
                target = held.at[x, :, core, rep]
                copies.append(pltpu.make_async_copy(zero_ref.at[x, core, rep], target, sems.at[x, core, rep]))
    for copy in copies:
        copy.start()
    return copies


def block_of(held, copies, j):
    for copy in copies[8 * j : 8 * (j + 1)]:
        copy.wait()
    width = held.shape[-1]
    return held[j].reshape(width, width)


def resid_kernel(ctl_ref, zero_ref, o_ref, held, sems):
    copies = fetch_zero(zero_ref, held, sems)
    for j in range(4):
        w = block_of(held, copies, j)
        o_ref[j] = jnp.dot(ctl_ref[...], w, preferred_element_type=F32).astype(BF)


def term_kernel(csum_ref, cot_ref, zero_ref, o_ref, held, sems):
    copies = fetch_zero(zero_ref, held, sems)
    total = 0.0
    for j in range(4):
        term = lax.dot_general(
            csum_ref[j],
            block_of(held, copies, j),
            (((1,), (1,)), ((), ())),
            preferred_element_type=F32,
        )
        if j == 0:
            term = term + cot_ref[...].astype(F32)
        total = total + term.astype(BF).astype(F32)
    o_ref[...] = total.astype(BF)


def with_zero(kernel, dense, zero, shape, name):
    _, _, reps, _, slab, width = zero.shape
    vmem = pl.BlockSpec(memory_space=pltpu.VMEM)
    return pl.pallas_call(
        kernel,
        in_specs=[vmem] * len(dense) + [pl.BlockSpec(memory_space=pl.ANY)],
        out_specs=vmem,
        out_shape=jax.ShapeDtypeStruct(shape, BF),
        scratch_shapes=[
            pltpu.VMEM((4, 2, 2, reps, slab, width), BF),
            pltpu.SemaphoreType.DMA((4, 2, reps)),
        ],
        compiler_params=pltpu.CompilerParams(vmem_limit_bytes=60 * MIB),
        cost_estimate=pl.CostEstimate(
            flops=8 * shape[-2] * width * width, bytes_accessed=8 * width * width, transcendentals=0
        ),
        name=name,
    )(*dense, zero)


def grad_kernel(x_ref, *refs):
    pieces, csum_ref, (o_ref, ctl_ref, sum_ref, sems) = refs[:4], refs[4], refs[5:]
    rows = pieces[0].shape[0]
    copies = [pltpu.make_async_copy(csum_ref, sum_ref, sems.at[4])]
    for step, piece in enumerate(pieces):
        start = pl.multiple_of(lax.rem(x_ref[0] + 4 - step, 4) * rows, rows)
        copies.append(pltpu.make_async_copy(piece, ctl_ref.at[pl.ds(start, rows), :], sems.at[step]))
    for copy in copies:
        copy.start()
    for copy in copies:
        copy.wait()
    o_ref[...] = lax.dot_general(
        ctl_ref[...],
        sum_ref[...].reshape(ctl_ref.shape),
        (((0,), (0,)), ((), ())),
        preferred_element_type=F32,
    ).astype(BF)


def grad_partial(x, ctl, csum):
    blocks, rows, width = csum.shape
    return pl.pallas_call(
        grad_kernel,
        in_specs=[pl.BlockSpec(memory_space=pltpu.SMEM)]
        + [pl.BlockSpec(memory_space=pl.ANY)] * 5,
        out_specs=pl.BlockSpec(memory_space=pltpu.VMEM),
        out_shape=jax.ShapeDtypeStruct((width, width), BF),
        scratch_shapes=[
            pltpu.VMEM((blocks * rows, width), BF),
            pltpu.VMEM(csum.shape, BF),
            pltpu.SemaphoreType.DMA((5,)),
        ],
        compiler_params=pltpu.CompilerParams(vmem_limit_bytes=40 * MIB),
        cost_estimate=pl.CostEstimate(
            flops=8 * rows * width * width, bytes_accessed=18 * rows * width, transcendentals=0
        ),
        name="grad_partial",
    )(x, *ctl, csum)


def pick(blocks, index):
    return lax.dynamic_index_in_dim(blocks, index, 0, keepdims=False)


def ordered(blocks, source):
    result = []
    for j in range(len(blocks)):
        block = blocks[0]
        for step in range(1, len(blocks)):
            block = jnp.where(source(step) == j, blocks[step], block)
        result.append(block)
    return result


def shards(hidden, queries_keys, values, text_len, timestep, gate_table, w_out, w_zero, cotangent):
    g = lax.axis_index("grp")
    x = lax.axis_index("x")
    core = lax.axis_index("core")
    rep = lax.axis_index("rep")
    zl = lax.axis_index("zl")
    is_control = g == 0
    n_grp, n_x, n_rep = SIZES["grp"], SIZES["x"], SIZES["rep"]
    tok, width = hidden.shape[2], w_zero.shape[1]

    def source(step):
        return (g - step) % n_grp

    w_sel = jnp.where(is_control, w_out[0], w_out[1])
    weight = lax.all_gather(w_sel, ("x", "core", "rep")).reshape(8, n_rep, *w_sel.shape)

    pair = queries_keys[0, 0].reshape(tok, 2, H, HEAD).transpose(2, 1, 0, 3)
    vals = values[0, 0].reshape(tok, 1, H, HEAD).transpose(2, 1, 0, 3)
    qkv = jnp.concatenate([pair, vals], axis=1)

    qkv = lax.all_to_all(qkv, SEQ, split_axis=0, concat_axis=0, tiled=True)
    turn = [(i * n_grp + j, j * n_grp + i) for i in range(n_x) for j in range(n_grp)]
    slab = w_zero.shape[0] // n_rep
    zero_slab = lax.dynamic_slice_in_dim(w_zero, rep * slab, slab, axis=0)
    zero_slab = lax.ppermute(zero_slab, ("grp", "x"), turn)

    def cot_block(index):
        return lax.dynamic_slice_in_dim(cotangent[0, 0], index * width, width, axis=1)

    cots = [cot_block(g)] + [
        shift(cot_block((g + step) % n_grp), "grp", step) for step in range(1, n_grp)
    ]
    csum = sum(jnp.where(source(step) == 0, 0.0, cots[step].astype(F32)) for step in range(n_grp))
    own_cot = sum(jnp.where(source(step) == 0, cots[step], 0) for step in range(n_grp))
    csum = csum.astype(BF)
    slab_other = shift(zero_slab, "zl", 1)
    attn, csum, own_cot, zero_slab, slab_other = gate(
        attend(qkv, text_len), csum, own_cot, zero_slab, slab_other
    )
    csums = [csum] + [shift(csum, "grp", step) for step in range(1, n_grp)]
    slabs = jnp.stack(
        [jnp.where(zl == 0, zero_slab, slab_other), jnp.where(zl == 0, slab_other, zero_slab)]
    )
    zero_rows = lax.all_gather(slabs, ("x", "core", "rep"))

    parts = attn.reshape(n_x, 2, 2, tok, HEAD).transpose(0, 2, 1, 3, 4).reshape(8, 2 * tok, HEAD)
    heads = lax.all_to_all(parts, ("x", "core"), split_axis=0, concat_axis=0, tiled=True)
    level = lax.dynamic_slice_in_dim(gate_table, timestep[0, 0], 1, axis=0)

    def finish(first, own, other):
        at = slice(first * width, first * width + own.shape[1])
        proj = own + other.astype(F32)
        return (hidden[0, 0][:, at].astype(F32) + level[:, at] * proj).astype(BF)

    own_b, other_b = project(zl.reshape(1), heads, weight, 2, 2)
    heads, other_b = gate(heads, other_b)
    other_b = shift(other_b, "zl", 1)
    own_a, other_a = project(zl.reshape(1), heads, weight, 0, 2)
    other_a, csums = gate(other_a, csums)
    other_a = shift(other_a, "zl", 1)
    csum_all = jnp.stack(ordered(csums, source))
    csum_x = lax.all_to_all(csum_all, "x", split_axis=0, concat_axis=0, tiled=True)
    (out_b,) = gate(finish(2, own_b, other_b))
    parts = [send(out_b[:, :width], "grp", [(0, 2)]), send(out_b[:, width:], "grp", [(0, 3)])]
    out_a = finish(0, own_a, other_a)
    parts = [send(out_a[:, width:], "grp", [(0, 1)])] + parts
    out = jnp.concatenate([out_a, out_b], axis=1)
    control = out_a[:, :width]
    for j in range(1, n_grp):
        control = jnp.where(g == j, parts[j - 1], control)
    zero_rows = zero_rows.reshape(n_x, 2, n_rep, 2, slab, width)
    control, zero_rows, csum_x = gate(control, zero_rows, csum_x)

    resid = with_zero(resid_kernel, [control], zero_rows, (n_grp, tok, width), "residual")
    resid, control = gate(resid, control)
    resid = lax.all_to_all(resid, "grp", split_axis=0, concat_axis=0, tiled=True)
    mine_r = jnp.sum(resid.astype(F32), axis=0).astype(BF)
    ctl_x = ring_gather(control, "x")
    partial = grad_partial(x.reshape(1), ctl_x, csum_x)
    rows = width // 16
    partial = partial.reshape(2, 2, n_rep * rows, width).transpose(1, 0, 2, 3)
    mine = pick(partial, core).astype(F32)
    got = shift(pick(partial, 1 - core), "core", 1)
    halves = (mine + got.astype(F32)).astype(BF).reshape(2 * n_rep, rows, width)
    halves, csum_all = gate(halves, csum_all)
    ctrl_grad = with_zero(
        term_kernel, [csum_all, own_cot], zero_rows, (tok, width), "control_gradient"
    )
    halves, mine_r, ctrl_grad = gate(halves, mine_r, ctrl_grad)
    halves = lax.all_to_all(halves, ("zl", "rep"), split_axis=0, concat_axis=0, tiled=True)
    grad = jnp.sum(halves.astype(F32), axis=0).astype(BF)
    grad_zero = lax.ppermute(grad, ("grp", "x"), turn).astype(F32)
    blocks = [mine_r]
    for step in range(1, n_grp):
        pairs = [(i, (i + step) % n_grp) for i in range(n_grp) if (i + step) % n_grp]
        blocks.append(send(mine_r, "grp", pairs))
    resid_all = jnp.concatenate(ordered(blocks, source), axis=1)
    final = jnp.where(is_control, out, (out.astype(F32) + resid_all.astype(F32)).astype(BF))

    return (final[None, None], ctrl_grad[None], grad_zero)


def solution(mesh):
    split = Mesh(mesh.devices.reshape(4, 4, 2, 2, 4), ("grp", "x", "zl", "core", "rep"))
    placed = (
        P("rep", "grp", SEQ, None),
        P("rep", "grp", SEQ, None, None),
        P("rep", "grp", SEQ, None),
        P("rep", "grp"),
        P("rep", "grp"),
        P(),
        P(None, SEQ, "rep"),
        P(SEQ, "grp"),
        P("rep", "grp", SEQ, None),
    )
    return jax.shard_map(
        shards,
        mesh=split,
        in_specs=placed,
        out_specs=(P("rep", "grp", SEQ, None), P("rep", SEQ, "grp"), P((*SEQ, "rep"), "grp")),
        check_vma=False,
    )
```

time: 258 us -> 238 us (0.922)
  the two profiles are of different devices: /device:TPU:112 before, /device:TPU:102 now
where the time goes in v2:
time: 238 us; the launch traced here: 237 us
  waiting for transfers between devices  98.7 us (41%)
  starting transfers between devices  68.1 us (29%)
  Pallas kernels  32.6 us (14%)
  between operations  15.8 us (7%)
  other arithmetic  13.4 us (6%)
  local copies, waits for them, and re-layouts  8.4 us (4%)
    ppermute x6, waiting for transfers between devices, send(): return lax.ppermute(value, axis, pairs)  35.6 us
    ppermute x1, waiting for transfers between devices, shards(): zero_slab = lax.ppermute(zero_slab, ('grp', 'x'), turn)  28.4 us
    ppermute x13, starting transfers between devices, shift(): return lax.ppermute(value, axis, [(i, (i + step) % n) for i in range(n)])  22.5 us
    ppermute x13, waiting for transfers between devices, shift(): return lax.ppermute(value, axis, [(i, (i + step) % n) for i in range(n)])  22.1 us
    ppermute x6, starting transfers between devices, send(): return lax.ppermute(value, axis, pairs)  12.2 us
    pallas_call x1, Pallas kernels, attend(): pl.pallas_call(functools.partial(attend_kernel, text_slots=length // 8, s...  11.6 us
    pallas_call x2, Pallas kernels, with_zero(): pl.pallas_call(kernel, in_specs=[vmem] * len(dense) + [pl.BlockSpec(memor...  11 us
    ppermute x1, waiting for transfers between devices, shards(): grad_zero = lax.ppermute(grad, ('grp', 'x'), turn).astype(F32)  8.65 us
  transfers between devices with their start and end apart: 28, of which 14 were waited for; matrix products, arithmetic and copies ran while one was open for 7% of the time, Pallas kernels for 12%

profile of v2, /device:TPU:102, one launch (start us, length us, event | category | flops | bytes accessed | tf_op | source)
XLA Modules:
  0.0 237.1 jit_solution(11935439358125443190)
XLA Ops:
  7.2 1.8 slice_select_fusion.1
  9.0 2.5 %copy.18 = bf16[1,1,128,2,2048]{2,4,3,1,0:T(8,128)(2,1)S(1)} copy(bf16[1,1,128,2,2048]{4,3,2,1,0:T(2,128)(2,1)} %param.10) | data formatting | bytes 2097152 | tf_op args[1]
  11.6 0.7 copy.19
  12.3 0.4 copy-done.8
  12.6 0.3 copy.20
  12.9 0.3 copy.21
  13.2 1.3 pad_maximum_fusion
  14.5 5.8 %all-to-all-start = ((bf16[16,3,128,128]{3,2,1,0:T(8,128)(2,1)}), bf16[16,3,128,128]{3,2,1,0:T(8,128)(2,1)S(1)}, u32[]{:S(2)}, u32[]{:S(2)}) async-start(bf16[16,3,128,128]{3,2,1,0:T(8,128)(2,1)} %pad_maximum_fusion), calls=%async_computation | async-start | bytes 3145728 | tf_op jit(solution)/shard_map/all_to_all | solution.py:285
  20.4 0.8 dynamic-slice_bitcast_fusion.3
  21.2 3.6 %collective-permute-start = (bf16[128,768]{1,0:T(8,128)(2,1)}, bf16[128,768]{1,0:T(8,128)(2,1)S(1)}, u32[]{:S(2)}, u32[]{:S(2)}) collective-permute-start(bf16[128,768]{1,0:T(8,128)(2,1)} %get-tuple-element.67), channel_id=1, source_target_pairs={{0,64},{64,128},{128,192},{192,0},{1,65},{65,129},{129,193},{193,1... | collective-permute-start | bytes 589832 | tf_op jit(solution)/shard_map/ppermute | solution.py:26
  24.8 0.9 collective-permute-start.1
  25.7 2.9 %collective-permute-start.2 = (bf16[128,768]{1,0:T(8,128)(2,1)S(1)}, bf16[128,768]{1,0:T(8,128)(2,1)S(1)}, u32[]{:S(2)}, u32[]{:S(2)}) collective-permute-start(bf16[128,768]{1,0:T(8,128)(2,1)S(1)} %get-tuple-element.68), channel_id=1, source_target_pairs={{0,192},{64,0},{128,64},{192,128},{1,193},{65,1},{129,65},{193,129... | collective-permute-start | bytes 589832 | tf_op jit(solution)/shard_map/ppermute | solution.py:26
  28.7 4.9 %collective-permute-start.3 = (bf16[48,768]{1,0:T(8,128)(2,1)S(1)}, bf16[48,768]{1,0:T(8,128)(2,1)}, u32[]{:S(2)}, u32[]{:S(2)}) collective-permute-start(bf16[48,768]{1,0:T(8,128)(2,1)S(1)} %constant_dynamic-slice_fusion), channel_id=1, source_target_pairs={{0,0},{16,64},{32,128},{48,192},{64,16},{80,80},{96,144},{112,208}... | collective-permute-start | bytes 221192 | tf_op jit(solution)/shard_map/ppermute | solution.py:289
  34.3 28.4 %collective-permute-done.3 = bf16[48,768]{1,0:T(8,128)(2,1)} collective-permute-done((bf16[48,768]{1,0:T(8,128)(2,1)S(1)}, bf16[48,768]{1,0:T(8,128)(2,1)}, u32[]{:S(2)}, u32[]{:S(2)}) %collective-permute-start.3) | collective-permute-done | bytes 73760 | tf_op jit(solution)/shard_map/ppermute | solution.py:289
  62.7 0.9 collective-permute-start.4
  63.8 0.8 fusion.8.cot_ref
  64.6 11.6 %attend.1 = bf16[2048,128]{1,0:T(8,128)(2,1)S(1)} custom-call(s32[1,1]{1,0:T(1,128)S(6)} %copy.23.tlen_ref, bf16[16,3,128,128]{3,2,1,0:T(8,128)(2,1)S(1)} %all-to-all-done.q_ref.k_ref.v_ref, bf16[16,3,128,128]{3,2,1,0:T(8,128)(2,1)S(1)} %all-to-all-done.q_ref.k_ref.v_ref, bf16[16,3,128,128]{3,2,1,0:T(8,128)(2,1)S(1)} %all-to-all-done.q_ref.k_ref.v_ref), custom_call_target="tpu_custom_call" | custom-call | flops 3221225472 | bytes 2097152 | tf_op jit(solution)/shard_map/attend/pallas_call | solution.py:62
  76.2 0.9 select_bitcast_fusion.9
  77.1 0.7 pad_maximum_fusion.2
  77.8 0.8 copy.22
  78.6 4.5 %all-to-all-start.1 = ((bf16[8,256,128]{2,1,0:T(8,128)(2,1)}), bf16[8,256,128]{2,1,0:T(8,128)(2,1)S(1)}, u32[]{:S(2)}, u32[]{:S(2)}) async-start(bf16[8,256,128]{2,1,0:T(8,128)(2,1)} %bitcast.14), calls=%async_computation.1 | async-start | bytes 1048576 | tf_op jit(solution)/shard_map/all_to_all | solution.py:311
  83.2 1.4 collective-permute-start.5
  84.5 4.3 %collective-permute-start.6 = (bf16[128,768]{1,0:T(8,128)(2,1)S(1)}, bf16[128,768]{1,0:T(8,128)(2,1)S(1)}, u32[]{:S(2)}, u32[]{:S(2)}) collective-permute-start(bf16[128,768]{1,0:T(8,128)(2,1)S(1)} %fusion.4), channel_id=1, source_target_pairs={{0,128},{64,192},{128,0},{192,64},{1,129},{65,193},{129,1},{193,65... | collective-permute-start | bytes 589832 | tf_op jit(solution)/shard_map/ppermute | solution.py:26
  89.5 0.9 dynamic-slice_reduce_fusion.1
  90.4 1.0 all-to-all-done.1.a_ref
  91.4 0.8 copy-done.2
  92.3 4.1 %project.2 = (f32[128,1536]{1,0:T(8,128)}, bf16[128,1536]{1,0:T(8,128)(2,1)}) custom-call(s32[1]{0:T(128)} %bitcast.2.zl_ref, bf16[8,256,128]{2,1,0:T(8,128)(2,1)} %copy-done.2, bf16[8,4,128,768]{3,2,1,0:T(8,128)(2,1)} %bitcast.70), custom_call_target="tpu_custom_call" | custom-call | flops 805306368 | bytes 3145728 | tf_op jit(solution)/shard_map/project/pallas_call | solution.py:117
  96.4 4.0 %project.3 = (f32[128,1536]{1,0:T(8,128)}, bf16[128,1536]{1,0:T(8,128)(2,1)}) custom-call(s32[1]{0:T(128)} %bitcast.2.zl_ref, bf16[8,256,128]{2,1,0:T(8,128)(2,1)} %copy-done.2, bf16[8,4,128,768]{3,2,1,0:T(8,128)(2,1)} %bitcast.71), custom_call_target="tpu_custom_call" | custom-call | flops 805306368 | bytes 3145728 | tf_op jit(solution)/shard_map/project/pallas_call | solution.py:117
  100.4 2.5 %collective-permute-done.7 = bf16[128,768]{1,0:T(8,128)(2,1)S(1)} collective-permute-done((bf16[128,768]{1,0:T(8,128)(2,1)S(1)}, bf16[128,768]{1,0:T(8,128)(2,1)S(1)}, u32[]{:S(2)}, u32[]{:S(2)}) %collective-permute-start.7) | collective-permute-done | bytes 196640 | tf_op jit(solution)/shard_map/ppermute | solution.py:26
  103.0 5.5 %collective-permute-start.8 = (bf16[128,1536]{1,0:T(8,128)(2,1)}, bf16[128,1536]{1,0:T(8,128)(2,1)S(1)}, u32[]{:S(2)}, u32[]{:S(2)}) collective-permute-start(bf16[128,1536]{1,0:T(8,128)(2,1)} %get-tuple-element.35), channel_id=1, source_target_pairs={{0,8},{8,0},{1,9},{9,1},{2,10},{10,2},{3,11},{11,3},{4,12},{12,4},... | collective-permute-start | bytes 1179656 | tf_op jit(solution)/shard_map/ppermute | solution.py:26
  108.6 1.0 pad_maximum_fusion.1.csum_ref
  109.6 4.8 %all-to-all-start.2 = ((bf16[4,128,768]{2,1,0:T(8,128)(2,1)}), bf16[4,128,768]{2,1,0:T(8,128)(2,1)S(1)}, u32[]{:S(2)}, u32[]{:S(2)}) async-start(bf16[4,128,768]{2,1,0:T(8,128)(2,1)} %pad_maximum_fusion.1.csum_ref), calls=%async_computation.2 | async-start | bytes 1572864 | tf_op jit(solution)/shard_map/all_to_all | solution.py:326
  114.4 4.2 %collective-permute-done.8 = bf16[128,1536]{1,0:T(8,128)(2,1)S(1)} collective-permute-done((bf16[128,1536]{1,0:T(8,128)(2,1)}, bf16[128,1536]{1,0:T(8,128)(2,1)S(1)}, u32[]{:S(2)}, u32[]{:S(2)}) %collective-permute-start.8) | collective-permute-done | bytes 393248 | tf_op jit(solution)/shard_map/ppermute | solution.py:26
  118.6 7.8 %collective-permute-done.9 = bf16[128,1536]{1,0:T(8,128)(2,1)S(1)} collective-permute-done((bf16[128,1536]{1,0:T(8,128)(2,1)}, bf16[128,1536]{1,0:T(8,128)(2,1)S(1)}, u32[]{:S(2)}, u32[]{:S(2)}) %collective-permute-start.9) | collective-permute-done | bytes 393248 | tf_op jit(solution)/shard_map/ppermute | solution.py:26
  126.4 0.7 copy-done.10
  127.1 1.7 add_convert_fusion.2
  128.9 0.7 collective-permute-start.10
  129.6 0.7 collective-permute-start.11
  130.3 1.3 collective-permute-start.12
  131.6 18.0 %collective-permute-done.12 = bf16[128,768]{1,0:T(8,128)(2,1)S(1)} collective-permute-done((bf16[128,768]{1,0:T(8,128)(2,1)S(1)}, bf16[128,768]{1,0:T(8,128)(2,1)S(1)}, u32[]{:S(2)}, u32[]{:S(2)}) %collective-permute-start.12) | collective-permute-done | bytes 196640 | tf_op jit(solution)/shard_map/ppermute | solution.py:21
  149.6 0.7 fusion.6.ctl_ref.refs_0_
  150.3 5.0 %residual.1 = bf16[4,128,768]{2,1,0:T(8,128)(2,1)} custom-call(bf16[128,768]{1,0:T(8,128)(2,1)} %fusion.6.ctl_ref.refs_0_, bf16[4,2,4,2,48,768]{5,4,3,2,1,0:T(8,128)(2,1)} %bitcast.72), custom_call_target="tpu_custom_call" | custom-call | flops 603979776 | bytes 4718592 | tf_op jit(solution)/shard_map/residual/pallas_call | solution.py:194
  155.4 0.4 collective-permute-start.13
  155.7 2.6 %collective-permute-start.14 = (bf16[128,768]{1,0:T(8,128)(2,1)S(1)}, bf16[128,768]{1,0:T(8,128)(2,1)S(1)}, u32[]{:S(2)}, u32[]{:S(2)}) collective-permute-start(bf16[128,768]{1,0:T(8,128)(2,1)S(1)} %copy-done.1), channel_id=1, source_target_pairs={{0,32},{16,48},{32,0},{48,16},{1,33},{17,49},{33,1},{49,17},{2,34}... | collective-permute-start | bytes 589832 | tf_op jit(solution)/shard_map/ppermute | solution.py:26
  158.3 4.2 %all-to-all-start.3 = ((bf16[4,128,768]{2,1,0:T(8,128)(2,1)}), bf16[4,128,768]{2,1,0:T(8,128)(2,1)}, u32[]{:S(2)}, u32[]{:S(2)}) async-start(bf16[4,128,768]{2,1,0:T(8,128)(2,1)} %residual.1), calls=%async_computation.3 | async-start | bytes 1572864 | tf_op jit(solution)/shard_map/all_to_all | solution.py:340
  162.5 0.7 collective-permute-done.13.refs_1_
  163.2 1.8 collective-permute-done.14.refs_2_
  165.0 3.0 %collective-permute-done.15.refs_3_ = bf16[128,768]{1,0:T(8,128)(2,1)S(1)} collective-permute-done((bf16[128,768]{1,0:T(8,128)(2,1)S(1)}, bf16[128,768]{1,0:T(8,128)(2,1)S(1)}, u32[]{:S(2)}, u32[]{:S(2)}) %collective-permute-start.15) | collective-permute-done | bytes 196640 | tf_op jit(solution)/shard_map/ppermute | solution.py:26
  168.1 1.9 grad_partial.1
  170.2 2.0 collective-permute-done.16
  172.2 1.0 fusion.1
  173.1 6.0 %control_gradient.1 = bf16[128,768]{1,0:T(8,128)(2,1)} custom-call(bf16[4,128,768]{2,1,0:T(8,128)(2,1)} %pad_maximum_fusion.1.csum_ref, bf16[128,768]{1,0:T(8,128)(2,1)} %fusion.8.cot_ref, bf16[4,2,4,2,48,768]{5,4,3,2,1,0:T(8,128)(2,1)} %bitcast.73), custom_call_target="tpu_custom_call" | custom-call | flops 603979776 | bytes 4718592 | tf_op jit(solution)/shard_map/control_gradient/pallas_call | solution.py:194
  179.1 2.8 %all-to-all-done.3 = bf16[4,128,768]{2,1,0:T(8,128)(2,1)} async-done(((bf16[4,128,768]{2,1,0:T(8,128)(2,1)}), bf16[4,128,768]{2,1,0:T(8,128)(2,1)}, u32[]{:S(2)}, u32[]{:S(2)}) %all-to-all-start.3) | async-done | bytes 786464 | tf_op jit(solution)/shard_map/all_to_all | solution.py:340
  181.9 1.3 reduce_sum.24
  183.2 6.3 %all-to-all-start.4 = ((bf16[8,48,768]{2,1,0:T(8,128)(2,1)}), bf16[8,48,768]{2,1,0:T(8,128)(2,1)S(1)}, u32[]{:S(2)}, u32[]{:S(2)}) async-start(bf16[8,48,768]{2,1,0:T(8,128)(2,1)} %bitcast.29), calls=%async_computation.4 | async-start | bytes 1179648 | tf_op jit(solution)/shard_map/all_to_all | solution.py:354
  189.5 1.3 collective-permute-start.17
  190.8 6.4 %collective-permute-start.18 = (bf16[128,768]{1,0:T(8,128)(2,1)S(1)}, bf16[128,768]{1,0:T(8,128)(2,1)S(1)}, u32[]{:S(2)}, u32[]{:S(2)}) collective-permute-start(bf16[128,768]{1,0:T(8,128)(2,1)S(1)} %reduce_sum.24), channel_id=1, source_target_pairs={{0,128},{64,192},{192,64},{1,129},{65,193},{193,65},{2,130},{66,19... | collective-permute-start | bytes 589832 | tf_op jit(solution)/shard_map/ppermute | solution.py:21
  197.2 1.9 collective-permute-start.19
  199.1 6.8 %collective-permute-done.17 = bf16[128,768]{1,0:T(8,128)(2,1)S(1)} collective-permute-done((bf16[128,768]{1,0:T(8,128)(2,1)S(1)}, bf16[128,768]{1,0:T(8,128)(2,1)S(1)}, u32[]{:S(2)}, u32[]{:S(2)}) %collective-permute-start.17) | collective-permute-done | bytes 196640 | tf_op jit(solution)/shard_map/ppermute | solution.py:21
  205.9 10.9 %collective-permute-done.18 = bf16[128,768]{1,0:T(8,128)(2,1)S(1)} collective-permute-done((bf16[128,768]{1,0:T(8,128)(2,1)S(1)}, bf16[128,768]{1,0:T(8,128)(2,1)S(1)}, u32[]{:S(2)}, u32[]{:S(2)}) %collective-permute-start.18) | collective-permute-done | bytes 196640 | tf_op jit(solution)/shard_map/ppermute | solution.py:21
  217.0 2.8 %collective-permute-start.20 = (bf16[48,768]{1,0:T(8,128)(2,1)S(1)}, bf16[48,768]{1,0:T(8,128)(2,1)S(1)}, u32[]{:S(2)}, u32[]{:S(2)}) collective-permute-start(bf16[48,768]{1,0:T(8,128)(2,1)S(1)} %reduce_sum.25), channel_id=1, source_target_pairs={{0,0},{16,64},{32,128},{48,192},{64,16},{80,80},{96,144},{112,208}... | collective-permute-start | bytes 221192 | tf_op jit(solution)/shard_map/ppermute | solution.py:356
  219.8 1.1 fusion
  220.9 8.7 %collective-permute-done.20 = bf16[48,768]{1,0:T(8,128)(2,1)S(1)} collective-permute-done((bf16[48,768]{1,0:T(8,128)(2,1)S(1)}, bf16[48,768]{1,0:T(8,128)(2,1)S(1)}, u32[]{:S(2)}, u32[]{:S(2)}) %collective-permute-start.20) | collective-permute-done | bytes 73760 | tf_op jit(solution)/shard_map/ppermute | solution.py:356
  229.5 0.7 convert_element_type.106
  (49 shorter events, 0.9 us)
Async XLA Ops:
  7.2 21.5 %copy-start = (bf16[192,768]{1,0:T(8,128)(2,1)S(1)}, bf16[192,768]{1,0:T(8,128)(2,1)}, u32[]{:S(2)}) copy-start(bf16[192,768]{1,0:T(8,128)(2,1)} %param.16) | copy-start | bytes 884740
  7.2 84.3 %all-gather.4.cloned.1.call-start = ((), (), s32[]{:S(2)}) async-start(), calls=%async_computation.5 | async-start | bytes 6488064 | tf_op jit(solution)/shard_map/all_gather | solution.py:279
  11.6 1.0 copy-start.8
  14.5 5.9 %copy-start.5 = (bf16[1,1,128,3072]{3,2,1,0:T(8,128)(2,1)S(1)}, bf16[1,1,128,3072]{3,2,1,0:T(8,128)(2,1)}, u32[]{:S(2)}) copy-start(bf16[1,1,128,3072]{3,2,1,0:T(8,128)(2,1)} %param.17) | copy-start | bytes 2359300
  14.5 50.1 %all-to-all-start = ((bf16[16,3,128,128]{3,2,1,0:T(8,128)(2,1)}), bf16[16,3,128,128]{3,2,1,0:T(8,128)(2,1)S(1)}, u32[]{:S(2)}, u32[]{:S(2)}) async-start(bf16[16,3,128,128]{3,2,1,0:T(8,128)(2,1)} %pad_maximum_fusion), calls=%async_computation | async-start | bytes 3145728 | tf_op jit(solution)/shard_map/all_to_all | solution.py:285
  20.3 130.0 %all-gather.6.cloned.1.call-start = ((), (), s32[]{:S(2)}) async-start(), calls=%async_computation.6 | async-start | bytes 4866048 | tf_op jit(solution)/shard_map/all_gather | solution.py:308
  21.2 42.4 %collective-permute-start = (bf16[128,768]{1,0:T(8,128)(2,1)}, bf16[128,768]{1,0:T(8,128)(2,1)S(1)}, u32[]{:S(2)}, u32[]{:S(2)}) collective-permute-start(bf16[128,768]{1,0:T(8,128)(2,1)} %get-tuple-element.67), channel_id=1, source_target_pairs={{0,64},{64,128},{128,192},{192,0},{1,65},{65,129},{129,193},{193,1... | collective-permute-start | bytes 589832 | tf_op jit(solution)/shard_map/ppermute | solution.py:26
  24.8 38.8 %collective-permute-start.1 = (bf16[128,768]{1,0:T(8,128)(2,1)}, bf16[128,768]{1,0:T(8,128)(2,1)S(1)}, u32[]{:S(2)}, u32[]{:S(2)}) collective-permute-start(bf16[128,768]{1,0:T(8,128)(2,1)} %get-tuple-element.69), channel_id=1, source_target_pairs={{0,128},{64,192},{128,0},{192,64},{1,129},{65,193},{129,1},{193,65... | collective-permute-start | bytes 589832 | tf_op jit(solution)/shard_map/ppermute | solution.py:26
  25.7 37.9 %collective-permute-start.2 = (bf16[128,768]{1,0:T(8,128)(2,1)S(1)}, bf16[128,768]{1,0:T(8,128)(2,1)S(1)}, u32[]{:S(2)}, u32[]{:S(2)}) collective-permute-start(bf16[128,768]{1,0:T(8,128)(2,1)S(1)} %get-tuple-element.68), channel_id=1, source_target_pairs={{0,192},{64,0},{128,64},{192,128},{1,193},{65,1},{129,65},{193,129... | collective-permute-start | bytes 589832 | tf_op jit(solution)/shard_map/ppermute | solution.py:26
  28.7 34.1 %collective-permute-start.3 = (bf16[48,768]{1,0:T(8,128)(2,1)S(1)}, bf16[48,768]{1,0:T(8,128)(2,1)}, u32[]{:S(2)}, u32[]{:S(2)}) collective-permute-start(bf16[48,768]{1,0:T(8,128)(2,1)S(1)} %constant_dynamic-slice_fusion), channel_id=1, source_target_pairs={{0,0},{16,64},{32,128},{48,192},{64,16},{80,80},{96,144},{112,208}... | collective-permute-start | bytes 221192 | tf_op jit(solution)/shard_map/ppermute | solution.py:289
  62.7 13.5 %collective-permute-start.4 = (bf16[48,768]{1,0:T(8,128)(2,1)}, bf16[48,768]{1,0:T(8,128)(2,1)S(1)}, u32[]{:S(2)}, u32[]{:S(2)}) collective-permute-start(bf16[48,768]{1,0:T(8,128)(2,1)} %collective-permute-done.3), channel_id=1, source_target_pairs={{0,8},{8,0},{1,9},{9,1},{2,10},{10,2},{3,11},{11,3},{4,12},{12,4},... | collective-permute-start | bytes 221192 | tf_op jit(solution)/shard_map/ppermute | solution.py:26
  78.6 12.8 %all-to-all-start.1 = ((bf16[8,256,128]{2,1,0:T(8,128)(2,1)}), bf16[8,256,128]{2,1,0:T(8,128)(2,1)S(1)}, u32[]{:S(2)}, u32[]{:S(2)}) async-start(bf16[8,256,128]{2,1,0:T(8,128)(2,1)} %bitcast.14), calls=%async_computation.1 | async-start | bytes 1048576 | tf_op jit(solution)/shard_map/all_to_all | solution.py:311
  83.2 17.3 %collective-permute-start.5 = (bf16[128,768]{1,0:T(8,128)(2,1)S(1)}, bf16[128,768]{1,0:T(8,128)(2,1)S(1)}, u32[]{:S(2)}, u32[]{:S(2)}) collective-permute-start(bf16[128,768]{1,0:T(8,128)(2,1)S(1)} %fusion.4), channel_id=1, source_target_pairs={{0,64},{64,128},{128,192},{192,0},{1,65},{65,129},{129,193},{193,1... | collective-permute-start | bytes 589832 | tf_op jit(solution)/shard_map/ppermute | solution.py:26
  84.5 15.9 %collective-permute-start.6 = (bf16[128,768]{1,0:T(8,128)(2,1)S(1)}, bf16[128,768]{1,0:T(8,128)(2,1)S(1)}, u32[]{:S(2)}, u32[]{:S(2)}) collective-permute-start(bf16[128,768]{1,0:T(8,128)(2,1)S(1)} %fusion.4), channel_id=1, source_target_pairs={{0,128},{64,192},{128,0},{192,64},{1,129},{65,193},{129,1},{193,65... | collective-permute-start | bytes 589832 | tf_op jit(solution)/shard_map/ppermute | solution.py:26
  88.8 14.2 %collective-permute-start.7 = (bf16[128,768]{1,0:T(8,128)(2,1)S(1)}, bf16[128,768]{1,0:T(8,128)(2,1)S(1)}, u32[]{:S(2)}, u32[]{:S(2)}) collective-permute-start(bf16[128,768]{1,0:T(8,128)(2,1)S(1)} %fusion.4), channel_id=1, source_target_pairs={{0,192},{64,0},{128,64},{192,128},{1,193},{65,1},{129,65},{193,129... | collective-permute-start | bytes 589832 | tf_op jit(solution)/shard_map/ppermute | solution.py:26
  91.4 0.8 copy-start.2
  103.0 15.6 %collective-permute-start.8 = (bf16[128,1536]{1,0:T(8,128)(2,1)}, bf16[128,1536]{1,0:T(8,128)(2,1)S(1)}, u32[]{:S(2)}, u32[]{:S(2)}) collective-permute-start(bf16[128,1536]{1,0:T(8,128)(2,1)} %get-tuple-element.35), channel_id=1, source_target_pairs={{0,8},{8,0},{1,9},{9,1},{2,10},{10,2},{3,11},{11,3},{4,12},{12,4},... | collective-permute-start | bytes 1179656 | tf_op jit(solution)/shard_map/ppermute | solution.py:26
  108.4 17.9 %collective-permute-start.9 = (bf16[128,1536]{1,0:T(8,128)(2,1)}, bf16[128,1536]{1,0:T(8,128)(2,1)S(1)}, u32[]{:S(2)}, u32[]{:S(2)}) collective-permute-start(bf16[128,1536]{1,0:T(8,128)(2,1)} %get-tuple-element.37), channel_id=1, source_target_pairs={{0,8},{8,0},{1,9},{9,1},{2,10},{10,2},{3,11},{11,3},{4,12},{12,4},... | collective-permute-start | bytes 1179656 | tf_op jit(solution)/shard_map/ppermute | solution.py:26
  108.6 18.5 %copy-start.6 = (bf16[1,1,128,3072]{3,2,1,0:T(8,128)(2,1)S(1)}, bf16[1,1,128,3072]{3,2,1,0:T(8,128)(2,1)}, u32[]{:S(2)}) copy-start(bf16[1,1,128,3072]{3,2,1,0:T(8,128)(2,1)} %param.9) | copy-start | bytes 2359300
  108.6 18.5 %copy-start.7 = (f32[128,1536]{1,0:T(8,128)S(1)}, f32[128,1536]{1,0:T(8,128)}, u32[]{:S(2)}) copy-start(f32[128,1536]{1,0:T(8,128)} %get-tuple-element.36) | copy-start | bytes 2359300
  109.6 40.7 %all-to-all-start.2 = ((bf16[4,128,768]{2,1,0:T(8,128)(2,1)}), bf16[4,128,768]{2,1,0:T(8,128)(2,1)S(1)}, u32[]{:S(2)}, u32[]{:S(2)}) async-start(bf16[4,128,768]{2,1,0:T(8,128)(2,1)} %pad_maximum_fusion.1.csum_ref), calls=%async_computation.2 | async-start | bytes 1572864 | tf_op jit(solution)/shard_map/all_to_all | solution.py:326
  118.6 7.8 %copy-start.9 = (bf16[128,1536]{1,0:T(8,128)(2,1)}, bf16[128,1536]{1,0:T(8,128)(2,1)S(1)}, u32[]{:S(2)}) copy-start(bf16[128,1536]{1,0:T(8,128)(2,1)S(1)} %collective-permute-done.8) | copy-start | bytes 1179652
  126.4 0.7 copy-start.10
  128.8 21.5 %copy-start.3 = (bf16[128,1536]{1,0:T(8,128)(2,1)}, bf16[128,1536]{1,0:T(8,128)(2,1)S(1)}, u32[]{:S(2)}) copy-start(bf16[128,1536]{1,0:T(8,128)(2,1)S(1)} %get-tuple-element.66) | copy-start | bytes 1179652
  128.9 2.7 %collective-permute-start.10 = (bf16[128,768]{1,0:T(8,128)(2,1)S(1)}, bf16[128,768]{1,0:T(8,128)(2,1)S(1)}, u32[]{:S(2)}, u32[]{:S(2)}) collective-permute-start(bf16[128,768]{1,0:T(8,128)(2,1)S(1)} %get-tuple-element.71), channel_id=1, source_target_pairs={{0,192},{1,193},{2,194},{3,195},{4,196},{5,197},{6,198},{7,199},{8... | collective-permute-start | bytes 589832 | tf_op jit(solution)/shard_map/ppermute | solution.py:21
  129.6 2.0 collective-permute-start.11
  130.3 19.3 %collective-permute-start.12 = (bf16[128,768]{1,0:T(8,128)(2,1)S(1)}, bf16[128,768]{1,0:T(8,128)(2,1)S(1)}, u32[]{:S(2)}, u32[]{:S(2)}) collective-permute-start(bf16[128,768]{1,0:T(8,128)(2,1)S(1)} %slice.44), channel_id=1, source_target_pairs={{0,64},{1,65},{2,66},{3,67},{4,68},{5,69},{6,70},{7,71},{8,72},{9,... | collective-permute-start | bytes 589832 | tf_op jit(solution)/shard_map/ppermute | solution.py:21
  150.3 5.0 %copy-start.1 = (bf16[128,768]{1,0:T(8,128)(2,1)S(1)}, bf16[128,768]{1,0:T(8,128)(2,1)}, u32[]{:S(2)}) copy-start(bf16[128,768]{1,0:T(8,128)(2,1)} %fusion.6.ctl_ref.refs_0_) | copy-start | bytes 589828
  155.4 7.8 %collective-permute-start.13 = (bf16[128,768]{1,0:T(8,128)(2,1)S(1)}, bf16[128,768]{1,0:T(8,128)(2,1)S(1)}, u32[]{:S(2)}, u32[]{:S(2)}) collective-permute-start(bf16[128,768]{1,0:T(8,128)(2,1)S(1)} %copy-done.1), channel_id=1, source_target_pairs={{0,16},{16,32},{32,48},{48,0},{1,17},{17,33},{33,49},{49,1},{2,18}... | collective-permute-start | bytes 589832 | tf_op jit(solution)/shard_map/ppermute | solution.py:26
  155.7 9.3 %collective-permute-start.14 = (bf16[128,768]{1,0:T(8,128)(2,1)S(1)}, bf16[128,768]{1,0:T(8,128)(2,1)S(1)}, u32[]{:S(2)}, u32[]{:S(2)}) collective-permute-start(bf16[128,768]{1,0:T(8,128)(2,1)S(1)} %copy-done.1), channel_id=1, source_target_pairs={{0,32},{16,48},{32,0},{48,16},{1,33},{17,49},{33,1},{49,17},{2,34}... | collective-permute-start | bytes 589832 | tf_op jit(solution)/shard_map/ppermute | solution.py:26
  158.3 9.8 %collective-permute-start.15 = (bf16[128,768]{1,0:T(8,128)(2,1)S(1)}, bf16[128,768]{1,0:T(8,128)(2,1)S(1)}, u32[]{:S(2)}, u32[]{:S(2)}) collective-permute-start(bf16[128,768]{1,0:T(8,128)(2,1)S(1)} %copy-done.1), channel_id=1, source_target_pairs={{0,48},{16,0},{32,16},{48,32},{1,49},{17,1},{33,17},{49,33},{2,50}... | collective-permute-start | bytes 589832 | tf_op jit(solution)/shard_map/ppermute | solution.py:26
  158.3 23.6 %all-to-all-start.3 = ((bf16[4,128,768]{2,1,0:T(8,128)(2,1)}), bf16[4,128,768]{2,1,0:T(8,128)(2,1)}, u32[]{:S(2)}, u32[]{:S(2)}) async-start(bf16[4,128,768]{2,1,0:T(8,128)(2,1)} %residual.1), calls=%async_computation.3 | async-start | bytes 1572864 | tf_op jit(solution)/shard_map/all_to_all | solution.py:340
  170.1 2.1 collective-permute-start.16
  183.2 36.6 %copy-start.4 = (bf16[128,1536]{1,0:T(8,128)(2,1)S(1)}, bf16[128,1536]{1,0:T(8,128)(2,1)}, u32[]{:S(2)}) copy-start(bf16[128,1536]{1,0:T(8,128)(2,1)} %copy-done.3) | copy-start | bytes 1179652
  183.2 33.7 %all-to-all-start.4 = ((bf16[8,48,768]{2,1,0:T(8,128)(2,1)}), bf16[8,48,768]{2,1,0:T(8,128)(2,1)S(1)}, u32[]{:S(2)}, u32[]{:S(2)}) async-start(bf16[8,48,768]{2,1,0:T(8,128)(2,1)} %bitcast.29), calls=%async_computation.4 | async-start | bytes 1179648 | tf_op jit(solution)/shard_map/all_to_all | solution.py:354
  189.5 16.4 %collective-permute-start.17 = (bf16[128,768]{1,0:T(8,128)(2,1)S(1)}, bf16[128,768]{1,0:T(8,128)(2,1)S(1)}, u32[]{:S(2)}, u32[]{:S(2)}) collective-permute-start(bf16[128,768]{1,0:T(8,128)(2,1)S(1)} %reduce_sum.24), channel_id=1, source_target_pairs={{0,192},{128,64},{192,128},{1,193},{129,65},{193,129},{2,194},{130... | collective-permute-start | bytes 589832 | tf_op jit(solution)/shard_map/ppermute | solution.py:21
  190.8 26.0 %collective-permute-start.18 = (bf16[128,768]{1,0:T(8,128)(2,1)S(1)}, bf16[128,768]{1,0:T(8,128)(2,1)S(1)}, u32[]{:S(2)}, u32[]{:S(2)}) collective-permute-start(bf16[128,768]{1,0:T(8,128)(2,1)S(1)} %reduce_sum.24), channel_id=1, source_target_pairs={{0,128},{64,192},{192,64},{1,129},{65,193},{193,65},{2,130},{66,19... | collective-permute-start | bytes 589832 | tf_op jit(solution)/shard_map/ppermute | solution.py:21
  197.2 19.6 %collective-permute-start.19 = (bf16[128,768]{1,0:T(8,128)(2,1)S(1)}, bf16[128,768]{1,0:T(8,128)(2,1)S(1)}, u32[]{:S(2)}, u32[]{:S(2)}) collective-permute-start(bf16[128,768]{1,0:T(8,128)(2,1)S(1)} %reduce_sum.24), channel_id=1, source_target_pairs={{0,64},{64,128},{128,192},{1,65},{65,129},{129,193},{2,66},{66,130... | collective-permute-start | bytes 589832 | tf_op jit(solution)/shard_map/ppermute | solution.py:21
  217.0 12.6 %collective-permute-start.20 = (bf16[48,768]{1,0:T(8,128)(2,1)S(1)}, bf16[48,768]{1,0:T(8,128)(2,1)S(1)}, u32[]{:S(2)}, u32[]{:S(2)}) collective-permute-start(bf16[48,768]{1,0:T(8,128)(2,1)S(1)} %reduce_sum.25), channel_id=1, source_target_pairs={{0,0},{16,64},{32,128},{48,192},{64,16},{80,80},{96,144},{112,208}... | collective-permute-start | bytes 221192 | tf_op jit(solution)/shard_map/ppermute | solution.py:356
Sparse Core Ops, SparseCore 0:
  11.2 62.4 all-gather.3
  77.9 56.2 all-gather.5

commit v3 on v2

--- a/solution.py
+++ b/solution.py
@@ -275,12 +275,11 @@
     def source(step):
         return (g - step) % n_grp
 
-    w_sel = jnp.where(is_control, w_out[0], w_out[1])
-    weight = lax.all_gather(w_sel, ("x", "core", "rep")).reshape(8, n_rep, *w_sel.shape)
-
     pair = queries_keys[0, 0].reshape(tok, 2, H, HEAD).transpose(2, 1, 0, 3)
     vals = values[0, 0].reshape(tok, 1, H, HEAD).transpose(2, 1, 0, 3)
-    qkv = jnp.concatenate([pair, vals], axis=1)
+    qkv, w_both = gate(jnp.concatenate([pair, vals], axis=1), w_out)
+    w_sel = jnp.where(is_control, w_both[0], w_both[1])
+    weight = lax.all_gather(w_sel, ("x", "core", "rep")).reshape(8, n_rep, *w_sel.shape)
 
     qkv = lax.all_to_all(qkv, SEQ, split_axis=0, concat_axis=0, tiled=True)
     turn = [(i * n_grp + j, j * n_grp + i) for i in range(n_x) for j in range(n_grp)]
@@ -288,27 +287,29 @@
     zero_slab = lax.dynamic_slice_in_dim(w_zero, rep * slab, slab, axis=0)
     zero_slab = lax.ppermute(zero_slab, ("grp", "x"), turn)
 
+    qkv, zero_slab, cot = gate(qkv, zero_slab, cotangent[0, 0])
+
     def cot_block(index):
-        return lax.dynamic_slice_in_dim(cotangent[0, 0], index * width, width, axis=1)
+        return lax.dynamic_slice_in_dim(cot, index * width, width, axis=1)
 
     cots = [cot_block(g)] + [
         shift(cot_block((g + step) % n_grp), "grp", step) for step in range(1, n_grp)
     ]
+    slab_other = shift(zero_slab, "zl", 1)
+    attn, zero_slab, slab_other, cots = gate(
+        attend(qkv, text_len), zero_slab, slab_other, cots
+    )
+    slabs = jnp.stack(
+        [jnp.where(zl == 0, zero_slab, slab_other), jnp.where(zl == 0, slab_other, zero_slab)]
+    )
+    zero_rows = lax.all_gather(slabs, ("x", "core", "rep"))
+
+    parts = attn.reshape(n_x, 2, 2, tok, HEAD).transpose(0, 2, 1, 3, 4).reshape(8, 2 * tok, HEAD)
+    heads = lax.all_to_all(parts, ("x", "core"), split_axis=0, concat_axis=0, tiled=True)
     csum = sum(jnp.where(source(step) == 0, 0.0, cots[step].astype(F32)) for step in range(n_grp))
     own_cot = sum(jnp.where(source(step) == 0, cots[step], 0) for step in range(n_grp))
     csum = csum.astype(BF)
-    slab_other = shift(zero_slab, "zl", 1)
-    attn, csum, own_cot, zero_slab, slab_other = gate(
-        attend(qkv, text_len), csum, own_cot, zero_slab, slab_other
-    )
     csums = [csum] + [shift(csum, "grp", step) for step in range(1, n_grp)]
-    slabs = jnp.stack(
-        [jnp.where(zl == 0, zero_slab, slab_other), jnp.where(zl == 0, slab_other, zero_slab)]
-    )
-    zero_rows = lax.all_gather(slabs, ("x", "core", "rep"))
-
-    parts = attn.reshape(n_x, 2, 2, tok, HEAD).transpose(0, 2, 1, 3, 4).reshape(8, 2 * tok, HEAD)
-    heads = lax.all_to_all(parts, ("x", "core"), split_axis=0, concat_axis=0, tiled=True)
     level = lax.dynamic_slice_in_dim(gate_table, timestep[0, 0], 1, axis=0)
 
     def finish(first, own, other):
@@ -322,13 +323,13 @@
     own_a, other_a = project(zl.reshape(1), heads, weight, 0, 2)
     other_a, csums = gate(other_a, csums)
     other_a = shift(other_a, "zl", 1)
-    csum_all = jnp.stack(ordered(csums, source))
-    csum_x = lax.all_to_all(csum_all, "x", split_axis=0, concat_axis=0, tiled=True)
     (out_b,) = gate(finish(2, own_b, other_b))
     parts = [send(out_b[:, :width], "grp", [(0, 2)]), send(out_b[:, width:], "grp", [(0, 3)])]
     out_a = finish(0, own_a, other_a)
     parts = [send(out_a[:, width:], "grp", [(0, 1)])] + parts
     out = jnp.concatenate([out_a, out_b], axis=1)
+    csum_all = jnp.stack(ordered(csums, source))
+    csum_x = lax.all_to_all(csum_all, "x", split_axis=0, concat_axis=0, tiled=True)
     control = out_a[:, :width]
     for j in range(1, n_grp):
         control = jnp.where(g == j, parts[j - 1], control)
@@ -358,6 +359,7 @@
     for step in range(1, n_grp):
         pairs = [(i, (i + step) % n_grp) for i in range(n_grp) if (i + step) % n_grp]
         blocks.append(send(mine_r, "grp", pairs))
+    blocks, grad_zero = gate(blocks, grad_zero)
     resid_all = jnp.concatenate(ordered(blocks, source), axis=1)
     final = jnp.where(is_control, out, (out.astype(F32) + resid_all.astype(F32)).astype(BF))
 

time: 238 us -> 224 us (0.941)
  the two profiles are of different devices: /device:TPU:102 before, /device:TPU:193 now
where the time goes in v3:
time: 224 us; the launch traced here: 223 us
  waiting for transfers between devices  87.7 us (39%)
  starting transfers between devices  67.3 us (30%)
  Pallas kernels  32.6 us (15%)
  between operations  15.8 us (7%)
  other arithmetic  12.3 us (5%)
  local copies, waits for them, and re-layouts  6.98 us (3%)
    ppermute x13, waiting for transfers between devices, shift(): return lax.ppermute(value, axis, [(i, (i + step) % n) for i in range(n)])  27.3 us
    ppermute x13, starting transfers between devices, shift(): return lax.ppermute(value, axis, [(i, (i + step) % n) for i in range(n)])  19.4 us
    ppermute x1, waiting for transfers between devices, shards(): zero_slab = lax.ppermute(zero_slab, ('grp', 'x'), turn)  18.2 us
    ppermute x1, waiting for transfers between devices, shards(): grad_zero = lax.ppermute(grad, ('grp', 'x'), turn).astype(F32)  17.4 us
    ppermute x6, waiting for transfers between devices, send(): return lax.ppermute(value, axis, pairs)  16.5 us
    ppermute x6, starting transfers between devices, send(): return lax.ppermute(value, axis, pairs)  12.1 us
    pallas_call x1, Pallas kernels, attend(): pl.pallas_call(functools.partial(attend_kernel, text_slots=length // 8, s...  11.5 us
    pallas_call x2, Pallas kernels, with_zero(): pl.pallas_call(kernel, in_specs=[vmem] * len(dense) + [pl.BlockSpec(memor...  11 us
  transfers between devices with their start and end apart: 28, of which 11 were waited for; matrix products, arithmetic and copies ran while one was open for 4% of the time, Pallas kernels for 12%

profile of v3, /device:TPU:193, one launch (start us, length us, event | category | flops | bytes accessed | tf_op | source)
XLA Modules:
  0.0 222.7 jit_solution(5226206016461127157)
XLA Ops:
  7.2 2.6 %copy.18 = bf16[1,1,128,2,2048]{2,4,3,1,0:T(8,128)(2,1)S(1)} copy(bf16[1,1,128,2,2048]{4,3,2,1,0:T(2,128)(2,1)} %param.10) | data formatting | bytes 2097152 | tf_op args[1]
  9.8 0.7 copy.19
  10.5 0.4 copy-done.12
  10.9 0.3 copy.20
  11.1 0.3 copy.21
  11.4 1.3 pad_maximum_fusion
  12.8 0.7 slice_select_fusion.1
  13.5 5.6 %all-to-all-start = ((bf16[16,3,128,128]{3,2,1,0:T(8,128)(2,1)}), bf16[16,3,128,128]{3,2,1,0:T(8,128)(2,1)S(1)}, u32[]{:S(2)}, u32[]{:S(2)}) async-start(bf16[16,3,128,128]{3,2,1,0:T(8,128)(2,1)} %pad_maximum_fusion), calls=%async_computation | async-start | bytes 3145728 | tf_op jit(solution)/shard_map/all_to_all | solution.py:284
  19.2 2.7 %collective-permute-start = (bf16[48,768]{1,0:T(8,128)(2,1)S(1)}, bf16[48,768]{1,0:T(8,128)(2,1)S(1)}, u32[]{:S(2)}, u32[]{:S(2)}) collective-permute-start(bf16[48,768]{1,0:T(8,128)(2,1)S(1)} %constant_dynamic-slice_fusion.4), channel_id=1, source_target_pairs={{0,0},{16,64},{32,128},{48,192},{64,16},{80,80},{96,144},{112,208}... | collective-permute-start | bytes 221192 | tf_op jit(solution)/shard_map/ppermute | solution.py:288
  22.6 18.2 %collective-permute-done = bf16[48,768]{1,0:T(8,128)(2,1)S(1)} collective-permute-done((bf16[48,768]{1,0:T(8,128)(2,1)S(1)}, bf16[48,768]{1,0:T(8,128)(2,1)S(1)}, u32[]{:S(2)}, u32[]{:S(2)}) %collective-permute-start) | collective-permute-done | bytes 73760 | tf_op jit(solution)/shard_map/ppermute | solution.py:288
  40.8 3.1 %all-to-all-done.q_ref.k_ref.v_ref = bf16[16,3,128,128]{3,2,1,0:T(8,128)(2,1)S(1)} async-done(((bf16[16,3,128,128]{3,2,1,0:T(8,128)(2,1)}), bf16[16,3,128,128]{3,2,1,0:T(8,128)(2,1)S(1)}, u32[]{:S(2)}, u32[]{:S(2)}) %all-to-all-start) | async-done | bytes 1572896 | tf_op jit(solution)/shard_map/all_to_all | solution.py:284
  43.9 0.1 collective-permute-start.2
  44.0 7.0 %collective-permute-start.3 = (bf16[128,768]{1,0:T(8,128)(2,1)S(1)}, bf16[128,768]{1,0:T(8,128)(2,1)S(1)}, u32[]{:S(2)}, u32[]{:S(2)}) collective-permute-start(bf16[128,768]{1,0:T(8,128)(2,1)S(1)} %get-tuple-element.92), channel_id=1, source_target_pairs={{0,128},{64,192},{128,0},{192,64},{1,129},{65,193},{129,1},{193,65... | collective-permute-start | bytes 589832 | tf_op jit(solution)/shard_map/ppermute | solution.py:26
  51.0 1.4 collective-permute-start.1
  52.4 11.5 %attend.1 = bf16[2048,128]{1,0:T(8,128)(2,1)S(1)} custom-call(s32[1,1]{1,0:T(1,128)S(6)} %copy.23.tlen_ref, bf16[16,3,128,128]{3,2,1,0:T(8,128)(2,1)S(1)} %all-to-all-done.q_ref.k_ref.v_ref, bf16[16,3,128,128]{3,2,1,0:T(8,128)(2,1)S(1)} %all-to-all-done.q_ref.k_ref.v_ref, bf16[16,3,128,128]{3,2,1,0:T(8,128)(2,1)S(1)} %all-to-all-done.q_ref.k_ref.v_ref), custom_call_target="tpu_custom_call" | custom-call | flops 3221225472 | bytes 2097152 | tf_op jit(solution)/shard_map/attend/pallas_call | solution.py:62
  64.0 8.0 %collective-permute-done.1 = bf16[48,768]{1,0:T(8,128)(2,1)S(1)} collective-permute-done((bf16[48,768]{1,0:T(8,128)(2,1)S(1)}, bf16[48,768]{1,0:T(8,128)(2,1)S(1)}, u32[]{:S(2)}, u32[]{:S(2)}) %collective-permute-start.1) | collective-permute-done | bytes 73760 | tf_op jit(solution)/shard_map/ppermute | solution.py:26
  72.0 0.8 pad_maximum_fusion.2
  72.8 0.8 copy.22
  73.7 4.0 %all-to-all-start.1 = ((bf16[8,256,128]{2,1,0:T(8,128)(2,1)}), bf16[8,256,128]{2,1,0:T(8,128)(2,1)S(1)}, u32[]{:S(2)}, u32[]{:S(2)}) async-start(bf16[8,256,128]{2,1,0:T(8,128)(2,1)} %bitcast.10), calls=%async_computation.1 | async-start | bytes 1048576 | tf_op jit(solution)/shard_map/all_to_all | solution.py:308
  77.7 0.2 add_convert_fusion.3
  77.9 0.6 collective-permute-start.5
  78.5 1.2 collective-permute-start.6
  79.7 1.0 collective-permute-start.7
  81.3 0.9 dynamic-slice_reduce_fusion.1
  82.3 4.9 %all-to-all-done.1.a_ref = bf16[8,256,128]{2,1,0:T(8,128)(2,1)S(1)} async-done(((bf16[8,256,128]{2,1,0:T(8,128)(2,1)}), bf16[8,256,128]{2,1,0:T(8,128)(2,1)S(1)}, u32[]{:S(2)}, u32[]{:S(2)}) %all-to-all-start.1) | async-done | bytes 524320 | tf_op jit(solution)/shard_map/all_to_all | solution.py:308
  87.2 0.8 copy-done.2
  88.0 4.1 %project.2 = (f32[128,1536]{1,0:T(8,128)}, bf16[128,1536]{1,0:T(8,128)(2,1)}) custom-call(s32[1]{0:T(128)} %bitcast.2.zl_ref, bf16[8,256,128]{2,1,0:T(8,128)(2,1)} %copy-done.2, bf16[8,4,128,768]{3,2,1,0:T(8,128)(2,1)} %bitcast.51), custom_call_target="tpu_custom_call" | custom-call | flops 805306368 | bytes 3145728 | tf_op jit(solution)/shard_map/project/pallas_call | solution.py:117
  92.1 4.0 %project.3 = (f32[128,1536]{1,0:T(8,128)}, bf16[128,1536]{1,0:T(8,128)(2,1)}) custom-call(s32[1]{0:T(128)} %bitcast.2.zl_ref, bf16[8,256,128]{2,1,0:T(8,128)(2,1)} %copy-done.2, bf16[8,4,128,768]{3,2,1,0:T(8,128)(2,1)} %bitcast.52), custom_call_target="tpu_custom_call" | custom-call | flops 805306368 | bytes 3145728 | tf_op jit(solution)/shard_map/project/pallas_call | solution.py:117
  96.2 4.4 %collective-permute-done.7 = bf16[128,768]{1,0:T(8,128)(2,1)S(1)} collective-permute-done((bf16[128,768]{1,0:T(8,128)(2,1)S(1)}, bf16[128,768]{1,0:T(8,128)(2,1)S(1)}, u32[]{:S(2)}, u32[]{:S(2)}) %collective-permute-start.7) | collective-permute-done | bytes 196640 | tf_op jit(solution)/shard_map/ppermute | solution.py:26
  100.6 1.5 collective-permute-start.9
  102.1 0.1 select_bitcast_fusion.7
  102.2 1.0 pad_maximum_fusion.1.csum_ref
  103.2 4.1 %all-to-all-start.2 = ((bf16[4,128,768]{2,1,0:T(8,128)(2,1)}), bf16[4,128,768]{2,1,0:T(8,128)(2,1)S(1)}, u32[]{:S(2)}, u32[]{:S(2)}) async-start(bf16[4,128,768]{2,1,0:T(8,128)(2,1)} %pad_maximum_fusion.1.csum_ref), calls=%async_computation.2 | async-start | bytes 1572864 | tf_op jit(solution)/shard_map/all_to_all | solution.py:332
  107.3 3.7 %collective-permute-done.8 = bf16[128,1536]{1,0:T(8,128)(2,1)S(1)} collective-permute-done((bf16[128,1536]{1,0:T(8,128)(2,1)}, bf16[128,1536]{1,0:T(8,128)(2,1)S(1)}, u32[]{:S(2)}, u32[]{:S(2)}) %collective-permute-start.8) | collective-permute-done | bytes 393248 | tf_op jit(solution)/shard_map/ppermute | solution.py:26
  111.0 8.5 %collective-permute-done.9 = bf16[128,1536]{1,0:T(8,128)(2,1)} collective-permute-done((bf16[128,1536]{1,0:T(8,128)(2,1)}, bf16[128,1536]{1,0:T(8,128)(2,1)}, u32[]{:S(2)}, u32[]{:S(2)}) %collective-permute-start.9) | collective-permute-done | bytes 393248 | tf_op jit(solution)/shard_map/ppermute | solution.py:26
  119.6 1.7 add_convert_fusion.2
  121.3 1.3 collective-permute-start.10
  122.6 0.7 collective-permute-start.11
  123.3 0.7 collective-permute-start.12
  124.0 16.4 %collective-permute-done.10 = bf16[128,768]{1,0:T(8,128)(2,1)S(1)} collective-permute-done((bf16[128,768]{1,0:T(8,128)(2,1)S(1)}, bf16[128,768]{1,0:T(8,128)(2,1)S(1)}, u32[]{:S(2)}, u32[]{:S(2)}) %collective-permute-start.10) | collective-permute-done | bytes 196640 | tf_op jit(solution)/shard_map/ppermute | solution.py:21
  140.4 0.7 fusion.3.ctl_ref.refs_0_
  141.2 5.0 %residual.1 = bf16[4,128,768]{2,1,0:T(8,128)(2,1)} custom-call(bf16[128,768]{1,0:T(8,128)(2,1)} %fusion.3.ctl_ref.refs_0_, bf16[4,2,4,2,48,768]{5,4,3,2,1,0:T(8,128)(2,1)} %bitcast.53), custom_call_target="tpu_custom_call" | custom-call | flops 603979776 | bytes 4718592 | tf_op jit(solution)/shard_map/residual/pallas_call | solution.py:194
  146.2 1.5 collective-permute-start.13
  147.8 2.4 %collective-permute-start.14 = (bf16[128,768]{1,0:T(8,128)(2,1)S(1)}, bf16[128,768]{1,0:T(8,128)(2,1)S(1)}, u32[]{:S(2)}, u32[]{:S(2)}) collective-permute-start(bf16[128,768]{1,0:T(8,128)(2,1)S(1)} %copy-done.1), channel_id=1, source_target_pairs={{0,32},{16,48},{32,0},{48,16},{1,33},{17,49},{33,1},{49,17},{2,34}... | collective-permute-start | bytes 589832 | tf_op jit(solution)/shard_map/ppermute | solution.py:26
  150.2 1.2 collective-permute-start.15
  151.4 4.8 %all-to-all-start.3 = ((bf16[4,128,768]{2,1,0:T(8,128)(2,1)}), bf16[4,128,768]{2,1,0:T(8,128)(2,1)}, u32[]{:S(2)}, u32[]{:S(2)}) async-start(bf16[4,128,768]{2,1,0:T(8,128)(2,1)} %residual.1), calls=%async_computation.3 | async-start | bytes 1572864 | tf_op jit(solution)/shard_map/all_to_all | solution.py:341
  156.2 2.6 %collective-permute-done.14.refs_2_ = bf16[128,768]{1,0:T(8,128)(2,1)S(1)} collective-permute-done((bf16[128,768]{1,0:T(8,128)(2,1)S(1)}, bf16[128,768]{1,0:T(8,128)(2,1)S(1)}, u32[]{:S(2)}, u32[]{:S(2)}) %collective-permute-start.14) | collective-permute-done | bytes 196640 | tf_op jit(solution)/shard_map/ppermute | solution.py:26
  158.9 1.9 grad_partial.1
  160.9 1.5 collective-permute-start.16
  162.4 1.6 select_add_fusion.cot_ref
  164.0 1.0 fusion.1
  165.0 6.0 %control_gradient.1 = bf16[128,768]{1,0:T(8,128)(2,1)} custom-call(bf16[4,128,768]{2,1,0:T(8,128)(2,1)} %pad_maximum_fusion.1.csum_ref, bf16[128,768]{1,0:T(8,128)(2,1)} %select_add_fusion.cot_ref, bf16[4,2,4,2,48,768]{5,4,3,2,1,0:T(8,128)(2,1)} %bitcast.54), custom_call_target="tpu_custom_call" | custom-call | flops 603979776 | bytes 4718592 | tf_op jit(solution)/shard_map/control_gradient/pallas_call | solution.py:194
  170.9 0.3 all-to-all-done.3
  171.2 1.3 reduce_sum.24
  172.5 9.2 %all-to-all-start.4 = ((bf16[8,48,768]{2,1,0:T(8,128)(2,1)}), bf16[8,48,768]{2,1,0:T(8,128)(2,1)S(1)}, u32[]{:S(2)}, u32[]{:S(2)}) async-start(bf16[8,48,768]{2,1,0:T(8,128)(2,1)} %bitcast.25), calls=%async_computation.4 | async-start | bytes 1179648 | tf_op jit(solution)/shard_map/all_to_all | solution.py:355
  181.7 1.3 collective-permute-start.17
  183.0 6.3 %collective-permute-start.18 = (bf16[128,768]{1,0:T(8,128)(2,1)S(1)}, bf16[128,768]{1,0:T(8,128)(2,1)S(1)}, u32[]{:S(2)}, u32[]{:S(2)}) collective-permute-start(bf16[128,768]{1,0:T(8,128)(2,1)S(1)} %reduce_sum.24), channel_id=1, source_target_pairs={{0,128},{64,192},{192,64},{1,129},{65,193},{193,65},{2,130},{66,19... | collective-permute-start | bytes 589832 | tf_op jit(solution)/shard_map/ppermute | solution.py:21
  189.2 1.9 collective-permute-start.19
  191.2 0.1 reduce_sum.25
  191.3 5.3 %collective-permute-start.20 = (bf16[48,768]{1,0:T(8,128)(2,1)S(1)}, bf16[48,768]{1,0:T(8,128)(2,1)S(1)}, u32[]{:S(2)}, u32[]{:S(2)}) collective-permute-start(bf16[48,768]{1,0:T(8,128)(2,1)S(1)} %reduce_sum.25), channel_id=1, source_target_pairs={{0,0},{16,64},{32,128},{48,192},{64,16},{80,80},{96,144},{112,208}... | collective-permute-start | bytes 221192 | tf_op jit(solution)/shard_map/ppermute | solution.py:357
  196.6 17.4 %collective-permute-done.20 = bf16[48,768]{1,0:T(8,128)(2,1)S(1)} collective-permute-done((bf16[48,768]{1,0:T(8,128)(2,1)S(1)}, bf16[48,768]{1,0:T(8,128)(2,1)S(1)}, u32[]{:S(2)}, u32[]{:S(2)}) %collective-permute-start.20) | collective-permute-done | bytes 73760 | tf_op jit(solution)/shard_map/ppermute | solution.py:357
  214.0 0.7 convert_element_type.103
  214.7 0.1 select_bitcast_fusion.3
  214.8 1.1 fusion
  (57 shorter events, 0.4 us)
Async XLA Ops:
  7.2 12.0 %copy-start = (bf16[192,768]{1,0:T(8,128)(2,1)S(1)}, bf16[192,768]{1,0:T(8,128)(2,1)}, u32[]{:S(2)}) copy-start(bf16[192,768]{1,0:T(8,128)(2,1)} %param.16) | copy-start | bytes 884740
  7.2 80.0 %all-gather.4.cloned.1.call-start = ((), (), s32[]{:S(2)}) async-start(), calls=%async_computation.5 | async-start | bytes 6488064 | tf_op jit(solution)/shard_map/all_gather | solution.py:282
  9.8 1.0 copy-start.12
  11.4 1.4 copy-start.13
  13.5 30.3 %copy-start.6 = (bf16[1,1,128,3072]{3,2,1,0:T(8,128)(2,1)S(1)}, bf16[1,1,128,3072]{3,2,1,0:T(8,128)(2,1)}, u32[]{:S(2)}) copy-start(bf16[1,1,128,3072]{3,2,1,0:T(8,128)(2,1)} %param.17) | copy-start | bytes 2359300
  13.5 30.3 %all-to-all-start = ((bf16[16,3,128,128]{3,2,1,0:T(8,128)(2,1)}), bf16[16,3,128,128]{3,2,1,0:T(8,128)(2,1)S(1)}, u32[]{:S(2)}, u32[]{:S(2)}) async-start(bf16[16,3,128,128]{3,2,1,0:T(8,128)(2,1)} %pad_maximum_fusion), calls=%async_computation | async-start | bytes 3145728 | tf_op jit(solution)/shard_map/all_to_all | solution.py:284
  19.1 122.1 %all-gather.6.cloned.1.call-start = ((), (), s32[]{:S(2)}) async-start(), calls=%async_computation.6 | async-start | bytes 4866048 | tf_op jit(solution)/shard_map/all_gather | solution.py:305
  19.2 21.6 %collective-permute-start = (bf16[48,768]{1,0:T(8,128)(2,1)S(1)}, bf16[48,768]{1,0:T(8,128)(2,1)S(1)}, u32[]{:S(2)}, u32[]{:S(2)}) collective-permute-start(bf16[48,768]{1,0:T(8,128)(2,1)S(1)} %constant_dynamic-slice_fusion.4), channel_id=1, source_target_pairs={{0,0},{16,64},{32,128},{48,192},{64,16},{80,80},{96,144},{112,208}... | collective-permute-start | bytes 221192 | tf_op jit(solution)/shard_map/ppermute | solution.py:288
  43.9 33.8 %copy-start.5 = (bf16[128,768]{1,0:T(8,128)(2,1)}, bf16[128,768]{1,0:T(8,128)(2,1)S(1)}, u32[]{:S(2)}) copy-start(bf16[128,768]{1,0:T(8,128)(2,1)S(1)} %get-tuple-element.51) | copy-start | bytes 589828
  43.9 28.0 %collective-permute-start.2 = (bf16[128,768]{1,0:T(8,128)(2,1)S(1)}, bf16[128,768]{1,0:T(8,128)(2,1)S(1)}, u32[]{:S(2)}, u32[]{:S(2)}) collective-permute-start(bf16[128,768]{1,0:T(8,128)(2,1)S(1)} %get-tuple-element.93), channel_id=1, source_target_pairs={{0,64},{64,128},{128,192},{192,0},{1,65},{65,129},{129,193},{193,1... | collective-permute-start | bytes 589832 | tf_op jit(solution)/shard_map/ppermute | solution.py:26
  44.0 27.9 %collective-permute-start.3 = (bf16[128,768]{1,0:T(8,128)(2,1)S(1)}, bf16[128,768]{1,0:T(8,128)(2,1)S(1)}, u32[]{:S(2)}, u32[]{:S(2)}) collective-permute-start(bf16[128,768]{1,0:T(8,128)(2,1)S(1)} %get-tuple-element.92), channel_id=1, source_target_pairs={{0,128},{64,192},{128,0},{192,64},{1,129},{65,193},{129,1},{193,65... | collective-permute-start | bytes 589832 | tf_op jit(solution)/shard_map/ppermute | solution.py:26
  51.0 21.0 %collective-permute-start.4 = (bf16[128,768]{1,0:T(8,128)(2,1)S(1)}, bf16[128,768]{1,0:T(8,128)(2,1)S(1)}, u32[]{:S(2)}, u32[]{:S(2)}) collective-permute-start(bf16[128,768]{1,0:T(8,128)(2,1)S(1)} %get-tuple-element.91), channel_id=1, source_target_pairs={{0,192},{64,0},{128,64},{192,128},{1,193},{65,1},{129,65},{193,129... | collective-permute-start | bytes 589832 | tf_op jit(solution)/shard_map/ppermute | solution.py:26
  51.0 20.9 %collective-permute-start.1 = (bf16[48,768]{1,0:T(8,128)(2,1)S(1)}, bf16[48,768]{1,0:T(8,128)(2,1)S(1)}, u32[]{:S(2)}, u32[]{:S(2)}) collective-permute-start(bf16[48,768]{1,0:T(8,128)(2,1)S(1)} %collective-permute-done), channel_id=1, source_target_pairs={{0,8},{8,0},{1,9},{9,1},{2,10},{10,2},{3,11},{11,3},{4,12},{12,4},... | collective-permute-start | bytes 221192 | tf_op jit(solution)/shard_map/ppermute | solution.py:26
  72.0 5.9 %copy-start.9 = (bf16[128,768]{1,0:T(8,128)(2,1)}, bf16[128,768]{1,0:T(8,128)(2,1)S(1)}, u32[]{:S(2)}) copy-start(bf16[128,768]{1,0:T(8,128)(2,1)S(1)} %collective-permute-done.2) | copy-start | bytes 589828
  72.0 5.9 %copy-start.10 = (bf16[128,768]{1,0:T(8,128)(2,1)}, bf16[128,768]{1,0:T(8,128)(2,1)S(1)}, u32[]{:S(2)}) copy-start(bf16[128,768]{1,0:T(8,128)(2,1)S(1)} %collective-permute-done.3) | copy-start | bytes 589828
  72.0 5.9 %copy-start.11 = (bf16[128,768]{1,0:T(8,128)(2,1)}, bf16[128,768]{1,0:T(8,128)(2,1)S(1)}, u32[]{:S(2)}) copy-start(bf16[128,768]{1,0:T(8,128)(2,1)S(1)} %collective-permute-done.4) | copy-start | bytes 589828
  73.7 13.5 %all-to-all-start.1 = ((bf16[8,256,128]{2,1,0:T(8,128)(2,1)}), bf16[8,256,128]{2,1,0:T(8,128)(2,1)S(1)}, u32[]{:S(2)}, u32[]{:S(2)}) async-start(bf16[8,256,128]{2,1,0:T(8,128)(2,1)} %bitcast.10), calls=%async_computation.1 | async-start | bytes 1048576 | tf_op jit(solution)/shard_map/all_to_all | solution.py:308
  77.9 18.3 %collective-permute-start.5 = (bf16[128,768]{1,0:T(8,128)(2,1)S(1)}, bf16[128,768]{1,0:T(8,128)(2,1)S(1)}, u32[]{:S(2)}, u32[]{:S(2)}) collective-permute-start(bf16[128,768]{1,0:T(8,128)(2,1)S(1)} %add_convert_fusion.3), channel_id=1, source_target_pairs={{0,64},{64,128},{128,192},{192,0},{1,65},{65,129},{129,193},{193,1... | collective-permute-start | bytes 589832 | tf_op jit(solution)/shard_map/ppermute | solution.py:26
  78.5 17.7 %collective-permute-start.6 = (bf16[128,768]{1,0:T(8,128)(2,1)S(1)}, bf16[128,768]{1,0:T(8,128)(2,1)S(1)}, u32[]{:S(2)}, u32[]{:S(2)}) collective-permute-start(bf16[128,768]{1,0:T(8,128)(2,1)S(1)} %add_convert_fusion.3), channel_id=1, source_target_pairs={{0,128},{64,192},{128,0},{192,64},{1,129},{65,193},{129,1},{193,65... | collective-permute-start | bytes 589832 | tf_op jit(solution)/shard_map/ppermute | solution.py:26
  79.7 20.9 %collective-permute-start.7 = (bf16[128,768]{1,0:T(8,128)(2,1)S(1)}, bf16[128,768]{1,0:T(8,128)(2,1)S(1)}, u32[]{:S(2)}, u32[]{:S(2)}) collective-permute-start(bf16[128,768]{1,0:T(8,128)(2,1)S(1)} %add_convert_fusion.3), channel_id=1, source_target_pairs={{0,192},{64,0},{128,64},{192,128},{1,193},{65,1},{129,65},{193,129... | collective-permute-start | bytes 589832 | tf_op jit(solution)/shard_map/ppermute | solution.py:26
  87.2 0.8 copy-start.2
  100.6 10.4 %collective-permute-start.8 = (bf16[128,1536]{1,0:T(8,128)(2,1)}, bf16[128,1536]{1,0:T(8,128)(2,1)S(1)}, u32[]{:S(2)}, u32[]{:S(2)}) collective-permute-start(bf16[128,1536]{1,0:T(8,128)(2,1)} %get-tuple-element.55), channel_id=1, source_target_pairs={{0,8},{8,0},{1,9},{9,1},{2,10},{10,2},{3,11},{11,3},{4,12},{12,4},... | collective-permute-start | bytes 1179656 | tf_op jit(solution)/shard_map/ppermute | solution.py:26
  100.6 18.9 %collective-permute-start.9 = (bf16[128,1536]{1,0:T(8,128)(2,1)}, bf16[128,1536]{1,0:T(8,128)(2,1)}, u32[]{:S(2)}, u32[]{:S(2)}) collective-permute-start(bf16[128,1536]{1,0:T(8,128)(2,1)} %get-tuple-element.57), channel_id=1, source_target_pairs={{0,8},{8,0},{1,9},{9,1},{2,10},{10,2},{3,11},{11,3},{4,12},{12,4},... | collective-permute-start | bytes 1179656 | tf_op jit(solution)/shard_map/ppermute | solution.py:26
  102.2 17.4 %copy-start.7 = (bf16[1,1,128,3072]{3,2,1,0:T(8,128)(2,1)S(1)}, bf16[1,1,128,3072]{3,2,1,0:T(8,128)(2,1)}, u32[]{:S(2)}) copy-start(bf16[1,1,128,3072]{3,2,1,0:T(8,128)(2,1)} %param.9) | copy-start | bytes 2359300
  102.2 17.4 %copy-start.8 = (f32[128,1536]{1,0:T(8,128)S(1)}, f32[128,1536]{1,0:T(8,128)}, u32[]{:S(2)}) copy-start(f32[128,1536]{1,0:T(8,128)} %get-tuple-element.56) | copy-start | bytes 2359300
  103.2 38.0 %all-to-all-start.2 = ((bf16[4,128,768]{2,1,0:T(8,128)(2,1)}), bf16[4,128,768]{2,1,0:T(8,128)(2,1)S(1)}, u32[]{:S(2)}, u32[]{:S(2)}) async-start(bf16[4,128,768]{2,1,0:T(8,128)(2,1)} %pad_maximum_fusion.1.csum_ref), calls=%async_computation.2 | async-start | bytes 1572864 | tf_op jit(solution)/shard_map/all_to_all | solution.py:332
  111.0 8.5 %copy-start.14 = (bf16[128,1536]{1,0:T(8,128)(2,1)}, bf16[128,1536]{1,0:T(8,128)(2,1)S(1)}, u32[]{:S(2)}) copy-start(bf16[128,1536]{1,0:T(8,128)(2,1)S(1)} %collective-permute-done.8) | copy-start | bytes 1179652
  121.3 19.9 %copy-start.3 = (bf16[128,1536]{1,0:T(8,128)(2,1)}, bf16[128,1536]{1,0:T(8,128)(2,1)S(1)}, u32[]{:S(2)}) copy-start(bf16[128,1536]{1,0:T(8,128)(2,1)S(1)} %get-tuple-element.90) | copy-start | bytes 1179652
  121.3 19.1 %collective-permute-start.10 = (bf16[128,768]{1,0:T(8,128)(2,1)S(1)}, bf16[128,768]{1,0:T(8,128)(2,1)S(1)}, u32[]{:S(2)}, u32[]{:S(2)}) collective-permute-start(bf16[128,768]{1,0:T(8,128)(2,1)S(1)} %get-tuple-element.96), channel_id=1, source_target_pairs={{0,192},{1,193},{2,194},{3,195},{4,196},{5,197},{6,198},{7,199},{8... | collective-permute-start | bytes 589832 | tf_op jit(solution)/shard_map/ppermute | solution.py:21
  122.6 17.8 %collective-permute-start.11 = (bf16[128,768]{1,0:T(8,128)(2,1)S(1)}, bf16[128,768]{1,0:T(8,128)(2,1)S(1)}, u32[]{:S(2)}, u32[]{:S(2)}) collective-permute-start(bf16[128,768]{1,0:T(8,128)(2,1)S(1)} %get-tuple-element.95), channel_id=1, source_target_pairs={{0,128},{1,129},{2,130},{3,131},{4,132},{5,133},{6,134},{7,135},{8... | collective-permute-start | bytes 589832 | tf_op jit(solution)/shard_map/ppermute | solution.py:21
  123.3 17.1 %collective-permute-start.12 = (bf16[128,768]{1,0:T(8,128)(2,1)S(1)}, bf16[128,768]{1,0:T(8,128)(2,1)S(1)}, u32[]{:S(2)}, u32[]{:S(2)}) collective-permute-start(bf16[128,768]{1,0:T(8,128)(2,1)S(1)} %slice.44), channel_id=1, source_target_pairs={{0,64},{1,65},{2,66},{3,67},{4,68},{5,69},{6,70},{7,71},{8,72},{9,... | collective-permute-start | bytes 589832 | tf_op jit(solution)/shard_map/ppermute | solution.py:21
  141.2 5.0 %copy-start.1 = (bf16[128,768]{1,0:T(8,128)(2,1)S(1)}, bf16[128,768]{1,0:T(8,128)(2,1)}, u32[]{:S(2)}) copy-start(bf16[128,768]{1,0:T(8,128)(2,1)} %fusion.3.ctl_ref.refs_0_) | copy-start | bytes 589828
  146.2 10.0 %collective-permute-start.13 = (bf16[128,768]{1,0:T(8,128)(2,1)S(1)}, bf16[128,768]{1,0:T(8,128)(2,1)S(1)}, u32[]{:S(2)}, u32[]{:S(2)}) collective-permute-start(bf16[128,768]{1,0:T(8,128)(2,1)S(1)} %copy-done.1), channel_id=1, source_target_pairs={{0,16},{16,32},{32,48},{48,0},{1,17},{17,33},{33,49},{49,1},{2,18}... | collective-permute-start | bytes 589832 | tf_op jit(solution)/shard_map/ppermute | solution.py:26
  147.8 11.1 %collective-permute-start.14 = (bf16[128,768]{1,0:T(8,128)(2,1)S(1)}, bf16[128,768]{1,0:T(8,128)(2,1)S(1)}, u32[]{:S(2)}, u32[]{:S(2)}) collective-permute-start(bf16[128,768]{1,0:T(8,128)(2,1)S(1)} %copy-done.1), channel_id=1, source_target_pairs={{0,32},{16,48},{32,0},{48,16},{1,33},{17,49},{33,1},{49,17},{2,34}... | collective-permute-start | bytes 589832 | tf_op jit(solution)/shard_map/ppermute | solution.py:26
  150.2 8.7 %collective-permute-start.15 = (bf16[128,768]{1,0:T(8,128)(2,1)S(1)}, bf16[128,768]{1,0:T(8,128)(2,1)S(1)}, u32[]{:S(2)}, u32[]{:S(2)}) collective-permute-start(bf16[128,768]{1,0:T(8,128)(2,1)S(1)} %copy-done.1), channel_id=1, source_target_pairs={{0,48},{16,0},{32,16},{48,32},{1,49},{17,1},{33,17},{49,33},{2,50}... | collective-permute-start | bytes 589832 | tf_op jit(solution)/shard_map/ppermute | solution.py:26
  151.4 19.8 %all-to-all-start.3 = ((bf16[4,128,768]{2,1,0:T(8,128)(2,1)}), bf16[4,128,768]{2,1,0:T(8,128)(2,1)}, u32[]{:S(2)}, u32[]{:S(2)}) async-start(bf16[4,128,768]{2,1,0:T(8,128)(2,1)} %residual.1), calls=%async_computation.3 | async-start | bytes 1572864 | tf_op jit(solution)/shard_map/all_to_all | solution.py:341
  160.9 3.1 %collective-permute-start.16 = (bf16[2,192,768]{2,1,0:T(8,128)(2,1)S(1)}, bf16[2,192,768]{2,1,0:T(8,128)(2,1)S(1)}, u32[]{:S(2)}, u32[]{:S(2)}) collective-permute-start(bf16[2,192,768]{2,1,0:T(8,128)(2,1)S(1)} %dynamic-slice_bitcast_fusion), channel_id=1, source_target_pairs={{0,4},{4,0},{1,5},{5,1},{2,6},{6,2},{3,7},{7,3},{8,12},{12,8},{9,1... | collective-permute-start | bytes 1769480 | tf_op jit(solution)/shard_map/ppermute | solution.py:26
  172.5 42.3 %copy-start.4 = (bf16[128,1536]{1,0:T(8,128)(2,1)S(1)}, bf16[128,1536]{1,0:T(8,128)(2,1)}, u32[]{:S(2)}) copy-start(bf16[128,1536]{1,0:T(8,128)(2,1)} %copy-done.3) | copy-start | bytes 1179652
  172.5 18.7 %all-to-all-start.4 = ((bf16[8,48,768]{2,1,0:T(8,128)(2,1)}), bf16[8,48,768]{2,1,0:T(8,128)(2,1)S(1)}, u32[]{:S(2)}, u32[]{:S(2)}) async-start(bf16[8,48,768]{2,1,0:T(8,128)(2,1)} %bitcast.25), calls=%async_computation.4 | async-start | bytes 1179648 | tf_op jit(solution)/shard_map/all_to_all | solution.py:355
  181.7 33.0 %collective-permute-start.17 = (bf16[128,768]{1,0:T(8,128)(2,1)S(1)}, bf16[128,768]{1,0:T(8,128)(2,1)S(1)}, u32[]{:S(2)}, u32[]{:S(2)}) collective-permute-start(bf16[128,768]{1,0:T(8,128)(2,1)S(1)} %reduce_sum.24), channel_id=1, source_target_pairs={{0,64},{64,128},{128,192},{1,65},{65,129},{129,193},{2,66},{66,130... | collective-permute-start | bytes 589832 | tf_op jit(solution)/shard_map/ppermute | solution.py:21
  183.0 31.7 %collective-permute-start.18 = (bf16[128,768]{1,0:T(8,128)(2,1)S(1)}, bf16[128,768]{1,0:T(8,128)(2,1)S(1)}, u32[]{:S(2)}, u32[]{:S(2)}) collective-permute-start(bf16[128,768]{1,0:T(8,128)(2,1)S(1)} %reduce_sum.24), channel_id=1, source_target_pairs={{0,128},{64,192},{192,64},{1,129},{65,193},{193,65},{2,130},{66,19... | collective-permute-start | bytes 589832 | tf_op jit(solution)/shard_map/ppermute | solution.py:21
  189.2 25.4 %collective-permute-start.19 = (bf16[128,768]{1,0:T(8,128)(2,1)S(1)}, bf16[128,768]{1,0:T(8,128)(2,1)S(1)}, u32[]{:S(2)}, u32[]{:S(2)}) collective-permute-start(bf16[128,768]{1,0:T(8,128)(2,1)S(1)} %reduce_sum.24), channel_id=1, source_target_pairs={{0,192},{128,64},{192,128},{1,193},{129,65},{193,129},{2,194},{130... | collective-permute-start | bytes 589832 | tf_op jit(solution)/shard_map/ppermute | solution.py:21
  191.3 22.7 %collective-permute-start.20 = (bf16[48,768]{1,0:T(8,128)(2,1)S(1)}, bf16[48,768]{1,0:T(8,128)(2,1)S(1)}, u32[]{:S(2)}, u32[]{:S(2)}) collective-permute-start(bf16[48,768]{1,0:T(8,128)(2,1)S(1)} %reduce_sum.25), channel_id=1, source_target_pairs={{0,0},{16,64},{32,128},{48,192},{64,16},{80,80},{96,144},{112,208}... | collective-permute-start | bytes 221192 | tf_op jit(solution)/shard_map/ppermute | solution.py:357
Sparse Core Ops, SparseCore 0:
  13.6 63.3 all-gather.3
  80.1 52.3 all-gather.5

commit v4 on v3

--- a/solution.py
+++ b/solution.py
@@ -33,30 +33,33 @@
         wide_ref[:, :HEAD] = v_ref[...].reshape(length, HEAD)
         wide_ref[:, HEAD:] = jnp.ones((length, HEAD), BF)
 
-    rows = o_ref.shape[0]
-    q = q_ref[...].reshape(rows, HEAD)
     length = wide_ref.shape[0]
     k = k_ref[...].reshape(length, HEAD)
-    s = lax.dot_general(q, k, (((1,), (1,)), ((), ())), preferred_element_type=F32)
-    place = lax.broadcasted_iota(jnp.int32, (rows, text_slots), 1)
-    head = jnp.where(place < tlen_ref[0, 0], s[:, :text_slots], -jnp.inf)
-    tail = s[:, text_slots:]
-    top = jnp.maximum(
-        jnp.max(head, axis=1, keepdims=True), jnp.max(tail, axis=1, keepdims=True)
-    )
     factor = scale * math.log2(math.e)
-    p_head = jnp.exp2((head - top) * factor).astype(BF)
-    p_tail = jnp.exp2((tail - top) * factor).astype(BF)
-    both = jnp.dot(p_head, wide_ref[:text_slots, :], preferred_element_type=F32) + jnp.dot(
-        p_tail, wide_ref[text_slots:, :], preferred_element_type=F32
-    )
-    o_ref[...] = (both[:, :HEAD] / both[:, HEAD:]).astype(BF)
+    blocks, rows, _ = q_ref.shape
+    for at in range(0, blocks, 2):
+        q = q_ref[at : at + 2].reshape(2 * rows, HEAD)
+        s = lax.dot_general(q, k, (((1,), (1,)), ((), ())), preferred_element_type=F32)
+        place = lax.broadcasted_iota(jnp.int32, (2 * rows, text_slots), 1)
+        head = jnp.where(place < tlen_ref[0, 0], s[:, :text_slots], -jnp.inf)
+        tail = s[:, text_slots:]
+        top = jnp.maximum(
+            jnp.max(head, axis=1, keepdims=True), jnp.max(tail, axis=1, keepdims=True)
+        )
+        p_head = jnp.exp2((head - top) * factor).astype(BF)
+        p_tail = jnp.exp2((tail - top) * factor).astype(BF)
+        both = jnp.dot(p_head, wide_ref[:text_slots, :], preferred_element_type=F32) + jnp.dot(
+            p_tail, wide_ref[text_slots:, :], preferred_element_type=F32
+        )
+        result = (both[:, :HEAD] / both[:, HEAD:]).astype(BF)
+        o_ref[at // 4, 0, at % 4 // 2] = result[:rows]
+        o_ref[at // 4, 1, at % 4 // 2] = result[rows:]
 
 
 def attend(qkv, tlen):
     blocks, _, per, _ = qkv.shape
     length = blocks * per
-    q_blocks = 2
+    q_blocks = 8
     rows = q_blocks * per
     whole = lambda part: pl.BlockSpec((blocks, None, per, HEAD), lambda i: (0, part, 0, 0))
     return pl.pallas_call(
@@ -68,10 +71,10 @@
             whole(1),
             whole(2),
         ],
-        out_specs=pl.BlockSpec((rows, HEAD), lambda i: (i, 0)),
-        out_shape=jax.ShapeDtypeStruct((length, HEAD), BF),
+        out_specs=pl.BlockSpec((q_blocks // 4, 2, 2, per, HEAD), lambda i: (i, 0, 0, 0, 0)),
+        out_shape=jax.ShapeDtypeStruct((blocks // 4, 2, 2, per, HEAD), BF),
         scratch_shapes=[pltpu.VMEM((length, 2 * HEAD), BF)],
-        compiler_params=pltpu.CompilerParams(vmem_limit_bytes=40 * MIB),
+        compiler_params=pltpu.CompilerParams(vmem_limit_bytes=56 * MIB),
         cost_estimate=pl.CostEstimate(
             flops=6 * length * length * HEAD,
             bytes_accessed=8 * length * HEAD,
@@ -163,13 +166,6 @@
         copy.wait()
     width = held.shape[-1]
     return held[j].reshape(width, width)
-
-
-def resid_kernel(ctl_ref, zero_ref, o_ref, held, sems):
-    copies = fetch_zero(zero_ref, held, sems)
-    for j in range(4):
-        w = block_of(held, copies, j)
-        o_ref[j] = jnp.dot(ctl_ref[...], w, preferred_element_type=F32).astype(BF)
 
 
 def term_kernel(csum_ref, cot_ref, zero_ref, o_ref, held, sems):
@@ -287,7 +283,11 @@
     zero_slab = lax.dynamic_slice_in_dim(w_zero, rep * slab, slab, axis=0)
     zero_slab = lax.ppermute(zero_slab, ("grp", "x"), turn)
 
-    qkv, zero_slab, cot = gate(qkv, zero_slab, cotangent[0, 0])
+    slab_other = shift(zero_slab, "zl", 1)
+    slabs = jnp.stack(
+        [jnp.where(zl == 0, zero_slab, slab_other), jnp.where(zl == 0, slab_other, zero_slab)]
+    )
+    qkv, slabs, cot = gate(qkv, slabs, cotangent[0, 0])
 
     def cot_block(index):
         return lax.dynamic_slice_in_dim(cot, index * width, width, axis=1)
@@ -295,17 +295,10 @@
     cots = [cot_block(g)] + [
         shift(cot_block((g + step) % n_grp), "grp", step) for step in range(1, n_grp)
     ]
-    slab_other = shift(zero_slab, "zl", 1)
-    attn, zero_slab, slab_other, cots = gate(
-        attend(qkv, text_len), zero_slab, slab_other, cots
-    )
-    slabs = jnp.stack(
-        [jnp.where(zl == 0, zero_slab, slab_other), jnp.where(zl == 0, slab_other, zero_slab)]
-    )
+    attn, slabs, cots = gate(attend(qkv, text_len), slabs, cots)
     zero_rows = lax.all_gather(slabs, ("x", "core", "rep"))
 
-    parts = attn.reshape(n_x, 2, 2, tok, HEAD).transpose(0, 2, 1, 3, 4).reshape(8, 2 * tok, HEAD)
-    heads = lax.all_to_all(parts, ("x", "core"), split_axis=0, concat_axis=0, tiled=True)
+    heads = lax.all_to_all(attn.reshape(8, 2 * tok, HEAD), ("x", "core"), split_axis=0, concat_axis=0, tiled=True)
     csum = sum(jnp.where(source(step) == 0, 0.0, cots[step].astype(F32)) for step in range(n_grp))
     own_cot = sum(jnp.where(source(step) == 0, cots[step], 0) for step in range(n_grp))
     csum = csum.astype(BF)
@@ -334,9 +327,10 @@
     for j in range(1, n_grp):
         control = jnp.where(g == j, parts[j - 1], control)
     zero_rows = zero_rows.reshape(n_x, 2, n_rep, 2, slab, width)
-    control, zero_rows, csum_x = gate(control, zero_rows, csum_x)
-
-    resid = with_zero(resid_kernel, [control], zero_rows, (n_grp, tok, width), "residual")
+    zero_flat = zero_rows.transpose(0, 3, 1, 2, 4, 5).reshape(n_grp, width, width)
+    control, zero_rows, zero_flat, csum_x = gate(control, zero_rows, zero_flat, csum_x)
+
+    resid = jnp.einsum("tr,brc->btc", control, zero_flat, preferred_element_type=F32).astype(BF)
     resid, control = gate(resid, control)
     resid = lax.all_to_all(resid, "grp", split_axis=0, concat_axis=0, tiled=True)
     mine_r = jnp.sum(resid.astype(F32), axis=0).astype(BF)

time: 224 us -> 222 us (level)
  Pallas kernels: 32.6 us -> 24.5 us
  matrix products: 0 us -> 4.66 us
  local copies, waits for them, and re-layouts: 6.98 us -> 11.5 us
  waiting for transfers between devices: 87.7 us -> 83.7 us
    ppermute x6, waiting for transfers between devices: 16.5 us -> 1.93 us  [send(): return lax.ppermute(value, axis, pairs)]
    all_gather x1, waiting for transfers between devices: 0.01 us -> 9.56 us  [shards(): zero_rows = lax.all_gather(slabs, ('x', 'core', 'rep'))]
    transpose x0 -> x1, local copies, waits for them, and re-layouts: none -> 5.04 us  [shards(): zero_rows.transpose(0, 3, 1, 2, 4, 5).reshape(n_grp, width, width)]
    pallas_call x2 -> x1, Pallas kernels: 11 us -> 5.96 us  [with_zero(): pl.pallas_call(kernel, in_specs=[vmem] * len(dense) + [pl.BlockSpec(memor...]
    dot_general x0 -> x1, matrix products: none -> 4.66 us  [shards(): jnp.einsum('tr,brc->btc', control, zero_flat, preferred_element_type=F32)]
    ppermute x13, waiting for transfers between devices: 27.3 us -> 31.4 us  [shift(): return lax.ppermute(value, axis, [(i, (i + step) % n) for i in range(n)])]
    all_to_all x1, waiting for transfers between devices: 4.92 us -> 1.5 us  [shards(): lax.all_to_all(attn.reshape(8, 2 * tok, HEAD), ('x', 'core'), split_axis=...]
    pallas_call x1, Pallas kernels: 11.5 us -> 8.42 us  [attend(): pl.pallas_call(functools.partial(attend_kernel, text_slots=length // 8, s...]
  transfers between devices with their start and end apart: 28 -> 28, of which waited for: 11 -> 14; matrix products, arithmetic and copies ran while one was open for 4% -> 6% of each run, Pallas kernels for 12% -> 11%
where the time goes in v4:
time: 222 us; the launch traced here: 221 us
  waiting for transfers between devices  83.7 us (38%)
  starting transfers between devices  69.4 us (31%)
  Pallas kernels  24.5 us (11%)
  between operations  15.8 us (7%)
  other arithmetic  11.6 us (5%)
  local copies, waits for them, and re-layouts  11.5 us (5%)
  matrix products  4.66 us (2%)
    ppermute x13, waiting for transfers between devices, shift(): return lax.ppermute(value, axis, [(i, (i + step) % n) for i in range(n)])  31.4 us
    ppermute x13, starting transfers between devices, shift(): return lax.ppermute(value, axis, [(i, (i + step) % n) for i in range(n)])  20.6 us
    ppermute x1, waiting for transfers between devices, shards(): zero_slab = lax.ppermute(zero_slab, ('grp', 'x'), turn)  18.9 us
    ppermute x1, waiting for transfers between devices, shards(): grad_zero = lax.ppermute(grad, ('grp', 'x'), turn).astype(F32)  18.3 us
    ppermute x6, starting transfers between devices, send(): return lax.ppermute(value, axis, pairs)  10.9 us
    all_to_all x1, starting transfers between devices, shards(): lax.all_to_all(halves, ('zl', 'rep'), split_axis=0, concat_axis=0, tiled=...  10.9 us
    all_gather x1, waiting for transfers between devices, shards(): zero_rows = lax.all_gather(slabs, ('x', 'core', 'rep'))  9.56 us
    pallas_call x1, Pallas kernels, attend(): pl.pallas_call(functools.partial(attend_kernel, text_slots=length // 8, s...  8.42 us
  transfers between devices with their start and end apart: 28, of which 14 were waited for; matrix products, arithmetic and copies ran while one was open for 6% of the time, Pallas kernels for 11%

profile of v4, /device:TPU:193, one launch (start us, length us, event | category | flops | bytes accessed | tf_op | source)
XLA Modules:
  0.0 221.1 jit_solution(3200539172350775736)
XLA Ops:
  7.2 2.6 %copy.18 = bf16[1,1,128,2,2048]{2,4,3,1,0:T(8,128)(2,1)S(1)} copy(bf16[1,1,128,2,2048]{4,3,2,1,0:T(2,128)(2,1)} %param.10) | data formatting | bytes 2097152 | tf_op args[1]
  9.8 0.7 copy.19
  10.5 0.4 copy-done.12
  10.9 0.3 copy.20
  11.1 0.3 copy.21
  11.4 1.3 pad_maximum_fusion
  12.8 0.7 slice_select_fusion.1
  13.5 5.6 %all-to-all-start = ((bf16[16,3,128,128]{3,2,1,0:T(8,128)(2,1)}), bf16[16,3,128,128]{3,2,1,0:T(8,128)(2,1)S(1)}, u32[]{:S(2)}, u32[]{:S(2)}) async-start(bf16[16,3,128,128]{3,2,1,0:T(8,128)(2,1)} %pad_maximum_fusion), calls=%async_computation | async-start | bytes 3145728 | tf_op jit(solution)/shard_map/all_to_all | solution.py:280
  19.2 2.7 %collective-permute-start = (bf16[48,768]{1,0:T(8,128)(2,1)S(1)}, bf16[48,768]{1,0:T(8,128)(2,1)S(1)}, u32[]{:S(2)}, u32[]{:S(2)}) collective-permute-start(bf16[48,768]{1,0:T(8,128)(2,1)S(1)} %constant_dynamic-slice_fusion.4), channel_id=1, source_target_pairs={{0,0},{16,64},{32,128},{48,192},{64,16},{80,80},{96,144},{112,208}... | collective-permute-start | bytes 221192 | tf_op jit(solution)/shard_map/ppermute | solution.py:284
  21.9 18.9 %collective-permute-done = bf16[48,768]{1,0:T(8,128)(2,1)S(1)} collective-permute-done((bf16[48,768]{1,0:T(8,128)(2,1)S(1)}, bf16[48,768]{1,0:T(8,128)(2,1)S(1)}, u32[]{:S(2)}, u32[]{:S(2)}) %collective-permute-start) | collective-permute-done | bytes 73760 | tf_op jit(solution)/shard_map/ppermute | solution.py:284
  40.8 0.3 collective-permute-start.1
  41.8 2.6 %collective-permute-done.1 = bf16[48,768]{1,0:T(8,128)(2,1)S(1)} collective-permute-done((bf16[48,768]{1,0:T(8,128)(2,1)S(1)}, bf16[48,768]{1,0:T(8,128)(2,1)S(1)}, u32[]{:S(2)}, u32[]{:S(2)}) %collective-permute-start.1) | collective-permute-done | bytes 73760 | tf_op jit(solution)/shard_map/ppermute | solution.py:26
  44.4 0.7 pad_maximum_fusion.2
  45.3 6.0 %collective-permute-start.3 = (bf16[128,768]{1,0:T(8,128)(2,1)S(1)}, bf16[128,768]{1,0:T(8,128)(2,1)S(1)}, u32[]{:S(2)}, u32[]{:S(2)}) collective-permute-start(bf16[128,768]{1,0:T(8,128)(2,1)S(1)} %get-tuple-element.92), channel_id=1, source_target_pairs={{0,128},{64,192},{128,0},{192,64},{1,129},{65,193},{129,1},{193,65... | collective-permute-start | bytes 589832 | tf_op jit(solution)/shard_map/ppermute | solution.py:26
  51.3 8.4 %attend.1 = bf16[4,2,2,128,128]{4,3,2,1,0:T(8,128)(2,1)} custom-call(s32[1,1]{1,0:T(1,128)S(6)} %copy.32.tlen_ref, bf16[16,3,128,128]{3,2,1,0:T(8,128)(2,1)} %copy-done.5, bf16[16,3,128,128]{3,2,1,0:T(8,128)(2,1)} %copy-done.5, bf16[16,3,128,128]{3,2,1,0:T(8,128)(2,1)} %copy-done.5), custom_call_target="tpu_custom_call" | custom-call | flops 3221225472 | bytes 2097152 | tf_op jit(solution)/shard_map/attend/pallas_call | solution.py:65
  59.7 3.0 %collective-permute-done.3 = bf16[128,768]{1,0:T(8,128)(2,1)S(1)} collective-permute-done((bf16[128,768]{1,0:T(8,128)(2,1)S(1)}, bf16[128,768]{1,0:T(8,128)(2,1)S(1)}, u32[]{:S(2)}, u32[]{:S(2)}) %collective-permute-start.3) | collective-permute-done | bytes 196640 | tf_op jit(solution)/shard_map/ppermute | solution.py:26
  62.7 6.5 %collective-permute-done.4 = bf16[128,768]{1,0:T(8,128)(2,1)S(1)} collective-permute-done((bf16[128,768]{1,0:T(8,128)(2,1)S(1)}, bf16[128,768]{1,0:T(8,128)(2,1)S(1)}, u32[]{:S(2)}, u32[]{:S(2)}) %collective-permute-start.4) | collective-permute-done | bytes 196640 | tf_op jit(solution)/shard_map/ppermute | solution.py:26
  69.3 6.0 %all-to-all-start.1 = ((bf16[8,256,128]{2,1,0:T(8,128)(2,1)}), bf16[8,256,128]{2,1,0:T(8,128)(2,1)S(1)}, u32[]{:S(2)}, u32[]{:S(2)}) async-start(bf16[8,256,128]{2,1,0:T(8,128)(2,1)} %bitcast.69), calls=%async_computation.1 | async-start | bytes 1048576 | tf_op jit(solution)/shard_map/all_to_all | solution.py:301
  75.3 0.2 add_convert_fusion.3
  75.4 2.2 %collective-permute-start.5 = (bf16[128,768]{1,0:T(8,128)(2,1)S(1)}, bf16[128,768]{1,0:T(8,128)(2,1)S(1)}, u32[]{:S(2)}, u32[]{:S(2)}) collective-permute-start(bf16[128,768]{1,0:T(8,128)(2,1)S(1)} %add_convert_fusion.3), channel_id=1, source_target_pairs={{0,64},{64,128},{128,192},{192,0},{1,65},{65,129},{129,193},{193,1... | collective-permute-start | bytes 589832 | tf_op jit(solution)/shard_map/ppermute | solution.py:26
  77.7 2.4 %collective-permute-start.6 = (bf16[128,768]{1,0:T(8,128)(2,1)S(1)}, bf16[128,768]{1,0:T(8,128)(2,1)S(1)}, u32[]{:S(2)}, u32[]{:S(2)}) collective-permute-start(bf16[128,768]{1,0:T(8,128)(2,1)S(1)} %add_convert_fusion.3), channel_id=1, source_target_pairs={{0,128},{64,192},{128,0},{192,64},{1,129},{65,193},{129,1},{193,65... | collective-permute-start | bytes 589832 | tf_op jit(solution)/shard_map/ppermute | solution.py:26
  80.1 1.6 collective-permute-start.7
  82.3 0.9 dynamic-slice_reduce_fusion.1
  83.3 1.5 all-to-all-done.1.a_ref
  84.8 0.8 copy-done.1
  85.6 4.1 %project.2 = (f32[128,1536]{1,0:T(8,128)}, bf16[128,1536]{1,0:T(8,128)(2,1)}) custom-call(s32[1]{0:T(128)} %bitcast.2.zl_ref, bf16[8,256,128]{2,1,0:T(8,128)(2,1)} %copy-done.1, bf16[8,4,128,768]{3,2,1,0:T(8,128)(2,1)} %bitcast.57), custom_call_target="tpu_custom_call" | custom-call | flops 805306368 | bytes 3145728 | tf_op jit(solution)/shard_map/project/pallas_call | solution.py:120
  89.7 4.1 %project.3 = (f32[128,1536]{1,0:T(8,128)}, bf16[128,1536]{1,0:T(8,128)(2,1)}) custom-call(s32[1]{0:T(128)} %bitcast.2.zl_ref, bf16[8,256,128]{2,1,0:T(8,128)(2,1)} %copy-done.1, bf16[8,4,128,768]{3,2,1,0:T(8,128)(2,1)} %bitcast.58), custom_call_target="tpu_custom_call" | custom-call | flops 805306368 | bytes 3145728 | tf_op jit(solution)/shard_map/project/pallas_call | solution.py:120
  93.8 4.5 %collective-permute-done.7 = bf16[128,768]{1,0:T(8,128)(2,1)S(1)} collective-permute-done((bf16[128,768]{1,0:T(8,128)(2,1)S(1)}, bf16[128,768]{1,0:T(8,128)(2,1)S(1)}, u32[]{:S(2)}, u32[]{:S(2)}) %collective-permute-start.7) | collective-permute-done | bytes 196640 | tf_op jit(solution)/shard_map/ppermute | solution.py:26
  98.3 1.5 collective-permute-start.9
  99.9 1.0 pad_maximum_fusion.1.csum_ref
  100.9 4.2 %all-to-all-start.2 = ((bf16[4,128,768]{2,1,0:T(8,128)(2,1)}), bf16[4,128,768]{2,1,0:T(8,128)(2,1)S(1)}, u32[]{:S(2)}, u32[]{:S(2)}) async-start(bf16[4,128,768]{2,1,0:T(8,128)(2,1)} %pad_maximum_fusion.1.csum_ref), calls=%async_computation.2 | async-start | bytes 1572864 | tf_op jit(solution)/shard_map/all_to_all | solution.py:325
  105.1 3.6 %collective-permute-done.8 = bf16[128,1536]{1,0:T(8,128)(2,1)S(1)} collective-permute-done((bf16[128,1536]{1,0:T(8,128)(2,1)}, bf16[128,1536]{1,0:T(8,128)(2,1)S(1)}, u32[]{:S(2)}, u32[]{:S(2)}) %collective-permute-start.8) | collective-permute-done | bytes 393248 | tf_op jit(solution)/shard_map/ppermute | solution.py:26
  108.7 8.5 %collective-permute-done.9 = bf16[128,1536]{1,0:T(8,128)(2,1)} collective-permute-done((bf16[128,1536]{1,0:T(8,128)(2,1)}, bf16[128,1536]{1,0:T(8,128)(2,1)}, u32[]{:S(2)}, u32[]{:S(2)}) %collective-permute-start.9) | collective-permute-done | bytes 393248 | tf_op jit(solution)/shard_map/ppermute | solution.py:26
  117.2 1.7 add_convert_fusion.2
  119.0 1.3 collective-permute-start.10
  120.3 0.7 collective-permute-start.11
  121.0 0.7 collective-permute-start.12
  121.7 9.6 %all-gather.6.cloned.1.call-done = bf16[64,48,768]{2,1,0:T(8,128)(2,1)} async-done(((bf16[2,48,768]{2,1,0:T(8,128)(2,1)}), bf16[64,48,768]{2,1,0:T(8,128)(2,1)}) %all-gather.6.cloned.1.call-update) | async-done | bytes 4718608 | tf_op jit(solution)/shard_map/all_gather | solution.py:299
  131.2 5.0 %copy.22 = bf16[4,2,2,4,48,768]{5,4,3,2,1,0:T(8,128)(2,1)} copy(bf16[4,2,2,4,48,768]{5,4,1,3,2,0:T(8,128)(2,1)} %bitcast.59) | data formatting | bytes 9437184 | tf_op jit(solution)/shard_map/transpose | solution.py:330
  136.2 1.9 collective-permute-done.10
  138.2 4.7 %fusion = bf16[4,128,768]{1,2,0:T(8,128)(2,1)} fusion(bf16[4,768,768]{2,1,0:T(8,128)(2,1)} %bitcast.56, bf16[128,768]{1,0:T(8,128)(2,1)S(1)} %fusion.4.refs_0_), kind=kOutput, calls=%fused_computation.3 | convolution fusion | flops 604372992 | bytes 5701632 | tf_op jit(solution)/shard_map/tr,brc->btc/dot_general | solution.py:333
  142.9 1.4 collective-permute-start.13
  144.3 2.4 %collective-permute-start.14 = (bf16[128,768]{1,0:T(8,128)(2,1)S(1)}, bf16[128,768]{1,0:T(8,128)(2,1)S(1)}, u32[]{:S(2)}, u32[]{:S(2)}) collective-permute-start(bf16[128,768]{1,0:T(8,128)(2,1)S(1)} %fusion.4.refs_0_), channel_id=1, source_target_pairs={{0,32},{16,48},{32,0},{48,16},{1,33},{17,49},{33,1},{49,17},{2,34}... | collective-permute-start | bytes 589832 | tf_op jit(solution)/shard_map/ppermute | solution.py:26
  146.7 1.2 collective-permute-start.15
  147.9 4.8 %all-to-all-start.3 = ((bf16[4,128,768]{1,2,0:T(8,128)(2,1)}), bf16[4,128,768]{1,2,0:T(8,128)(2,1)}, u32[]{:S(2)}, u32[]{:S(2)}) async-start(bf16[4,128,768]{1,2,0:T(8,128)(2,1)} %fusion), calls=%async_computation.3 | async-start | bytes 1572864 | tf_op jit(solution)/shard_map/all_to_all | solution.py:335
  152.7 2.7 %collective-permute-done.14.refs_2_ = bf16[128,768]{1,0:T(8,128)(2,1)S(1)} collective-permute-done((bf16[128,768]{1,0:T(8,128)(2,1)S(1)}, bf16[128,768]{1,0:T(8,128)(2,1)S(1)}, u32[]{:S(2)}, u32[]{:S(2)}) %collective-permute-start.14) | collective-permute-done | bytes 196640 | tf_op jit(solution)/shard_map/ppermute | solution.py:26
  155.4 1.9 grad_partial.1
  157.4 1.5 collective-permute-start.16
  158.9 1.7 select_add_fusion.cot_ref
  160.5 0.9 fusion.2
  161.5 6.0 %control_gradient.1 = bf16[128,768]{1,0:T(8,128)(2,1)} custom-call(bf16[4,128,768]{2,1,0:T(8,128)(2,1)} %pad_maximum_fusion.1.csum_ref, bf16[128,768]{1,0:T(8,128)(2,1)} %select_add_fusion.cot_ref, bf16[4,2,4,2,48,768]{5,4,3,2,1,0:T(8,128)(2,1)} %bitcast.60), custom_call_target="tpu_custom_call" | custom-call | flops 603979776 | bytes 4718592 | tf_op jit(solution)/shard_map/control_gradient/pallas_call | solution.py:190
  167.4 0.3 all-to-all-done.3
  167.8 1.3 reduce_sum.24
  169.1 10.9 %all-to-all-start.4 = ((bf16[8,48,768]{2,1,0:T(8,128)(2,1)}), bf16[8,48,768]{2,1,0:T(8,128)(2,1)S(1)}, u32[]{:S(2)}, u32[]{:S(2)}) async-start(bf16[8,48,768]{2,1,0:T(8,128)(2,1)} %bitcast.27), calls=%async_computation.4 | async-start | bytes 1179648 | tf_op jit(solution)/shard_map/all_to_all | solution.py:349
  179.9 0.1 copy.24
  180.1 1.3 collective-permute-start.17
  181.4 5.1 %collective-permute-start.18 = (bf16[128,768]{1,0:T(8,128)(2,1)S(1)}, bf16[128,768]{1,0:T(8,128)(2,1)S(1)}, u32[]{:S(2)}, u32[]{:S(2)}) collective-permute-start(bf16[128,768]{1,0:T(8,128)(2,1)S(1)} %copy.24), channel_id=1, source_target_pairs={{0,128},{64,192},{192,64},{1,129},{65,193},{193,65},{2,130},{66,19... | collective-permute-start | bytes 589832 | tf_op jit(solution)/shard_map/ppermute | solution.py:21
  186.5 1.9 collective-permute-start.19
  188.4 1.7 all-to-all-done.4
  190.2 3.7 %collective-permute-start.20 = (bf16[48,768]{1,0:T(8,128)(2,1)S(1)}, bf16[48,768]{1,0:T(8,128)(2,1)S(1)}, u32[]{:S(2)}, u32[]{:S(2)}) collective-permute-start(bf16[48,768]{1,0:T(8,128)(2,1)S(1)} %reduce_sum.25), channel_id=1, source_target_pairs={{0,0},{16,64},{32,128},{48,192},{64,16},{80,80},{96,144},{112,208}... | collective-permute-start | bytes 221192 | tf_op jit(solution)/shard_map/ppermute | solution.py:351
  193.9 18.3 %collective-permute-done.20 = bf16[48,768]{1,0:T(8,128)(2,1)S(1)} collective-permute-done((bf16[48,768]{1,0:T(8,128)(2,1)S(1)}, bf16[48,768]{1,0:T(8,128)(2,1)S(1)}, u32[]{:S(2)}, u32[]{:S(2)}) %collective-permute-start.20) | collective-permute-done | bytes 73760 | tf_op jit(solution)/shard_map/ppermute | solution.py:351
  212.1 0.7 convert_element_type.111
  212.8 0.1 copy.27
  213.1 1.1 fusion.1
  (59 shorter events, 0.8 us)
Async XLA Ops:
  7.2 12.0 %copy-start = (bf16[192,768]{1,0:T(8,128)(2,1)S(1)}, bf16[192,768]{1,0:T(8,128)(2,1)}, u32[]{:S(2)}) copy-start(bf16[192,768]{1,0:T(8,128)(2,1)} %param.16) | copy-start | bytes 884740
  7.2 77.6 %all-gather.4.cloned.1.call-start = ((), (), s32[]{:S(2)}) async-start(), calls=%async_computation.5 | async-start | bytes 6488064 | tf_op jit(solution)/shard_map/all_gather | solution.py:278
  9.8 1.0 copy-start.12
  11.4 1.4 copy-start.13
  13.5 31.6 %copy-start.6 = (bf16[1,1,128,3072]{3,2,1,0:T(8,128)(2,1)S(1)}, bf16[1,1,128,3072]{3,2,1,0:T(8,128)(2,1)}, u32[]{:S(2)}) copy-start(bf16[1,1,128,3072]{3,2,1,0:T(8,128)(2,1)} %param.17) | copy-start | bytes 2359300
  13.5 31.6 %all-to-all-start = ((bf16[16,3,128,128]{3,2,1,0:T(8,128)(2,1)}), bf16[16,3,128,128]{3,2,1,0:T(8,128)(2,1)S(1)}, u32[]{:S(2)}, u32[]{:S(2)}) async-start(bf16[16,3,128,128]{3,2,1,0:T(8,128)(2,1)} %pad_maximum_fusion), calls=%async_computation | async-start | bytes 3145728 | tf_op jit(solution)/shard_map/all_to_all | solution.py:280
  19.1 112.1 %all-gather.6.cloned.1.call-start = ((), (), s32[]{:S(2)}) async-start(), calls=%async_computation.6 | async-start | bytes 4866048 | tf_op jit(solution)/shard_map/all_gather | solution.py:299
  19.2 21.6 %collective-permute-start = (bf16[48,768]{1,0:T(8,128)(2,1)S(1)}, bf16[48,768]{1,0:T(8,128)(2,1)S(1)}, u32[]{:S(2)}, u32[]{:S(2)}) collective-permute-start(bf16[48,768]{1,0:T(8,128)(2,1)S(1)} %constant_dynamic-slice_fusion.4), channel_id=1, source_target_pairs={{0,0},{16,64},{32,128},{48,192},{64,16},{80,80},{96,144},{112,208}... | collective-permute-start | bytes 221192 | tf_op jit(solution)/shard_map/ppermute | solution.py:284
  40.8 3.6 %collective-permute-start.1 = (bf16[48,768]{1,0:T(8,128)(2,1)S(1)}, bf16[48,768]{1,0:T(8,128)(2,1)S(1)}, u32[]{:S(2)}, u32[]{:S(2)}) collective-permute-start(bf16[48,768]{1,0:T(8,128)(2,1)S(1)} %collective-permute-done), channel_id=1, source_target_pairs={{0,8},{8,0},{1,9},{9,1},{2,10},{10,2},{3,11},{11,3},{4,12},{12,4},... | collective-permute-start | bytes 221192 | tf_op jit(solution)/shard_map/ppermute | solution.py:26
  45.1 6.2 %copy-start.5 = (bf16[16,3,128,128]{3,2,1,0:T(8,128)(2,1)}, bf16[16,3,128,128]{3,2,1,0:T(8,128)(2,1)S(1)}, u32[]{:S(2)}) copy-start(bf16[16,3,128,128]{3,2,1,0:T(8,128)(2,1)S(1)} %all-to-all-done.q_ref.k_ref.v_ref) | copy-start | bytes 4718596
  45.2 30.1 %copy-start.4 = (bf16[128,768]{1,0:T(8,128)(2,1)}, bf16[128,768]{1,0:T(8,128)(2,1)S(1)}, u32[]{:S(2)}) copy-start(bf16[128,768]{1,0:T(8,128)(2,1)S(1)} %get-tuple-element.51) | copy-start | bytes 589828
  45.2 14.5 %collective-permute-start.2 = (bf16[128,768]{1,0:T(8,128)(2,1)S(1)}, bf16[128,768]{1,0:T(8,128)(2,1)S(1)}, u32[]{:S(2)}, u32[]{:S(2)}) collective-permute-start(bf16[128,768]{1,0:T(8,128)(2,1)S(1)} %get-tuple-element.93), channel_id=1, source_target_pairs={{0,64},{64,128},{128,192},{192,0},{1,65},{65,129},{129,193},{193,1... | collective-permute-start | bytes 589832 | tf_op jit(solution)/shard_map/ppermute | solution.py:26
  45.3 17.4 %collective-permute-start.3 = (bf16[128,768]{1,0:T(8,128)(2,1)S(1)}, bf16[128,768]{1,0:T(8,128)(2,1)S(1)}, u32[]{:S(2)}, u32[]{:S(2)}) collective-permute-start(bf16[128,768]{1,0:T(8,128)(2,1)S(1)} %get-tuple-element.92), channel_id=1, source_target_pairs={{0,128},{64,192},{128,0},{192,64},{1,129},{65,193},{129,1},{193,65... | collective-permute-start | bytes 589832 | tf_op jit(solution)/shard_map/ppermute | solution.py:26
  51.3 18.0 %collective-permute-start.4 = (bf16[128,768]{1,0:T(8,128)(2,1)S(1)}, bf16[128,768]{1,0:T(8,128)(2,1)S(1)}, u32[]{:S(2)}, u32[]{:S(2)}) collective-permute-start(bf16[128,768]{1,0:T(8,128)(2,1)S(1)} %get-tuple-element.91), channel_id=1, source_target_pairs={{0,192},{64,0},{128,64},{192,128},{1,193},{65,1},{129,65},{193,129... | collective-permute-start | bytes 589832 | tf_op jit(solution)/shard_map/ppermute | solution.py:26
  59.7 30.0 %copy-start.9 = (bf16[128,768]{1,0:T(8,128)(2,1)}, bf16[128,768]{1,0:T(8,128)(2,1)S(1)}, u32[]{:S(2)}) copy-start(bf16[128,768]{1,0:T(8,128)(2,1)S(1)} %collective-permute-done.2) | copy-start | bytes 589828
  62.7 27.0 %copy-start.10 = (bf16[128,768]{1,0:T(8,128)(2,1)}, bf16[128,768]{1,0:T(8,128)(2,1)S(1)}, u32[]{:S(2)}) copy-start(bf16[128,768]{1,0:T(8,128)(2,1)S(1)} %collective-permute-done.3) | copy-start | bytes 589828
  69.2 20.5 %copy-start.11 = (bf16[128,768]{1,0:T(8,128)(2,1)}, bf16[128,768]{1,0:T(8,128)(2,1)S(1)}, u32[]{:S(2)}) copy-start(bf16[128,768]{1,0:T(8,128)(2,1)S(1)} %collective-permute-done.4) | copy-start | bytes 589828
  69.3 15.5 %all-to-all-start.1 = ((bf16[8,256,128]{2,1,0:T(8,128)(2,1)}), bf16[8,256,128]{2,1,0:T(8,128)(2,1)S(1)}, u32[]{:S(2)}, u32[]{:S(2)}) async-start(bf16[8,256,128]{2,1,0:T(8,128)(2,1)} %bitcast.69), calls=%async_computation.1 | async-start | bytes 1048576 | tf_op jit(solution)/shard_map/all_to_all | solution.py:301
  75.4 18.4 %collective-permute-start.5 = (bf16[128,768]{1,0:T(8,128)(2,1)S(1)}, bf16[128,768]{1,0:T(8,128)(2,1)S(1)}, u32[]{:S(2)}, u32[]{:S(2)}) collective-permute-start(bf16[128,768]{1,0:T(8,128)(2,1)S(1)} %add_convert_fusion.3), channel_id=1, source_target_pairs={{0,64},{64,128},{128,192},{192,0},{1,65},{65,129},{129,193},{193,1... | collective-permute-start | bytes 589832 | tf_op jit(solution)/shard_map/ppermute | solution.py:26
  77.7 16.1 %collective-permute-start.6 = (bf16[128,768]{1,0:T(8,128)(2,1)S(1)}, bf16[128,768]{1,0:T(8,128)(2,1)S(1)}, u32[]{:S(2)}, u32[]{:S(2)}) collective-permute-start(bf16[128,768]{1,0:T(8,128)(2,1)S(1)} %add_convert_fusion.3), channel_id=1, source_target_pairs={{0,128},{64,192},{128,0},{192,64},{1,129},{65,193},{129,1},{193,65... | collective-permute-start | bytes 589832 | tf_op jit(solution)/shard_map/ppermute | solution.py:26
  80.1 18.2 %collective-permute-start.7 = (bf16[128,768]{1,0:T(8,128)(2,1)S(1)}, bf16[128,768]{1,0:T(8,128)(2,1)S(1)}, u32[]{:S(2)}, u32[]{:S(2)}) collective-permute-start(bf16[128,768]{1,0:T(8,128)(2,1)S(1)} %add_convert_fusion.3), channel_id=1, source_target_pairs={{0,192},{64,0},{128,64},{192,128},{1,193},{65,1},{129,65},{193,129... | collective-permute-start | bytes 589832 | tf_op jit(solution)/shard_map/ppermute | solution.py:26
  84.8 0.8 copy-start.1
  98.3 10.4 %collective-permute-start.8 = (bf16[128,1536]{1,0:T(8,128)(2,1)}, bf16[128,1536]{1,0:T(8,128)(2,1)S(1)}, u32[]{:S(2)}, u32[]{:S(2)}) collective-permute-start(bf16[128,1536]{1,0:T(8,128)(2,1)} %get-tuple-element.55), channel_id=1, source_target_pairs={{0,8},{8,0},{1,9},{9,1},{2,10},{10,2},{3,11},{11,3},{4,12},{12,4},... | collective-permute-start | bytes 1179656 | tf_op jit(solution)/shard_map/ppermute | solution.py:26
  98.3 18.9 %collective-permute-start.9 = (bf16[128,1536]{1,0:T(8,128)(2,1)}, bf16[128,1536]{1,0:T(8,128)(2,1)}, u32[]{:S(2)}, u32[]{:S(2)}) collective-permute-start(bf16[128,1536]{1,0:T(8,128)(2,1)} %get-tuple-element.57), channel_id=1, source_target_pairs={{0,8},{8,0},{1,9},{9,1},{2,10},{10,2},{3,11},{11,3},{4,12},{12,4},... | collective-permute-start | bytes 1179656 | tf_op jit(solution)/shard_map/ppermute | solution.py:26
  99.9 17.4 %copy-start.7 = (bf16[1,1,128,3072]{3,2,1,0:T(8,128)(2,1)S(1)}, bf16[1,1,128,3072]{3,2,1,0:T(8,128)(2,1)}, u32[]{:S(2)}) copy-start(bf16[1,1,128,3072]{3,2,1,0:T(8,128)(2,1)} %param.9) | copy-start | bytes 2359300
  99.9 17.4 %copy-start.8 = (f32[128,1536]{1,0:T(8,128)S(1)}, f32[128,1536]{1,0:T(8,128)}, u32[]{:S(2)}) copy-start(f32[128,1536]{1,0:T(8,128)} %get-tuple-element.56) | copy-start | bytes 2359300
  100.9 37.3 %all-to-all-start.2 = ((bf16[4,128,768]{2,1,0:T(8,128)(2,1)}), bf16[4,128,768]{2,1,0:T(8,128)(2,1)S(1)}, u32[]{:S(2)}, u32[]{:S(2)}) async-start(bf16[4,128,768]{2,1,0:T(8,128)(2,1)} %pad_maximum_fusion.1.csum_ref), calls=%async_computation.2 | async-start | bytes 1572864 | tf_op jit(solution)/shard_map/all_to_all | solution.py:325
  108.7 8.5 %copy-start.14 = (bf16[128,1536]{1,0:T(8,128)(2,1)}, bf16[128,1536]{1,0:T(8,128)(2,1)S(1)}, u32[]{:S(2)}) copy-start(bf16[128,1536]{1,0:T(8,128)(2,1)S(1)} %collective-permute-done.8) | copy-start | bytes 1179652
  118.9 17.3 %copy-start.2 = (bf16[128,1536]{1,0:T(8,128)(2,1)}, bf16[128,1536]{1,0:T(8,128)(2,1)S(1)}, u32[]{:S(2)}) copy-start(bf16[128,1536]{1,0:T(8,128)(2,1)S(1)} %get-tuple-element.90) | copy-start | bytes 1179652
  119.0 19.2 %collective-permute-start.10 = (bf16[128,768]{1,0:T(8,128)(2,1)S(1)}, bf16[128,768]{1,0:T(8,128)(2,1)S(1)}, u32[]{:S(2)}, u32[]{:S(2)}) collective-permute-start(bf16[128,768]{1,0:T(8,128)(2,1)S(1)} %get-tuple-element.96), channel_id=1, source_target_pairs={{0,192},{1,193},{2,194},{3,195},{4,196},{5,197},{6,198},{7,199},{8... | collective-permute-start | bytes 589832 | tf_op jit(solution)/shard_map/ppermute | solution.py:21
  120.3 17.9 %collective-permute-start.11 = (bf16[128,768]{1,0:T(8,128)(2,1)S(1)}, bf16[128,768]{1,0:T(8,128)(2,1)S(1)}, u32[]{:S(2)}, u32[]{:S(2)}) collective-permute-start(bf16[128,768]{1,0:T(8,128)(2,1)S(1)} %get-tuple-element.95), channel_id=1, source_target_pairs={{0,128},{1,129},{2,130},{3,131},{4,132},{5,133},{6,134},{7,135},{8... | collective-permute-start | bytes 589832 | tf_op jit(solution)/shard_map/ppermute | solution.py:21
  121.0 17.2 %collective-permute-start.12 = (bf16[128,768]{1,0:T(8,128)(2,1)S(1)}, bf16[128,768]{1,0:T(8,128)(2,1)S(1)}, u32[]{:S(2)}, u32[]{:S(2)}) collective-permute-start(bf16[128,768]{1,0:T(8,128)(2,1)S(1)} %slice.44), channel_id=1, source_target_pairs={{0,64},{1,65},{2,66},{3,67},{4,68},{5,69},{6,70},{7,71},{8,72},{9,... | collective-permute-start | bytes 589832 | tf_op jit(solution)/shard_map/ppermute | solution.py:21
  142.9 9.8 %collective-permute-start.13 = (bf16[128,768]{1,0:T(8,128)(2,1)S(1)}, bf16[128,768]{1,0:T(8,128)(2,1)S(1)}, u32[]{:S(2)}, u32[]{:S(2)}) collective-permute-start(bf16[128,768]{1,0:T(8,128)(2,1)S(1)} %fusion.4.refs_0_), channel_id=1, source_target_pairs={{0,16},{16,32},{32,48},{48,0},{1,17},{17,33},{33,49},{49,1},{2,18}... | collective-permute-start | bytes 589832 | tf_op jit(solution)/shard_map/ppermute | solution.py:26
  144.3 11.1 %collective-permute-start.14 = (bf16[128,768]{1,0:T(8,128)(2,1)S(1)}, bf16[128,768]{1,0:T(8,128)(2,1)S(1)}, u32[]{:S(2)}, u32[]{:S(2)}) collective-permute-start(bf16[128,768]{1,0:T(8,128)(2,1)S(1)} %fusion.4.refs_0_), channel_id=1, source_target_pairs={{0,32},{16,48},{32,0},{48,16},{1,33},{17,49},{33,1},{49,17},{2,34}... | collective-permute-start | bytes 589832 | tf_op jit(solution)/shard_map/ppermute | solution.py:26
  146.7 8.7 %collective-permute-start.15 = (bf16[128,768]{1,0:T(8,128)(2,1)S(1)}, bf16[128,768]{1,0:T(8,128)(2,1)S(1)}, u32[]{:S(2)}, u32[]{:S(2)}) collective-permute-start(bf16[128,768]{1,0:T(8,128)(2,1)S(1)} %fusion.4.refs_0_), channel_id=1, source_target_pairs={{0,48},{16,0},{32,16},{48,32},{1,49},{17,1},{33,17},{49,33},{2,50}... | collective-permute-start | bytes 589832 | tf_op jit(solution)/shard_map/ppermute | solution.py:26
  147.9 19.9 %all-to-all-start.3 = ((bf16[4,128,768]{1,2,0:T(8,128)(2,1)}), bf16[4,128,768]{1,2,0:T(8,128)(2,1)}, u32[]{:S(2)}, u32[]{:S(2)}) async-start(bf16[4,128,768]{1,2,0:T(8,128)(2,1)} %fusion), calls=%async_computation.3 | async-start | bytes 1572864 | tf_op jit(solution)/shard_map/all_to_all | solution.py:335
  157.4 3.1 %collective-permute-start.16 = (bf16[2,192,768]{2,1,0:T(8,128)(2,1)S(1)}, bf16[2,192,768]{2,1,0:T(8,128)(2,1)S(1)}, u32[]{:S(2)}, u32[]{:S(2)}) collective-permute-start(bf16[2,192,768]{2,1,0:T(8,128)(2,1)S(1)} %dynamic-slice_bitcast_fusion), channel_id=1, source_target_pairs={{0,4},{4,0},{1,5},{5,1},{2,6},{6,2},{3,7},{7,3},{8,12},{12,8},{9,1... | collective-permute-start | bytes 1769480 | tf_op jit(solution)/shard_map/ppermute | solution.py:26
  169.1 21.0 %all-to-all-start.4 = ((bf16[8,48,768]{2,1,0:T(8,128)(2,1)}), bf16[8,48,768]{2,1,0:T(8,128)(2,1)S(1)}, u32[]{:S(2)}, u32[]{:S(2)}) async-start(bf16[8,48,768]{2,1,0:T(8,128)(2,1)} %bitcast.27), calls=%async_computation.4 | async-start | bytes 1179648 | tf_op jit(solution)/shard_map/all_to_all | solution.py:349
  179.9 33.2 %copy-start.3 = (bf16[128,1536]{1,0:T(8,128)(2,1)S(1)}, bf16[128,1536]{1,0:T(8,128)(2,1)}, u32[]{:S(2)}) copy-start(bf16[128,1536]{1,0:T(8,128)(2,1)} %copy-done.2) | copy-start | bytes 1179652
  180.1 32.7 %collective-permute-start.17 = (bf16[128,768]{1,0:T(8,128)(2,1)S(1)}, bf16[128,768]{1,0:T(8,128)(2,1)S(1)}, u32[]{:S(2)}, u32[]{:S(2)}) collective-permute-start(bf16[128,768]{1,0:T(8,128)(2,1)S(1)} %copy.24), channel_id=1, source_target_pairs={{0,64},{64,128},{128,192},{1,65},{65,129},{129,193},{2,66},{66,130... | collective-permute-start | bytes 589832 | tf_op jit(solution)/shard_map/ppermute | solution.py:21
  181.4 31.4 %collective-permute-start.18 = (bf16[128,768]{1,0:T(8,128)(2,1)S(1)}, bf16[128,768]{1,0:T(8,128)(2,1)S(1)}, u32[]{:S(2)}, u32[]{:S(2)}) collective-permute-start(bf16[128,768]{1,0:T(8,128)(2,1)S(1)} %copy.24), channel_id=1, source_target_pairs={{0,128},{64,192},{192,64},{1,129},{65,193},{193,65},{2,130},{66,19... | collective-permute-start | bytes 589832 | tf_op jit(solution)/shard_map/ppermute | solution.py:21
  186.5 26.4 %collective-permute-start.19 = (bf16[128,768]{1,0:T(8,128)(2,1)S(1)}, bf16[128,768]{1,0:T(8,128)(2,1)S(1)}, u32[]{:S(2)}, u32[]{:S(2)}) collective-permute-start(bf16[128,768]{1,0:T(8,128)(2,1)S(1)} %copy.24), channel_id=1, source_target_pairs={{0,192},{128,64},{192,128},{1,193},{129,65},{193,129},{2,194},{130... | collective-permute-start | bytes 589832 | tf_op jit(solution)/shard_map/ppermute | solution.py:21
  190.2 22.0 %collective-permute-start.20 = (bf16[48,768]{1,0:T(8,128)(2,1)S(1)}, bf16[48,768]{1,0:T(8,128)(2,1)S(1)}, u32[]{:S(2)}, u32[]{:S(2)}) collective-permute-start(bf16[48,768]{1,0:T(8,128)(2,1)S(1)} %reduce_sum.25), channel_id=1, source_target_pairs={{0,0},{16,64},{32,128},{48,192},{64,16},{80,80},{96,144},{112,208}... | collective-permute-start | bytes 221192 | tf_op jit(solution)/shard_map/ppermute | solution.py:351
Sparse Core Ops, SparseCore 0:
  13.6 63.3 all-gather.3
  80.1 51.0 all-gather.5

commit v5 on v4

--- a/solution.py
+++ b/solution.py
@@ -314,8 +314,9 @@
     heads, other_b = gate(heads, other_b)
     other_b = shift(other_b, "zl", 1)
     own_a, other_a = project(zl.reshape(1), heads, weight, 0, 2)
-    other_a, csums = gate(other_a, csums)
+    other_a, csums[1], csums[3] = gate(other_a, csums[1], csums[3])
     other_a = shift(other_a, "zl", 1)
+    own_b, csums = gate(own_b, csums)
     (out_b,) = gate(finish(2, own_b, other_b))
     parts = [send(out_b[:, :width], "grp", [(0, 2)]), send(out_b[:, width:], "grp", [(0, 3)])]
     out_a = finish(0, own_a, other_a)

time: 222 us -> 220 us (level)
    ppermute x13, waiting for transfers between devices: 31.4 us -> 26.8 us  [shift(): return lax.ppermute(value, axis, [(i, (i + step) % n) for i in range(n)])]
    all_gather x1, waiting for transfers between devices: 9.56 us -> 13.3 us  [shards(): zero_rows = lax.all_gather(slabs, ('x', 'core', 'rep'))]
  transfers between devices with their start and end apart: 28 -> 28, of which waited for: 14 -> 13; matrix products, arithmetic and copies ran while one was open for 6% -> 6% of each run, Pallas kernels for 11% -> 11%
where the time goes in v5:
time: 220 us; the launch traced here: 219 us
  waiting for transfers between devices  83.4 us (38%)
  starting transfers between devices  67.7 us (31%)
  Pallas kernels  24.5 us (11%)
  between operations  15.8 us (7%)
  other arithmetic  11.6 us (5%)
  local copies, waits for them, and re-layouts  11.5 us (5%)
  matrix products  4.66 us (2%)
    ppermute x13, waiting for transfers between devices, shift(): return lax.ppermute(value, axis, [(i, (i + step) % n) for i in range(n)])  26.8 us
    ppermute x13, starting transfers between devices, shift(): return lax.ppermute(value, axis, [(i, (i + step) % n) for i in range(n)])  19.1 us
    ppermute x1, waiting for transfers between devices, shards(): zero_slab = lax.ppermute(zero_slab, ('grp', 'x'), turn)  18.9 us
    ppermute x1, waiting for transfers between devices, shards(): grad_zero = lax.ppermute(grad, ('grp', 'x'), turn).astype(F32)  18.8 us
    all_gather x1, waiting for transfers between devices, shards(): zero_rows = lax.all_gather(slabs, ('x', 'core', 'rep'))  13.3 us
    all_to_all x1, starting transfers between devices, shards(): lax.all_to_all(halves, ('zl', 'rep'), split_axis=0, concat_axis=0, tiled=...  10.4 us
    ppermute x6, starting transfers between devices, send(): return lax.ppermute(value, axis, pairs)  10.3 us
    pallas_call x1, Pallas kernels, attend(): pl.pallas_call(functools.partial(attend_kernel, text_slots=length // 8, s...  8.42 us
  transfers between devices with their start and end apart: 28, of which 13 were waited for; matrix products, arithmetic and copies ran while one was open for 6% of the time, Pallas kernels for 11%

profile of v5, /device:TPU:193, one launch (start us, length us, event | category | flops | bytes accessed | tf_op | source)
XLA Modules:
  0.0 219.1 jit_solution(9886469868092626509)
XLA Ops:
  7.2 2.6 %copy.18 = bf16[1,1,128,2,2048]{2,4,3,1,0:T(8,128)(2,1)S(1)} copy(bf16[1,1,128,2,2048]{4,3,2,1,0:T(2,128)(2,1)} %param.10) | data formatting | bytes 2097152 | tf_op args[1]
  9.8 0.7 copy.19
  10.5 0.4 copy-done.12
  10.9 0.3 copy.20
  11.1 0.3 copy.21
  11.4 1.3 pad_maximum_fusion
  12.8 0.7 slice_select_fusion.1
  13.5 5.6 %all-to-all-start = ((bf16[16,3,128,128]{3,2,1,0:T(8,128)(2,1)}), bf16[16,3,128,128]{3,2,1,0:T(8,128)(2,1)S(1)}, u32[]{:S(2)}, u32[]{:S(2)}) async-start(bf16[16,3,128,128]{3,2,1,0:T(8,128)(2,1)} %pad_maximum_fusion), calls=%async_computation | async-start | bytes 3145728 | tf_op jit(solution)/shard_map/all_to_all | solution.py:280
  19.2 2.7 %collective-permute-start = (bf16[48,768]{1,0:T(8,128)(2,1)S(1)}, bf16[48,768]{1,0:T(8,128)(2,1)S(1)}, u32[]{:S(2)}, u32[]{:S(2)}) collective-permute-start(bf16[48,768]{1,0:T(8,128)(2,1)S(1)} %constant_dynamic-slice_fusion.4), channel_id=1, source_target_pairs={{0,0},{16,64},{32,128},{48,192},{64,16},{80,80},{96,144},{112,208}... | collective-permute-start | bytes 221192 | tf_op jit(solution)/shard_map/ppermute | solution.py:284
  21.9 18.9 %collective-permute-done = bf16[48,768]{1,0:T(8,128)(2,1)S(1)} collective-permute-done((bf16[48,768]{1,0:T(8,128)(2,1)S(1)}, bf16[48,768]{1,0:T(8,128)(2,1)S(1)}, u32[]{:S(2)}, u32[]{:S(2)}) %collective-permute-start) | collective-permute-done | bytes 73760 | tf_op jit(solution)/shard_map/ppermute | solution.py:284
  40.8 0.3 collective-permute-start.1
  41.8 2.6 %collective-permute-done.1 = bf16[48,768]{1,0:T(8,128)(2,1)S(1)} collective-permute-done((bf16[48,768]{1,0:T(8,128)(2,1)S(1)}, bf16[48,768]{1,0:T(8,128)(2,1)S(1)}, u32[]{:S(2)}, u32[]{:S(2)}) %collective-permute-start.1) | collective-permute-done | bytes 73760 | tf_op jit(solution)/shard_map/ppermute | solution.py:26
  44.4 0.7 pad_maximum_fusion.2
  45.3 6.0 %collective-permute-start.3 = (bf16[128,768]{1,0:T(8,128)(2,1)S(1)}, bf16[128,768]{1,0:T(8,128)(2,1)S(1)}, u32[]{:S(2)}, u32[]{:S(2)}) collective-permute-start(bf16[128,768]{1,0:T(8,128)(2,1)S(1)} %get-tuple-element.98), channel_id=1, source_target_pairs={{0,128},{64,192},{128,0},{192,64},{1,129},{65,193},{129,1},{193,65... | collective-permute-start | bytes 589832 | tf_op jit(solution)/shard_map/ppermute | solution.py:26
  51.3 8.4 %attend.1 = bf16[4,2,2,128,128]{4,3,2,1,0:T(8,128)(2,1)} custom-call(s32[1,1]{1,0:T(1,128)S(6)} %copy.32.tlen_ref, bf16[16,3,128,128]{3,2,1,0:T(8,128)(2,1)} %copy-done.5, bf16[16,3,128,128]{3,2,1,0:T(8,128)(2,1)} %copy-done.5, bf16[16,3,128,128]{3,2,1,0:T(8,128)(2,1)} %copy-done.5), custom_call_target="tpu_custom_call" | custom-call | flops 3221225472 | bytes 2097152 | tf_op jit(solution)/shard_map/attend/pallas_call | solution.py:65
  59.7 3.0 %collective-permute-done.3 = bf16[128,768]{1,0:T(8,128)(2,1)S(1)} collective-permute-done((bf16[128,768]{1,0:T(8,128)(2,1)S(1)}, bf16[128,768]{1,0:T(8,128)(2,1)S(1)}, u32[]{:S(2)}, u32[]{:S(2)}) %collective-permute-start.3) | collective-permute-done | bytes 196640 | tf_op jit(solution)/shard_map/ppermute | solution.py:26
  62.7 6.5 %collective-permute-done.4 = bf16[128,768]{1,0:T(8,128)(2,1)S(1)} collective-permute-done((bf16[128,768]{1,0:T(8,128)(2,1)S(1)}, bf16[128,768]{1,0:T(8,128)(2,1)S(1)}, u32[]{:S(2)}, u32[]{:S(2)}) %collective-permute-start.4) | collective-permute-done | bytes 196640 | tf_op jit(solution)/shard_map/ppermute | solution.py:26
  69.3 6.0 %all-to-all-start.1 = ((bf16[8,256,128]{2,1,0:T(8,128)(2,1)}), bf16[8,256,128]{2,1,0:T(8,128)(2,1)S(1)}, u32[]{:S(2)}, u32[]{:S(2)}) async-start(bf16[8,256,128]{2,1,0:T(8,128)(2,1)} %bitcast.69), calls=%async_computation.1 | async-start | bytes 1048576 | tf_op jit(solution)/shard_map/all_to_all | solution.py:301
  75.3 0.2 add_convert_fusion.3
  75.4 2.2 %collective-permute-start.5 = (bf16[128,768]{1,0:T(8,128)(2,1)S(1)}, bf16[128,768]{1,0:T(8,128)(2,1)S(1)}, u32[]{:S(2)}, u32[]{:S(2)}) collective-permute-start(bf16[128,768]{1,0:T(8,128)(2,1)S(1)} %add_convert_fusion.3), channel_id=1, source_target_pairs={{0,64},{64,128},{128,192},{192,0},{1,65},{65,129},{129,193},{193,1... | collective-permute-start | bytes 589832 | tf_op jit(solution)/shard_map/ppermute | solution.py:26
  77.7 0.2 collective-permute-start.6
  77.9 3.8 %collective-permute-start.8 = (bf16[128,768]{1,0:T(8,128)(2,1)S(1)}, bf16[128,768]{1,0:T(8,128)(2,1)S(1)}, u32[]{:S(2)}, u32[]{:S(2)}) collective-permute-start(bf16[128,768]{1,0:T(8,128)(2,1)S(1)} %add_convert_fusion.3), channel_id=1, source_target_pairs={{0,128},{64,192},{128,0},{192,64},{1,129},{65,193},{129,1},{193,65... | collective-permute-start | bytes 589832 | tf_op jit(solution)/shard_map/ppermute | solution.py:26
  82.3 0.9 dynamic-slice_reduce_fusion.1
  83.3 1.5 all-to-all-done.1.a_ref
  84.8 0.8 copy-done.1
  85.6 4.1 %project.2 = (f32[128,1536]{1,0:T(8,128)}, bf16[128,1536]{1,0:T(8,128)(2,1)}) custom-call(s32[1]{0:T(128)} %bitcast.2.zl_ref, bf16[8,256,128]{2,1,0:T(8,128)(2,1)} %copy-done.1, bf16[8,4,128,768]{3,2,1,0:T(8,128)(2,1)} %bitcast.57), custom_call_target="tpu_custom_call" | custom-call | flops 805306368 | bytes 3145728 | tf_op jit(solution)/shard_map/project/pallas_call | solution.py:120
  89.7 4.1 %project.3 = (f32[128,1536]{1,0:T(8,128)}, bf16[128,1536]{1,0:T(8,128)(2,1)}) custom-call(s32[1]{0:T(128)} %bitcast.2.zl_ref, bf16[8,256,128]{2,1,0:T(8,128)(2,1)} %copy-done.1, bf16[8,4,128,768]{3,2,1,0:T(8,128)(2,1)} %bitcast.58), custom_call_target="tpu_custom_call" | custom-call | flops 805306368 | bytes 3145728 | tf_op jit(solution)/shard_map/project/pallas_call | solution.py:120
  93.8 0.3 collective-permute-done.6
  94.2 1.5 collective-permute-start.9
  95.8 1.0 pad_maximum_fusion.1.csum_ref
  96.8 4.3 %all-to-all-start.2 = ((bf16[4,128,768]{2,1,0:T(8,128)(2,1)}), bf16[4,128,768]{2,1,0:T(8,128)(2,1)S(1)}, u32[]{:S(2)}, u32[]{:S(2)}) async-start(bf16[4,128,768]{2,1,0:T(8,128)(2,1)} %pad_maximum_fusion.1.csum_ref), calls=%async_computation.2 | async-start | bytes 1572864 | tf_op jit(solution)/shard_map/all_to_all | solution.py:326
  101.0 3.7 %collective-permute-done.7 = bf16[128,1536]{1,0:T(8,128)(2,1)S(1)} collective-permute-done((bf16[128,1536]{1,0:T(8,128)(2,1)}, bf16[128,1536]{1,0:T(8,128)(2,1)S(1)}, u32[]{:S(2)}, u32[]{:S(2)}) %collective-permute-start.7) | collective-permute-done | bytes 393248 | tf_op jit(solution)/shard_map/ppermute | solution.py:26
  104.8 8.5 %collective-permute-done.9 = bf16[128,1536]{1,0:T(8,128)(2,1)} collective-permute-done((bf16[128,1536]{1,0:T(8,128)(2,1)}, bf16[128,1536]{1,0:T(8,128)(2,1)}, u32[]{:S(2)}, u32[]{:S(2)}) %collective-permute-start.9) | collective-permute-done | bytes 393248 | tf_op jit(solution)/shard_map/ppermute | solution.py:26
  113.3 1.7 add_convert_fusion.2
  115.1 1.3 collective-permute-start.10
  116.4 0.7 collective-permute-start.11
  117.1 0.7 collective-permute-start.12
  117.7 13.3 %all-gather.6.cloned.1.call-done = bf16[64,48,768]{2,1,0:T(8,128)(2,1)} async-done(((bf16[2,48,768]{2,1,0:T(8,128)(2,1)}), bf16[64,48,768]{2,1,0:T(8,128)(2,1)}) %all-gather.6.cloned.1.call-update) | async-done | bytes 4718608 | tf_op jit(solution)/shard_map/all_gather | solution.py:299
  131.1 5.0 %copy.22 = bf16[4,2,2,4,48,768]{5,4,3,2,1,0:T(8,128)(2,1)} copy(bf16[4,2,2,4,48,768]{5,4,1,3,2,0:T(8,128)(2,1)} %bitcast.59) | data formatting | bytes 9437184 | tf_op jit(solution)/shard_map/transpose | solution.py:331
  136.2 4.7 %fusion = bf16[4,128,768]{1,2,0:T(8,128)(2,1)} fusion(bf16[4,768,768]{2,1,0:T(8,128)(2,1)} %bitcast.56, bf16[128,768]{1,0:T(8,128)(2,1)S(1)} %fusion.4.refs_0_), kind=kOutput, calls=%fused_computation.3 | convolution fusion | flops 604372992 | bytes 5701632 | tf_op jit(solution)/shard_map/tr,brc->btc/dot_general | solution.py:334
  140.8 0.9 collective-permute-start.13
  141.7 2.4 %collective-permute-start.14 = (bf16[128,768]{1,0:T(8,128)(2,1)S(1)}, bf16[128,768]{1,0:T(8,128)(2,1)S(1)}, u32[]{:S(2)}, u32[]{:S(2)}) collective-permute-start(bf16[128,768]{1,0:T(8,128)(2,1)S(1)} %fusion.4.refs_0_), channel_id=1, source_target_pairs={{0,32},{16,48},{32,0},{48,16},{1,33},{17,49},{33,1},{49,17},{2,34}... | collective-permute-start | bytes 589832 | tf_op jit(solution)/shard_map/ppermute | solution.py:26
  144.1 0.5 collective-permute-start.15
  144.6 6.5 %all-to-all-start.3 = ((bf16[4,128,768]{1,2,0:T(8,128)(2,1)}), bf16[4,128,768]{1,2,0:T(8,128)(2,1)}, u32[]{:S(2)}, u32[]{:S(2)}) async-start(bf16[4,128,768]{1,2,0:T(8,128)(2,1)} %fusion), calls=%async_computation.3 | async-start | bytes 1572864 | tf_op jit(solution)/shard_map/all_to_all | solution.py:336
  151.0 2.0 collective-permute-done.14.refs_2_
  153.0 1.9 grad_partial.1
  155.0 1.2 collective-permute-start.16
  156.3 1.7 select_add_fusion.cot_ref
  157.9 0.9 fusion.2
  158.9 6.0 %control_gradient.1 = bf16[128,768]{1,0:T(8,128)(2,1)} custom-call(bf16[4,128,768]{2,1,0:T(8,128)(2,1)} %pad_maximum_fusion.1.csum_ref, bf16[128,768]{1,0:T(8,128)(2,1)} %select_add_fusion.cot_ref, bf16[4,2,4,2,48,768]{5,4,3,2,1,0:T(8,128)(2,1)} %bitcast.60), custom_call_target="tpu_custom_call" | custom-call | flops 603979776 | bytes 4718592 | tf_op jit(solution)/shard_map/control_gradient/pallas_call | solution.py:190
  164.9 1.6 all-to-all-done.3
  166.4 1.3 reduce_sum.24
  167.7 10.4 %all-to-all-start.4 = ((bf16[8,48,768]{2,1,0:T(8,128)(2,1)}), bf16[8,48,768]{2,1,0:T(8,128)(2,1)S(1)}, u32[]{:S(2)}, u32[]{:S(2)}) async-start(bf16[8,48,768]{2,1,0:T(8,128)(2,1)} %bitcast.27), calls=%async_computation.4 | async-start | bytes 1179648 | tf_op jit(solution)/shard_map/all_to_all | solution.py:350
  178.1 0.1 copy.24
  178.3 1.3 collective-permute-start.17
  179.6 4.4 %collective-permute-start.18 = (bf16[128,768]{1,0:T(8,128)(2,1)S(1)}, bf16[128,768]{1,0:T(8,128)(2,1)S(1)}, u32[]{:S(2)}, u32[]{:S(2)}) collective-permute-start(bf16[128,768]{1,0:T(8,128)(2,1)S(1)} %copy.24), channel_id=1, source_target_pairs={{0,128},{64,192},{192,64},{1,129},{65,193},{193,65},{2,130},{66,19... | collective-permute-start | bytes 589832 | tf_op jit(solution)/shard_map/ppermute | solution.py:21
  184.0 1.9 collective-permute-start.19
  185.9 2.4 %all-to-all-done.4 = bf16[8,48,768]{2,1,0:T(8,128)(2,1)S(1)} async-done(((bf16[8,48,768]{2,1,0:T(8,128)(2,1)}), bf16[8,48,768]{2,1,0:T(8,128)(2,1)S(1)}, u32[]{:S(2)}, u32[]{:S(2)}) %all-to-all-start.4) | async-done | bytes 589856 | tf_op jit(solution)/shard_map/all_to_all | solution.py:350
  188.4 2.9 %collective-permute-start.20 = (bf16[48,768]{1,0:T(8,128)(2,1)S(1)}, bf16[48,768]{1,0:T(8,128)(2,1)S(1)}, u32[]{:S(2)}, u32[]{:S(2)}) collective-permute-start(bf16[48,768]{1,0:T(8,128)(2,1)S(1)} %reduce_sum.25), channel_id=1, source_target_pairs={{0,0},{16,64},{32,128},{48,192},{64,16},{80,80},{96,144},{112,208}... | collective-permute-start | bytes 221192 | tf_op jit(solution)/shard_map/ppermute | solution.py:352
  191.3 18.8 %collective-permute-done.20 = bf16[48,768]{1,0:T(8,128)(2,1)S(1)} collective-permute-done((bf16[48,768]{1,0:T(8,128)(2,1)S(1)}, bf16[48,768]{1,0:T(8,128)(2,1)S(1)}, u32[]{:S(2)}, u32[]{:S(2)}) %collective-permute-start.20) | collective-permute-done | bytes 73760 | tf_op jit(solution)/shard_map/ppermute | solution.py:352
  210.2 0.7 convert_element_type.111
  210.9 0.1 copy.27
  211.0 0.1 select_bitcast_fusion.3
  211.1 1.1 fusion.1
  (59 shorter events, 0.7 us)
Async XLA Ops:
  7.2 12.0 %copy-start = (bf16[192,768]{1,0:T(8,128)(2,1)S(1)}, bf16[192,768]{1,0:T(8,128)(2,1)}, u32[]{:S(2)}) copy-start(bf16[192,768]{1,0:T(8,128)(2,1)} %param.16) | copy-start | bytes 884740
  7.2 77.6 %all-gather.4.cloned.1.call-start = ((), (), s32[]{:S(2)}) async-start(), calls=%async_computation.5 | async-start | bytes 6488064 | tf_op jit(solution)/shard_map/all_gather | solution.py:278
  9.8 1.0 copy-start.12
  11.4 1.4 copy-start.13
  13.5 31.6 %copy-start.6 = (bf16[1,1,128,3072]{3,2,1,0:T(8,128)(2,1)S(1)}, bf16[1,1,128,3072]{3,2,1,0:T(8,128)(2,1)}, u32[]{:S(2)}) copy-start(bf16[1,1,128,3072]{3,2,1,0:T(8,128)(2,1)} %param.17) | copy-start | bytes 2359300
  13.5 31.6 %all-to-all-start = ((bf16[16,3,128,128]{3,2,1,0:T(8,128)(2,1)}), bf16[16,3,128,128]{3,2,1,0:T(8,128)(2,1)S(1)}, u32[]{:S(2)}, u32[]{:S(2)}) async-start(bf16[16,3,128,128]{3,2,1,0:T(8,128)(2,1)} %pad_maximum_fusion), calls=%async_computation | async-start | bytes 3145728 | tf_op jit(solution)/shard_map/all_to_all | solution.py:280
  19.1 111.9 %all-gather.6.cloned.1.call-start = ((), (), s32[]{:S(2)}) async-start(), calls=%async_computation.6 | async-start | bytes 4866048 | tf_op jit(solution)/shard_map/all_gather | solution.py:299
  19.2 21.6 %collective-permute-start = (bf16[48,768]{1,0:T(8,128)(2,1)S(1)}, bf16[48,768]{1,0:T(8,128)(2,1)S(1)}, u32[]{:S(2)}, u32[]{:S(2)}) collective-permute-start(bf16[48,768]{1,0:T(8,128)(2,1)S(1)} %constant_dynamic-slice_fusion.4), channel_id=1, source_target_pairs={{0,0},{16,64},{32,128},{48,192},{64,16},{80,80},{96,144},{112,208}... | collective-permute-start | bytes 221192 | tf_op jit(solution)/shard_map/ppermute | solution.py:284
  40.8 3.6 %collective-permute-start.1 = (bf16[48,768]{1,0:T(8,128)(2,1)S(1)}, bf16[48,768]{1,0:T(8,128)(2,1)S(1)}, u32[]{:S(2)}, u32[]{:S(2)}) collective-permute-start(bf16[48,768]{1,0:T(8,128)(2,1)S(1)} %collective-permute-done), channel_id=1, source_target_pairs={{0,8},{8,0},{1,9},{9,1},{2,10},{10,2},{3,11},{11,3},{4,12},{12,4},... | collective-permute-start | bytes 221192 | tf_op jit(solution)/shard_map/ppermute | solution.py:26
  45.1 6.2 %copy-start.5 = (bf16[16,3,128,128]{3,2,1,0:T(8,128)(2,1)}, bf16[16,3,128,128]{3,2,1,0:T(8,128)(2,1)S(1)}, u32[]{:S(2)}) copy-start(bf16[16,3,128,128]{3,2,1,0:T(8,128)(2,1)S(1)} %all-to-all-done.q_ref.k_ref.v_ref) | copy-start | bytes 4718596
  45.2 30.1 %copy-start.4 = (bf16[128,768]{1,0:T(8,128)(2,1)}, bf16[128,768]{1,0:T(8,128)(2,1)S(1)}, u32[]{:S(2)}) copy-start(bf16[128,768]{1,0:T(8,128)(2,1)S(1)} %get-tuple-element.54) | copy-start | bytes 589828
  45.2 14.5 %collective-permute-start.2 = (bf16[128,768]{1,0:T(8,128)(2,1)S(1)}, bf16[128,768]{1,0:T(8,128)(2,1)S(1)}, u32[]{:S(2)}, u32[]{:S(2)}) collective-permute-start(bf16[128,768]{1,0:T(8,128)(2,1)S(1)} %get-tuple-element.99), channel_id=1, source_target_pairs={{0,64},{64,128},{128,192},{192,0},{1,65},{65,129},{129,193},{193,1... | collective-permute-start | bytes 589832 | tf_op jit(solution)/shard_map/ppermute | solution.py:26
  45.3 17.4 %collective-permute-start.3 = (bf16[128,768]{1,0:T(8,128)(2,1)S(1)}, bf16[128,768]{1,0:T(8,128)(2,1)S(1)}, u32[]{:S(2)}, u32[]{:S(2)}) collective-permute-start(bf16[128,768]{1,0:T(8,128)(2,1)S(1)} %get-tuple-element.98), channel_id=1, source_target_pairs={{0,128},{64,192},{128,0},{192,64},{1,129},{65,193},{129,1},{193,65... | collective-permute-start | bytes 589832 | tf_op jit(solution)/shard_map/ppermute | solution.py:26
  51.3 18.0 %collective-permute-start.4 = (bf16[128,768]{1,0:T(8,128)(2,1)S(1)}, bf16[128,768]{1,0:T(8,128)(2,1)S(1)}, u32[]{:S(2)}, u32[]{:S(2)}) collective-permute-start(bf16[128,768]{1,0:T(8,128)(2,1)S(1)} %get-tuple-element.97), channel_id=1, source_target_pairs={{0,192},{64,0},{128,64},{192,128},{1,193},{65,1},{129,65},{193,129... | collective-permute-start | bytes 589832 | tf_op jit(solution)/shard_map/ppermute | solution.py:26
  59.7 30.0 %copy-start.9 = (bf16[128,768]{1,0:T(8,128)(2,1)}, bf16[128,768]{1,0:T(8,128)(2,1)S(1)}, u32[]{:S(2)}) copy-start(bf16[128,768]{1,0:T(8,128)(2,1)S(1)} %collective-permute-done.2) | copy-start | bytes 589828
  62.7 27.0 %copy-start.10 = (bf16[128,768]{1,0:T(8,128)(2,1)}, bf16[128,768]{1,0:T(8,128)(2,1)S(1)}, u32[]{:S(2)}) copy-start(bf16[128,768]{1,0:T(8,128)(2,1)S(1)} %collective-permute-done.3) | copy-start | bytes 589828
  69.2 20.5 %copy-start.11 = (bf16[128,768]{1,0:T(8,128)(2,1)}, bf16[128,768]{1,0:T(8,128)(2,1)S(1)}, u32[]{:S(2)}) copy-start(bf16[128,768]{1,0:T(8,128)(2,1)S(1)} %collective-permute-done.4) | copy-start | bytes 589828
  69.3 15.5 %all-to-all-start.1 = ((bf16[8,256,128]{2,1,0:T(8,128)(2,1)}), bf16[8,256,128]{2,1,0:T(8,128)(2,1)S(1)}, u32[]{:S(2)}, u32[]{:S(2)}) async-start(bf16[8,256,128]{2,1,0:T(8,128)(2,1)} %bitcast.69), calls=%async_computation.1 | async-start | bytes 1048576 | tf_op jit(solution)/shard_map/all_to_all | solution.py:301
  75.4 18.4 %collective-permute-start.5 = (bf16[128,768]{1,0:T(8,128)(2,1)S(1)}, bf16[128,768]{1,0:T(8,128)(2,1)S(1)}, u32[]{:S(2)}, u32[]{:S(2)}) collective-permute-start(bf16[128,768]{1,0:T(8,128)(2,1)S(1)} %add_convert_fusion.3), channel_id=1, source_target_pairs={{0,64},{64,128},{128,192},{192,0},{1,65},{65,129},{129,193},{193,1... | collective-permute-start | bytes 589832 | tf_op jit(solution)/shard_map/ppermute | solution.py:26
  77.7 16.5 %collective-permute-start.6 = (bf16[128,768]{1,0:T(8,128)(2,1)S(1)}, bf16[128,768]{1,0:T(8,128)(2,1)S(1)}, u32[]{:S(2)}, u32[]{:S(2)}) collective-permute-start(bf16[128,768]{1,0:T(8,128)(2,1)S(1)} %add_convert_fusion.3), channel_id=1, source_target_pairs={{0,192},{64,0},{128,64},{192,128},{1,193},{65,1},{129,65},{193,129... | collective-permute-start | bytes 589832 | tf_op jit(solution)/shard_map/ppermute | solution.py:26
  77.9 16.3 %collective-permute-start.8 = (bf16[128,768]{1,0:T(8,128)(2,1)S(1)}, bf16[128,768]{1,0:T(8,128)(2,1)S(1)}, u32[]{:S(2)}, u32[]{:S(2)}) collective-permute-start(bf16[128,768]{1,0:T(8,128)(2,1)S(1)} %add_convert_fusion.3), channel_id=1, source_target_pairs={{0,128},{64,192},{128,0},{192,64},{1,129},{65,193},{129,1},{193,65... | collective-permute-start | bytes 589832 | tf_op jit(solution)/shard_map/ppermute | solution.py:26
  84.8 0.8 copy-start.1
  94.2 10.6 %collective-permute-start.7 = (bf16[128,1536]{1,0:T(8,128)(2,1)}, bf16[128,1536]{1,0:T(8,128)(2,1)S(1)}, u32[]{:S(2)}, u32[]{:S(2)}) collective-permute-start(bf16[128,1536]{1,0:T(8,128)(2,1)} %get-tuple-element.58), channel_id=1, source_target_pairs={{0,8},{8,0},{1,9},{9,1},{2,10},{10,2},{3,11},{11,3},{4,12},{12,4},... | collective-permute-start | bytes 1179656 | tf_op jit(solution)/shard_map/ppermute | solution.py:26
  94.2 19.1 %collective-permute-start.9 = (bf16[128,1536]{1,0:T(8,128)(2,1)}, bf16[128,1536]{1,0:T(8,128)(2,1)}, u32[]{:S(2)}, u32[]{:S(2)}) collective-permute-start(bf16[128,1536]{1,0:T(8,128)(2,1)} %get-tuple-element.63), channel_id=1, source_target_pairs={{0,8},{8,0},{1,9},{9,1},{2,10},{10,2},{3,11},{11,3},{4,12},{12,4},... | collective-permute-start | bytes 1179656 | tf_op jit(solution)/shard_map/ppermute | solution.py:26
  95.7 17.6 %copy-start.7 = (bf16[1,1,128,3072]{3,2,1,0:T(8,128)(2,1)S(1)}, bf16[1,1,128,3072]{3,2,1,0:T(8,128)(2,1)}, u32[]{:S(2)}) copy-start(bf16[1,1,128,3072]{3,2,1,0:T(8,128)(2,1)} %param.9) | copy-start | bytes 2359300
  95.7 17.6 %copy-start.8 = (f32[128,1536]{1,0:T(8,128)S(1)}, f32[128,1536]{1,0:T(8,128)}, u32[]{:S(2)}) copy-start(f32[128,1536]{1,0:T(8,128)} %get-tuple-element.62) | copy-start | bytes 2359300
  96.8 39.4 %all-to-all-start.2 = ((bf16[4,128,768]{2,1,0:T(8,128)(2,1)}), bf16[4,128,768]{2,1,0:T(8,128)(2,1)S(1)}, u32[]{:S(2)}, u32[]{:S(2)}) async-start(bf16[4,128,768]{2,1,0:T(8,128)(2,1)} %pad_maximum_fusion.1.csum_ref), calls=%async_computation.2 | async-start | bytes 1572864 | tf_op jit(solution)/shard_map/all_to_all | solution.py:326
  104.8 8.5 %copy-start.14 = (bf16[128,1536]{1,0:T(8,128)(2,1)}, bf16[128,1536]{1,0:T(8,128)(2,1)S(1)}, u32[]{:S(2)}) copy-start(bf16[128,1536]{1,0:T(8,128)(2,1)S(1)} %collective-permute-done.7) | copy-start | bytes 1179652
  115.0 21.1 %copy-start.2 = (bf16[128,1536]{1,0:T(8,128)(2,1)}, bf16[128,1536]{1,0:T(8,128)(2,1)S(1)}, u32[]{:S(2)}) copy-start(bf16[128,1536]{1,0:T(8,128)(2,1)S(1)} %get-tuple-element.96) | copy-start | bytes 1179652
  115.1 21.0 %collective-permute-start.10 = (bf16[128,768]{1,0:T(8,128)(2,1)S(1)}, bf16[128,768]{1,0:T(8,128)(2,1)S(1)}, u32[]{:S(2)}, u32[]{:S(2)}) collective-permute-start(bf16[128,768]{1,0:T(8,128)(2,1)S(1)} %get-tuple-element.102), channel_id=1, source_target_pairs={{0,192},{1,193},{2,194},{3,195},{4,196},{5,197},{6,198},{7,199},{8... | collective-permute-start | bytes 589832 | tf_op jit(solution)/shard_map/ppermute | solution.py:21
  116.4 19.7 %collective-permute-start.11 = (bf16[128,768]{1,0:T(8,128)(2,1)S(1)}, bf16[128,768]{1,0:T(8,128)(2,1)S(1)}, u32[]{:S(2)}, u32[]{:S(2)}) collective-permute-start(bf16[128,768]{1,0:T(8,128)(2,1)S(1)} %get-tuple-element.101), channel_id=1, source_target_pairs={{0,128},{1,129},{2,130},{3,131},{4,132},{5,133},{6,134},{7,135},{8... | collective-permute-start | bytes 589832 | tf_op jit(solution)/shard_map/ppermute | solution.py:21
  117.1 19.1 %collective-permute-start.12 = (bf16[128,768]{1,0:T(8,128)(2,1)S(1)}, bf16[128,768]{1,0:T(8,128)(2,1)S(1)}, u32[]{:S(2)}, u32[]{:S(2)}) collective-permute-start(bf16[128,768]{1,0:T(8,128)(2,1)S(1)} %slice.44), channel_id=1, source_target_pairs={{0,64},{1,65},{2,66},{3,67},{4,68},{5,69},{6,70},{7,71},{8,72},{9,... | collective-permute-start | bytes 589832 | tf_op jit(solution)/shard_map/ppermute | solution.py:21
  140.8 10.2 %collective-permute-start.13 = (bf16[128,768]{1,0:T(8,128)(2,1)S(1)}, bf16[128,768]{1,0:T(8,128)(2,1)S(1)}, u32[]{:S(2)}, u32[]{:S(2)}) collective-permute-start(bf16[128,768]{1,0:T(8,128)(2,1)S(1)} %fusion.4.refs_0_), channel_id=1, source_target_pairs={{0,16},{16,32},{32,48},{48,0},{1,17},{17,33},{33,49},{49,1},{2,18}... | collective-permute-start | bytes 589832 | tf_op jit(solution)/shard_map/ppermute | solution.py:26
  141.7 11.3 %collective-permute-start.14 = (bf16[128,768]{1,0:T(8,128)(2,1)S(1)}, bf16[128,768]{1,0:T(8,128)(2,1)S(1)}, u32[]{:S(2)}, u32[]{:S(2)}) collective-permute-start(bf16[128,768]{1,0:T(8,128)(2,1)S(1)} %fusion.4.refs_0_), channel_id=1, source_target_pairs={{0,32},{16,48},{32,0},{48,16},{1,33},{17,49},{33,1},{49,17},{2,34}... | collective-permute-start | bytes 589832 | tf_op jit(solution)/shard_map/ppermute | solution.py:26
  144.1 9.0 %collective-permute-start.15 = (bf16[128,768]{1,0:T(8,128)(2,1)S(1)}, bf16[128,768]{1,0:T(8,128)(2,1)S(1)}, u32[]{:S(2)}, u32[]{:S(2)}) collective-permute-start(bf16[128,768]{1,0:T(8,128)(2,1)S(1)} %fusion.4.refs_0_), channel_id=1, source_target_pairs={{0,48},{16,0},{32,16},{48,32},{1,49},{17,1},{33,17},{49,33},{2,50}... | collective-permute-start | bytes 589832 | tf_op jit(solution)/shard_map/ppermute | solution.py:26
  144.6 21.9 %all-to-all-start.3 = ((bf16[4,128,768]{1,2,0:T(8,128)(2,1)}), bf16[4,128,768]{1,2,0:T(8,128)(2,1)}, u32[]{:S(2)}, u32[]{:S(2)}) async-start(bf16[4,128,768]{1,2,0:T(8,128)(2,1)} %fusion), calls=%async_computation.3 | async-start | bytes 1572864 | tf_op jit(solution)/shard_map/all_to_all | solution.py:336
  155.0 2.9 %collective-permute-start.16 = (bf16[2,192,768]{2,1,0:T(8,128)(2,1)S(1)}, bf16[2,192,768]{2,1,0:T(8,128)(2,1)S(1)}, u32[]{:S(2)}, u32[]{:S(2)}) collective-permute-start(bf16[2,192,768]{2,1,0:T(8,128)(2,1)S(1)} %dynamic-slice_bitcast_fusion), channel_id=1, source_target_pairs={{0,4},{4,0},{1,5},{5,1},{2,6},{6,2},{3,7},{7,3},{8,12},{12,8},{9,1... | collective-permute-start | bytes 1769480 | tf_op jit(solution)/shard_map/ppermute | solution.py:26
  167.7 20.6 %all-to-all-start.4 = ((bf16[8,48,768]{2,1,0:T(8,128)(2,1)}), bf16[8,48,768]{2,1,0:T(8,128)(2,1)S(1)}, u32[]{:S(2)}, u32[]{:S(2)}) async-start(bf16[8,48,768]{2,1,0:T(8,128)(2,1)} %bitcast.27), calls=%async_computation.4 | async-start | bytes 1179648 | tf_op jit(solution)/shard_map/all_to_all | solution.py:350
  178.1 33.0 %copy-start.3 = (bf16[128,1536]{1,0:T(8,128)(2,1)S(1)}, bf16[128,1536]{1,0:T(8,128)(2,1)}, u32[]{:S(2)}) copy-start(bf16[128,1536]{1,0:T(8,128)(2,1)} %copy-done.2) | copy-start | bytes 1179652
  178.3 32.6 %collective-permute-start.17 = (bf16[128,768]{1,0:T(8,128)(2,1)S(1)}, bf16[128,768]{1,0:T(8,128)(2,1)S(1)}, u32[]{:S(2)}, u32[]{:S(2)}) collective-permute-start(bf16[128,768]{1,0:T(8,128)(2,1)S(1)} %copy.24), channel_id=1, source_target_pairs={{0,64},{64,128},{128,192},{1,65},{65,129},{129,193},{2,66},{66,130... | collective-permute-start | bytes 589832 | tf_op jit(solution)/shard_map/ppermute | solution.py:21
  179.6 31.3 %collective-permute-start.18 = (bf16[128,768]{1,0:T(8,128)(2,1)S(1)}, bf16[128,768]{1,0:T(8,128)(2,1)S(1)}, u32[]{:S(2)}, u32[]{:S(2)}) collective-permute-start(bf16[128,768]{1,0:T(8,128)(2,1)S(1)} %copy.24), channel_id=1, source_target_pairs={{0,128},{64,192},{192,64},{1,129},{65,193},{193,65},{2,130},{66,19... | collective-permute-start | bytes 589832 | tf_op jit(solution)/shard_map/ppermute | solution.py:21
  184.0 26.9 %collective-permute-start.19 = (bf16[128,768]{1,0:T(8,128)(2,1)S(1)}, bf16[128,768]{1,0:T(8,128)(2,1)S(1)}, u32[]{:S(2)}, u32[]{:S(2)}) collective-permute-start(bf16[128,768]{1,0:T(8,128)(2,1)S(1)} %copy.24), channel_id=1, source_target_pairs={{0,192},{128,64},{192,128},{1,193},{129,65},{193,129},{2,194},{130... | collective-permute-start | bytes 589832 | tf_op jit(solution)/shard_map/ppermute | solution.py:21
  188.4 21.8 %collective-permute-start.20 = (bf16[48,768]{1,0:T(8,128)(2,1)S(1)}, bf16[48,768]{1,0:T(8,128)(2,1)S(1)}, u32[]{:S(2)}, u32[]{:S(2)}) collective-permute-start(bf16[48,768]{1,0:T(8,128)(2,1)S(1)} %reduce_sum.25), channel_id=1, source_target_pairs={{0,0},{16,64},{32,128},{48,192},{64,16},{80,80},{96,144},{112,208}... | collective-permute-start | bytes 221192 | tf_op jit(solution)/shard_map/ppermute | solution.py:352
Sparse Core Ops, SparseCore 0:
  13.6 63.3 all-gather.3
  80.1 50.8 all-gather.5

commit v6 on v5

--- a/solution.py
+++ b/solution.py
@@ -131,7 +131,7 @@
             pltpu.VMEM((heads, count, depth, width), BF),
             pltpu.SemaphoreType.DMA((heads + 1,)),
         ],
-        compiler_params=pltpu.CompilerParams(vmem_limit_bytes=60 * MIB),
+        compiler_params=pltpu.CompilerParams(vmem_limit_bytes=16 * MIB),
         cost_estimate=pl.CostEstimate(
             flops=2 * rows * heads * HEAD * count * width,
             bytes_accessed=2 * heads * HEAD * count * width,
@@ -196,7 +196,7 @@
             pltpu.VMEM((4, 2, 2, reps, slab, width), BF),
             pltpu.SemaphoreType.DMA((4, 2, reps)),
         ],
-        compiler_params=pltpu.CompilerParams(vmem_limit_bytes=60 * MIB),
+        compiler_params=pltpu.CompilerParams(vmem_limit_bytes=16 * MIB),
         cost_estimate=pl.CostEstimate(
             flops=8 * shape[-2] * width * width, bytes_accessed=8 * width * width, transcendentals=0
         ),
@@ -236,7 +236,7 @@
             pltpu.VMEM(csum.shape, BF),
             pltpu.SemaphoreType.DMA((5,)),
         ],
-        compiler_params=pltpu.CompilerParams(vmem_limit_bytes=40 * MIB),
+        compiler_params=pltpu.CompilerParams(vmem_limit_bytes=16 * MIB),
         cost_estimate=pl.CostEstimate(
             flops=8 * rows * width * width, bytes_accessed=18 * rows * width, transcendentals=0
         ),

time: 220 us -> 221 us (level)
  local copies, waits for them, and re-layouts: 11.5 us -> 16.6 us
  waiting for transfers between devices: 83.4 us -> 80.4 us
    unnamed x32 -> x40, local copies, waits for them, and re-layouts: 4.1 us -> 9.28 us
    all_to_all x1, starting transfers between devices: 10.4 us -> 7.61 us  [shards(): lax.all_to_all(halves, ('zl', 'rep'), split_axis=0, concat_axis=0, tiled=...]
    pallas_call x2, Pallas kernels: 8.17 us -> 5.5 us  [project(): pl.pallas_call(functools.partial(project_kernel, first=first), in_specs=[...]
where the time goes in v6:
time: 221 us; the launch traced here: 220 us
  waiting for transfers between devices  80.4 us (36%)
  starting transfers between devices  67.6 us (31%)
  Pallas kernels  23.5 us (11%)
  local copies, waits for them, and re-layouts  16.6 us (8%)
  between operations  15.8 us (7%)
  other arithmetic  11.1 us (5%)
  matrix products  4.66 us (2%)
    ppermute x13, waiting for transfers between devices, shift(): return lax.ppermute(value, axis, [(i, (i + step) % n) for i in range(n)])  27.6 us
    ppermute x13, starting transfers between devices, shift(): return lax.ppermute(value, axis, [(i, (i + step) % n) for i in range(n)])  19.1 us
    ppermute x1, waiting for transfers between devices, shards(): zero_slab = lax.ppermute(zero_slab, ('grp', 'x'), turn)  18.9 us
    ppermute x1, waiting for transfers between devices, shards(): grad_zero = lax.ppermute(grad, ('grp', 'x'), turn).astype(F32)  17.5 us
    all_gather x1, waiting for transfers between devices, shards(): zero_rows = lax.all_gather(slabs, ('x', 'core', 'rep'))  12.8 us
    ppermute x6, starting transfers between devices, send(): return lax.ppermute(value, axis, pairs)  10.7 us
    unnamed x40, local copies, waits for them, and re-layouts  9.28 us
    pallas_call x1, Pallas kernels, attend(): pl.pallas_call(functools.partial(attend_kernel, text_slots=length // 8, s...  8.42 us
  transfers between devices with their start and end apart: 28, of which 13 were waited for; matrix products, arithmetic and copies ran while one was open for 6% of the time, Pallas kernels for 11%

profile of v6, /device:TPU:193, one launch (start us, length us, event | category | flops | bytes accessed | tf_op | source)
XLA Modules:
  0.0 219.7 jit_solution(772477119580880089)
XLA Ops:
  7.2 2.6 %copy.18 = bf16[1,1,128,2,2048]{2,4,3,1,0:T(8,128)(2,1)S(1)} copy(bf16[1,1,128,2,2048]{4,3,2,1,0:T(2,128)(2,1)} %param.10) | data formatting | bytes 2097152 | tf_op args[1]
  9.8 0.7 copy.19
  10.5 0.4 copy-done.17
  10.9 0.3 copy.20
  11.1 0.3 copy.21
  11.4 1.3 pad_maximum_fusion
  12.8 0.7 slice_select_fusion.1
  13.5 5.6 %all-to-all-start = ((bf16[16,3,128,128]{3,2,1,0:T(8,128)(2,1)}), bf16[16,3,128,128]{3,2,1,0:T(8,128)(2,1)S(1)}, u32[]{:S(2)}, u32[]{:S(2)}) async-start(bf16[16,3,128,128]{3,2,1,0:T(8,128)(2,1)} %pad_maximum_fusion), calls=%async_computation | async-start | bytes 3145728 | tf_op jit(solution)/shard_map/all_to_all | solution.py:280
  19.2 2.7 %collective-permute-start = (bf16[48,768]{1,0:T(8,128)(2,1)S(1)}, bf16[48,768]{1,0:T(8,128)(2,1)S(1)}, u32[]{:S(2)}, u32[]{:S(2)}) collective-permute-start(bf16[48,768]{1,0:T(8,128)(2,1)S(1)} %constant_dynamic-slice_fusion.4), channel_id=1, source_target_pairs={{0,0},{16,64},{32,128},{48,192},{64,16},{80,80},{96,144},{112,208}... | collective-permute-start | bytes 221192 | tf_op jit(solution)/shard_map/ppermute | solution.py:284
  21.8 18.9 %collective-permute-done = bf16[48,768]{1,0:T(8,128)(2,1)S(1)} collective-permute-done((bf16[48,768]{1,0:T(8,128)(2,1)S(1)}, bf16[48,768]{1,0:T(8,128)(2,1)S(1)}, u32[]{:S(2)}, u32[]{:S(2)}) %collective-permute-start) | collective-permute-done | bytes 73760 | tf_op jit(solution)/shard_map/ppermute | solution.py:284
  40.8 0.3 collective-permute-start.1
  41.8 2.6 %collective-permute-done.1 = bf16[48,768]{1,0:T(8,128)(2,1)S(1)} collective-permute-done((bf16[48,768]{1,0:T(8,128)(2,1)S(1)}, bf16[48,768]{1,0:T(8,128)(2,1)S(1)}, u32[]{:S(2)}, u32[]{:S(2)}) %collective-permute-start.1) | collective-permute-done | bytes 73760 | tf_op jit(solution)/shard_map/ppermute | solution.py:26
  44.4 0.7 pad_maximum_fusion.2
  45.3 6.0 %collective-permute-start.3 = (bf16[128,768]{1,0:T(8,128)(2,1)S(1)}, bf16[128,768]{1,0:T(8,128)(2,1)S(1)}, u32[]{:S(2)}, u32[]{:S(2)}) collective-permute-start(bf16[128,768]{1,0:T(8,128)(2,1)S(1)} %get-tuple-element.98), channel_id=1, source_target_pairs={{0,128},{64,192},{128,0},{192,64},{1,129},{65,193},{129,1},{193,65... | collective-permute-start | bytes 589832 | tf_op jit(solution)/shard_map/ppermute | solution.py:26
  51.2 8.4 %attend.1 = bf16[4,2,2,128,128]{4,3,2,1,0:T(8,128)(2,1)} custom-call(s32[1,1]{1,0:T(1,128)S(6)} %copy.32.tlen_ref, bf16[16,3,128,128]{3,2,1,0:T(8,128)(2,1)} %copy-done.11, bf16[16,3,128,128]{3,2,1,0:T(8,128)(2,1)} %copy-done.11, bf16[16,3,128,128]{3,2,1,0:T(8,128)(2,1)} %copy-done.11), custom_call_target="tpu_custom_call" | custom-call | flops 3221225472 | bytes 2097152 | tf_op jit(solution)/shard_map/attend/pallas_call | solution.py:65
  59.7 3.0 %collective-permute-done.3 = bf16[128,768]{1,0:T(8,128)(2,1)S(1)} collective-permute-done((bf16[128,768]{1,0:T(8,128)(2,1)S(1)}, bf16[128,768]{1,0:T(8,128)(2,1)S(1)}, u32[]{:S(2)}, u32[]{:S(2)}) %collective-permute-start.3) | collective-permute-done | bytes 196640 | tf_op jit(solution)/shard_map/ppermute | solution.py:26
  62.7 6.5 %collective-permute-done.4 = bf16[128,768]{1,0:T(8,128)(2,1)S(1)} collective-permute-done((bf16[128,768]{1,0:T(8,128)(2,1)S(1)}, bf16[128,768]{1,0:T(8,128)(2,1)S(1)}, u32[]{:S(2)}, u32[]{:S(2)}) %collective-permute-start.4) | collective-permute-done | bytes 196640 | tf_op jit(solution)/shard_map/ppermute | solution.py:26
  69.2 6.0 %all-to-all-start.1 = ((bf16[8,256,128]{2,1,0:T(8,128)(2,1)}), bf16[8,256,128]{2,1,0:T(8,128)(2,1)S(1)}, u32[]{:S(2)}, u32[]{:S(2)}) async-start(bf16[8,256,128]{2,1,0:T(8,128)(2,1)} %bitcast.69), calls=%async_computation.1 | async-start | bytes 1048576 | tf_op jit(solution)/shard_map/all_to_all | solution.py:301
  75.3 0.2 add_convert_fusion.3
  75.4 2.2 %collective-permute-start.5 = (bf16[128,768]{1,0:T(8,128)(2,1)S(1)}, bf16[128,768]{1,0:T(8,128)(2,1)S(1)}, u32[]{:S(2)}, u32[]{:S(2)}) collective-permute-start(bf16[128,768]{1,0:T(8,128)(2,1)S(1)} %add_convert_fusion.3), channel_id=1, source_target_pairs={{0,64},{64,128},{128,192},{192,0},{1,65},{65,129},{129,193},{193,1... | collective-permute-start | bytes 589832 | tf_op jit(solution)/shard_map/ppermute | solution.py:26
  77.7 0.2 collective-permute-start.6
  77.9 3.8 %collective-permute-start.8 = (bf16[128,768]{1,0:T(8,128)(2,1)S(1)}, bf16[128,768]{1,0:T(8,128)(2,1)S(1)}, u32[]{:S(2)}, u32[]{:S(2)}) collective-permute-start(bf16[128,768]{1,0:T(8,128)(2,1)S(1)} %add_convert_fusion.3), channel_id=1, source_target_pairs={{0,128},{64,192},{128,0},{192,64},{1,129},{65,193},{129,1},{193,65... | collective-permute-start | bytes 589832 | tf_op jit(solution)/shard_map/ppermute | solution.py:26
  82.3 0.9 dynamic-slice_reduce_fusion.1
  83.2 1.5 all-to-all-done.1.a_ref
  84.8 2.8 %copy-done.1 = bf16[32,128,768]{2,1,0:T(8,128)(2,1)S(1)} copy-done((bf16[32,128,768]{2,1,0:T(8,128)(2,1)S(1)}, bf16[32,128,768]{2,1,0:T(8,128)(2,1)}, u32[]{:S(2)}) %copy-start.1) | copy-done | bytes 6291480
  87.5 2.7 %project.2 = (f32[128,1536]{1,0:T(8,128)S(1)}, bf16[128,1536]{1,0:T(8,128)(2,1)S(1)}) custom-call(s32[1]{0:T(128)} %bitcast.2.zl_ref, bf16[8,256,128]{2,1,0:T(8,128)(2,1)S(1)} %all-to-all-done.1.a_ref, bf16[8,4,128,768]{3,2,1,0:T(8,128)(2,1)S(1)} %bitcast.54), custom_call_target="tpu_custom_call" | custom-call | flops 805306368 | bytes 3145728 | tf_op jit(solution)/shard_map/project/pallas_call | solution.py:120
  90.3 2.8 %project.3 = (f32[128,1536]{1,0:T(8,128)S(1)}, bf16[128,1536]{1,0:T(8,128)(2,1)S(1)}) custom-call(s32[1]{0:T(128)} %bitcast.2.zl_ref, bf16[8,256,128]{2,1,0:T(8,128)(2,1)S(1)} %all-to-all-done.1.a_ref, bf16[8,4,128,768]{3,2,1,0:T(8,128)(2,1)S(1)} %bitcast.55), custom_call_target="tpu_custom_call" | custom-call | flops 805306368 | bytes 3145728 | tf_op jit(solution)/shard_map/project/pallas_call | solution.py:120
  93.1 0.9 copy-done.3
  93.9 0.2 collective-permute-done.6
  94.1 1.5 collective-permute-start.9
  95.7 1.0 pad_maximum_fusion.1.csum_ref
  96.7 4.3 %all-to-all-start.2 = ((bf16[4,128,768]{2,1,0:T(8,128)(2,1)}), bf16[4,128,768]{2,1,0:T(8,128)(2,1)S(1)}, u32[]{:S(2)}, u32[]{:S(2)}) async-start(bf16[4,128,768]{2,1,0:T(8,128)(2,1)} %pad_maximum_fusion.1.csum_ref), calls=%async_computation.2 | async-start | bytes 1572864 | tf_op jit(solution)/shard_map/all_to_all | solution.py:326
  101.0 4.2 %collective-permute-done.7 = bf16[128,1536]{1,0:T(8,128)(2,1)} collective-permute-done((bf16[128,1536]{1,0:T(8,128)(2,1)S(1)}, bf16[128,1536]{1,0:T(8,128)(2,1)}, u32[]{:S(2)}, u32[]{:S(2)}) %collective-permute-start.7) | collective-permute-done | bytes 393248 | tf_op jit(solution)/shard_map/ppermute | solution.py:26
  105.1 8.4 %collective-permute-done.9 = bf16[128,1536]{1,0:T(8,128)(2,1)} collective-permute-done((bf16[128,1536]{1,0:T(8,128)(2,1)S(1)}, bf16[128,1536]{1,0:T(8,128)(2,1)}, u32[]{:S(2)}, u32[]{:S(2)}) %collective-permute-start.9) | collective-permute-done | bytes 393248 | tf_op jit(solution)/shard_map/ppermute | solution.py:26
  113.6 1.9 add_convert_fusion.2
  115.6 1.3 collective-permute-start.10
  116.9 0.7 collective-permute-start.11
  117.6 0.7 collective-permute-start.12
  118.3 12.8 %all-gather.6.cloned.1.call-done = bf16[64,48,768]{2,1,0:T(8,128)(2,1)} async-done(((bf16[2,48,768]{2,1,0:T(8,128)(2,1)}), bf16[64,48,768]{2,1,0:T(8,128)(2,1)}) %all-gather.6.cloned.1.call-update) | async-done | bytes 4718608 | tf_op jit(solution)/shard_map/all_gather | solution.py:299
  131.0 5.0 %copy.22 = bf16[4,2,2,4,48,768]{5,4,3,2,1,0:T(8,128)(2,1)} copy(bf16[4,2,2,4,48,768]{5,4,1,3,2,0:T(8,128)(2,1)} %bitcast.56) | data formatting | bytes 9437184 | tf_op jit(solution)/shard_map/transpose | solution.py:331
  136.1 4.7 %fusion = bf16[4,128,768]{1,2,0:T(8,128)(2,1)} fusion(bf16[4,768,768]{2,1,0:T(8,128)(2,1)} %bitcast.60, bf16[128,768]{1,0:T(8,128)(2,1)S(1)} %fusion.4.refs_0_), kind=kOutput, calls=%fused_computation.3 | convolution fusion | flops 604372992 | bytes 5701632 | tf_op jit(solution)/shard_map/tr,brc->btc/dot_general | solution.py:334
  140.8 0.9 collective-permute-start.13
  141.7 2.4 %collective-permute-start.14 = (bf16[128,768]{1,0:T(8,128)(2,1)S(1)}, bf16[128,768]{1,0:T(8,128)(2,1)S(1)}, u32[]{:S(2)}, u32[]{:S(2)}) collective-permute-start(bf16[128,768]{1,0:T(8,128)(2,1)S(1)} %fusion.4.refs_0_), channel_id=1, source_target_pairs={{0,32},{16,48},{32,0},{48,16},{1,33},{17,49},{33,1},{49,17},{2,34}... | collective-permute-start | bytes 589832 | tf_op jit(solution)/shard_map/ppermute | solution.py:26
  144.0 0.5 collective-permute-start.15
  144.5 6.5 %all-to-all-start.3 = ((bf16[4,128,768]{1,2,0:T(8,128)(2,1)}), bf16[4,128,768]{1,2,0:T(8,128)(2,1)}, u32[]{:S(2)}, u32[]{:S(2)}) async-start(bf16[4,128,768]{1,2,0:T(8,128)(2,1)} %fusion), calls=%async_computation.3 | async-start | bytes 1572864 | tf_op jit(solution)/shard_map/all_to_all | solution.py:336
  151.0 2.0 collective-permute-done.14.refs_2_
  153.0 2.0 grad_partial.1
  155.0 1.2 collective-permute-start.16
  156.3 1.0 select_add_fusion.cot_ref
  157.2 0.6 collective-permute-done.16
  157.9 1.0 fusion.2
  158.8 2.3 %copy-done.2 = bf16[64,48,768]{2,1,0:T(8,128)(2,1)S(1)} copy-done((bf16[64,48,768]{2,1,0:T(8,128)(2,1)S(1)}, bf16[64,48,768]{2,1,0:T(8,128)(2,1)}, u32[]{:S(2)}) %copy-start.2) | copy-done | bytes 4718616
  161.2 7.6 %control_gradient.1 = bf16[128,768]{1,0:T(8,128)(2,1)} custom-call(bf16[4,128,768]{2,1,0:T(8,128)(2,1)} %pad_maximum_fusion.1.csum_ref, bf16[128,768]{1,0:T(8,128)(2,1)S(1)} %select_add_fusion.cot_ref, bf16[4,2,4,2,48,768]{5,4,3,2,1,0:T(8,128)(2,1)S(1)} %bitcast.57), custom_call_target="tpu_custom_call" | custom-call | flops 603979776 | bytes 4718592 | tf_op jit(solution)/shard_map/control_gradient/pallas_call | solution.py:190
  168.8 1.3 reduce_sum.24
  170.1 7.6 %all-to-all-start.4 = ((bf16[8,48,768]{2,1,0:T(8,128)(2,1)}), bf16[8,48,768]{2,1,0:T(8,128)(2,1)S(1)}, u32[]{:S(2)}, u32[]{:S(2)}) async-start(bf16[8,48,768]{2,1,0:T(8,128)(2,1)} %bitcast.27), calls=%async_computation.4 | async-start | bytes 1179648 | tf_op jit(solution)/shard_map/all_to_all | solution.py:350
  177.7 0.1 copy.24
  177.9 1.4 collective-permute-start.17
  179.3 4.8 %collective-permute-start.18 = (bf16[128,768]{1,0:T(8,128)(2,1)S(1)}, bf16[128,768]{1,0:T(8,128)(2,1)S(1)}, u32[]{:S(2)}, u32[]{:S(2)}) collective-permute-start(bf16[128,768]{1,0:T(8,128)(2,1)S(1)} %copy.24), channel_id=1, source_target_pairs={{0,128},{64,192},{192,64},{1,129},{65,193},{193,65},{2,130},{66,19... | collective-permute-start | bytes 589832 | tf_op jit(solution)/shard_map/ppermute | solution.py:21
  184.1 1.9 collective-permute-start.19
  186.0 2.1 all-to-all-done.4
  188.2 5.1 %collective-permute-start.20 = (bf16[48,768]{1,0:T(8,128)(2,1)S(1)}, bf16[48,768]{1,0:T(8,128)(2,1)S(1)}, u32[]{:S(2)}, u32[]{:S(2)}) collective-permute-start(bf16[48,768]{1,0:T(8,128)(2,1)S(1)} %reduce_sum.25), channel_id=1, source_target_pairs={{0,0},{16,64},{32,128},{48,192},{64,16},{80,80},{96,144},{112,208}... | collective-permute-start | bytes 221192 | tf_op jit(solution)/shard_map/ppermute | solution.py:352
  193.3 17.5 %collective-permute-done.20 = bf16[48,768]{1,0:T(8,128)(2,1)S(1)} collective-permute-done((bf16[48,768]{1,0:T(8,128)(2,1)S(1)}, bf16[48,768]{1,0:T(8,128)(2,1)S(1)}, u32[]{:S(2)}, u32[]{:S(2)}) %collective-permute-start.20) | collective-permute-done | bytes 73760 | tf_op jit(solution)/shard_map/ppermute | solution.py:352
  210.8 0.7 convert_element_type.111
  211.7 1.1 fusion.1
  (67 shorter events, 1.0 us)
Async XLA Ops:
  7.2 12.0 %copy-start = (bf16[192,768]{1,0:T(8,128)(2,1)S(1)}, bf16[192,768]{1,0:T(8,128)(2,1)}, u32[]{:S(2)}) copy-start(bf16[192,768]{1,0:T(8,128)(2,1)} %param.16) | copy-start | bytes 884740
  7.2 77.6 %all-gather.4.cloned.1.call-start = ((), (), s32[]{:S(2)}) async-start(), calls=%async_computation.5 | async-start | bytes 6488064 | tf_op jit(solution)/shard_map/all_gather | solution.py:278
  9.8 1.0 copy-start.17
  11.4 1.3 copy-start.18
  13.5 31.6 %copy-start.12 = (bf16[1,1,128,3072]{3,2,1,0:T(8,128)(2,1)S(1)}, bf16[1,1,128,3072]{3,2,1,0:T(8,128)(2,1)}, u32[]{:S(2)}) copy-start(bf16[1,1,128,3072]{3,2,1,0:T(8,128)(2,1)} %param.17) | copy-start | bytes 2359300
  13.5 31.6 %all-to-all-start = ((bf16[16,3,128,128]{3,2,1,0:T(8,128)(2,1)}), bf16[16,3,128,128]{3,2,1,0:T(8,128)(2,1)S(1)}, u32[]{:S(2)}, u32[]{:S(2)}) async-start(bf16[16,3,128,128]{3,2,1,0:T(8,128)(2,1)} %pad_maximum_fusion), calls=%async_computation | async-start | bytes 3145728 | tf_op jit(solution)/shard_map/all_to_all | solution.py:280
  19.1 111.9 %all-gather.6.cloned.1.call-start = ((), (), s32[]{:S(2)}) async-start(), calls=%async_computation.6 | async-start | bytes 4866048 | tf_op jit(solution)/shard_map/all_gather | solution.py:299
  19.2 21.6 %collective-permute-start = (bf16[48,768]{1,0:T(8,128)(2,1)S(1)}, bf16[48,768]{1,0:T(8,128)(2,1)S(1)}, u32[]{:S(2)}, u32[]{:S(2)}) collective-permute-start(bf16[48,768]{1,0:T(8,128)(2,1)S(1)} %constant_dynamic-slice_fusion.4), channel_id=1, source_target_pairs={{0,0},{16,64},{32,128},{48,192},{64,16},{80,80},{96,144},{112,208}... | collective-permute-start | bytes 221192 | tf_op jit(solution)/shard_map/ppermute | solution.py:284
  40.8 3.6 %collective-permute-start.1 = (bf16[48,768]{1,0:T(8,128)(2,1)S(1)}, bf16[48,768]{1,0:T(8,128)(2,1)S(1)}, u32[]{:S(2)}, u32[]{:S(2)}) collective-permute-start(bf16[48,768]{1,0:T(8,128)(2,1)S(1)} %collective-permute-done), channel_id=1, source_target_pairs={{0,8},{8,0},{1,9},{9,1},{2,10},{10,2},{3,11},{11,3},{4,12},{12,4},... | collective-permute-start | bytes 221192 | tf_op jit(solution)/shard_map/ppermute | solution.py:26
  45.1 6.2 %copy-start.11 = (bf16[16,3,128,128]{3,2,1,0:T(8,128)(2,1)}, bf16[16,3,128,128]{3,2,1,0:T(8,128)(2,1)S(1)}, u32[]{:S(2)}) copy-start(bf16[16,3,128,128]{3,2,1,0:T(8,128)(2,1)S(1)} %all-to-all-done.q_ref.k_ref.v_ref) | copy-start | bytes 4718596
  45.2 30.1 %copy-start.9 = (bf16[128,768]{1,0:T(8,128)(2,1)}, bf16[128,768]{1,0:T(8,128)(2,1)S(1)}, u32[]{:S(2)}) copy-start(bf16[128,768]{1,0:T(8,128)(2,1)S(1)} %get-tuple-element.54) | copy-start | bytes 589828
  45.2 14.5 %collective-permute-start.2 = (bf16[128,768]{1,0:T(8,128)(2,1)S(1)}, bf16[128,768]{1,0:T(8,128)(2,1)S(1)}, u32[]{:S(2)}, u32[]{:S(2)}) collective-permute-start(bf16[128,768]{1,0:T(8,128)(2,1)S(1)} %get-tuple-element.99), channel_id=1, source_target_pairs={{0,64},{64,128},{128,192},{192,0},{1,65},{65,129},{129,193},{193,1... | collective-permute-start | bytes 589832 | tf_op jit(solution)/shard_map/ppermute | solution.py:26
  45.3 17.4 %collective-permute-start.3 = (bf16[128,768]{1,0:T(8,128)(2,1)S(1)}, bf16[128,768]{1,0:T(8,128)(2,1)S(1)}, u32[]{:S(2)}, u32[]{:S(2)}) collective-permute-start(bf16[128,768]{1,0:T(8,128)(2,1)S(1)} %get-tuple-element.98), channel_id=1, source_target_pairs={{0,128},{64,192},{128,0},{192,64},{1,129},{65,193},{129,1},{193,65... | collective-permute-start | bytes 589832 | tf_op jit(solution)/shard_map/ppermute | solution.py:26
  51.2 18.0 %collective-permute-start.4 = (bf16[128,768]{1,0:T(8,128)(2,1)S(1)}, bf16[128,768]{1,0:T(8,128)(2,1)S(1)}, u32[]{:S(2)}, u32[]{:S(2)}) collective-permute-start(bf16[128,768]{1,0:T(8,128)(2,1)S(1)} %get-tuple-element.97), channel_id=1, source_target_pairs={{0,192},{64,0},{128,64},{192,128},{1,193},{65,1},{129,65},{193,129... | collective-permute-start | bytes 589832 | tf_op jit(solution)/shard_map/ppermute | solution.py:26
  59.7 25.1 %copy-start.13 = (bf16[128,768]{1,0:T(8,128)(2,1)}, bf16[128,768]{1,0:T(8,128)(2,1)S(1)}, u32[]{:S(2)}) copy-start(bf16[128,768]{1,0:T(8,128)(2,1)S(1)} %collective-permute-done.2) | copy-start | bytes 589828
  62.7 22.1 %copy-start.15 = (bf16[128,768]{1,0:T(8,128)(2,1)}, bf16[128,768]{1,0:T(8,128)(2,1)S(1)}, u32[]{:S(2)}) copy-start(bf16[128,768]{1,0:T(8,128)(2,1)S(1)} %collective-permute-done.3) | copy-start | bytes 589828
  69.2 21.1 %copy-start.16 = (bf16[128,768]{1,0:T(8,128)(2,1)}, bf16[128,768]{1,0:T(8,128)(2,1)S(1)}, u32[]{:S(2)}) copy-start(bf16[128,768]{1,0:T(8,128)(2,1)S(1)} %collective-permute-done.4) | copy-start | bytes 589828
  69.2 15.5 %all-to-all-start.1 = ((bf16[8,256,128]{2,1,0:T(8,128)(2,1)}), bf16[8,256,128]{2,1,0:T(8,128)(2,1)S(1)}, u32[]{:S(2)}, u32[]{:S(2)}) async-start(bf16[8,256,128]{2,1,0:T(8,128)(2,1)} %bitcast.69), calls=%async_computation.1 | async-start | bytes 1048576 | tf_op jit(solution)/shard_map/all_to_all | solution.py:301
  75.4 18.5 %collective-permute-start.5 = (bf16[128,768]{1,0:T(8,128)(2,1)S(1)}, bf16[128,768]{1,0:T(8,128)(2,1)S(1)}, u32[]{:S(2)}, u32[]{:S(2)}) collective-permute-start(bf16[128,768]{1,0:T(8,128)(2,1)S(1)} %add_convert_fusion.3), channel_id=1, source_target_pairs={{0,64},{64,128},{128,192},{192,0},{1,65},{65,129},{129,193},{193,1... | collective-permute-start | bytes 589832 | tf_op jit(solution)/shard_map/ppermute | solution.py:26
  77.7 16.5 %collective-permute-start.6 = (bf16[128,768]{1,0:T(8,128)(2,1)S(1)}, bf16[128,768]{1,0:T(8,128)(2,1)S(1)}, u32[]{:S(2)}, u32[]{:S(2)}) collective-permute-start(bf16[128,768]{1,0:T(8,128)(2,1)S(1)} %add_convert_fusion.3), channel_id=1, source_target_pairs={{0,192},{64,0},{128,64},{192,128},{1,193},{65,1},{129,65},{193,129... | collective-permute-start | bytes 589832 | tf_op jit(solution)/shard_map/ppermute | solution.py:26
  77.9 16.3 %collective-permute-start.8 = (bf16[128,768]{1,0:T(8,128)(2,1)S(1)}, bf16[128,768]{1,0:T(8,128)(2,1)S(1)}, u32[]{:S(2)}, u32[]{:S(2)}) collective-permute-start(bf16[128,768]{1,0:T(8,128)(2,1)S(1)} %add_convert_fusion.3), channel_id=1, source_target_pairs={{0,128},{64,192},{128,0},{192,64},{1,129},{65,193},{129,1},{193,65... | collective-permute-start | bytes 589832 | tf_op jit(solution)/shard_map/ppermute | solution.py:26
  84.8 2.8 %copy-start.1 = (bf16[32,128,768]{2,1,0:T(8,128)(2,1)S(1)}, bf16[32,128,768]{2,1,0:T(8,128)(2,1)}, u32[]{:S(2)}) copy-start(bf16[32,128,768]{2,1,0:T(8,128)(2,1)} %all-gather.4.cloned.1.call-done) | copy-start | bytes 18874372
  93.1 0.9 copy-start.3
  94.1 11.0 %collective-permute-start.7 = (bf16[128,1536]{1,0:T(8,128)(2,1)S(1)}, bf16[128,1536]{1,0:T(8,128)(2,1)}, u32[]{:S(2)}, u32[]{:S(2)}) collective-permute-start(bf16[128,1536]{1,0:T(8,128)(2,1)S(1)} %get-tuple-element.58), channel_id=1, source_target_pairs={{0,8},{8,0},{1,9},{9,1},{2,10},{10,2},{3,11},{11,3},{4,12},{12,4},... | collective-permute-start | bytes 1179656 | tf_op jit(solution)/shard_map/ppermute | solution.py:26
  94.1 19.4 %collective-permute-start.9 = (bf16[128,1536]{1,0:T(8,128)(2,1)S(1)}, bf16[128,1536]{1,0:T(8,128)(2,1)}, u32[]{:S(2)}, u32[]{:S(2)}) collective-permute-start(bf16[128,1536]{1,0:T(8,128)(2,1)S(1)} %get-tuple-element.63), channel_id=1, source_target_pairs={{0,8},{8,0},{1,9},{9,1},{2,10},{10,2},{3,11},{11,3},{4,12},{12,4},... | collective-permute-start | bytes 1179656 | tf_op jit(solution)/shard_map/ppermute | solution.py:26
  95.7 17.9 %copy-start.4 = (f32[128,1536]{1,0:T(8,128)S(1)}, f32[128,1536]{1,0:T(8,128)}, u32[]{:S(2)}) copy-start(f32[128,1536]{1,0:T(8,128)} %copy-done.3) | copy-start | bytes 2359300
  96.7 39.4 %all-to-all-start.2 = ((bf16[4,128,768]{2,1,0:T(8,128)(2,1)}), bf16[4,128,768]{2,1,0:T(8,128)(2,1)S(1)}, u32[]{:S(2)}, u32[]{:S(2)}) async-start(bf16[4,128,768]{2,1,0:T(8,128)(2,1)} %pad_maximum_fusion.1.csum_ref), calls=%async_computation.2 | async-start | bytes 1572864 | tf_op jit(solution)/shard_map/all_to_all | solution.py:326
  115.5 20.5 %copy-start.7 = (bf16[128,1536]{1,0:T(8,128)(2,1)}, bf16[128,1536]{1,0:T(8,128)(2,1)S(1)}, u32[]{:S(2)}) copy-start(bf16[128,1536]{1,0:T(8,128)(2,1)S(1)} %get-tuple-element.96) | copy-start | bytes 1179652
  115.5 20.5 %copy-start.5 = (bf16[128,1536]{1,0:T(8,128)(2,1)}, bf16[128,1536]{1,0:T(8,128)(2,1)S(1)}, u32[]{:S(2)}) copy-start(bf16[128,1536]{1,0:T(8,128)(2,1)S(1)} %get-tuple-element.95) | copy-start | bytes 1179652
  115.6 20.5 %collective-permute-start.10 = (bf16[128,768]{1,0:T(8,128)(2,1)S(1)}, bf16[128,768]{1,0:T(8,128)(2,1)S(1)}, u32[]{:S(2)}, u32[]{:S(2)}) collective-permute-start(bf16[128,768]{1,0:T(8,128)(2,1)S(1)} %get-tuple-element.102), channel_id=1, source_target_pairs={{0,192},{1,193},{2,194},{3,195},{4,196},{5,197},{6,198},{7,199},{8... | collective-permute-start | bytes 589832 | tf_op jit(solution)/shard_map/ppermute | solution.py:21
  116.9 19.2 %collective-permute-start.11 = (bf16[128,768]{1,0:T(8,128)(2,1)S(1)}, bf16[128,768]{1,0:T(8,128)(2,1)S(1)}, u32[]{:S(2)}, u32[]{:S(2)}) collective-permute-start(bf16[128,768]{1,0:T(8,128)(2,1)S(1)} %get-tuple-element.101), channel_id=1, source_target_pairs={{0,128},{1,129},{2,130},{3,131},{4,132},{5,133},{6,134},{7,135},{8... | collective-permute-start | bytes 589832 | tf_op jit(solution)/shard_map/ppermute | solution.py:21
  117.6 18.5 %collective-permute-start.12 = (bf16[128,768]{1,0:T(8,128)(2,1)S(1)}, bf16[128,768]{1,0:T(8,128)(2,1)S(1)}, u32[]{:S(2)}, u32[]{:S(2)}) collective-permute-start(bf16[128,768]{1,0:T(8,128)(2,1)S(1)} %slice.44), channel_id=1, source_target_pairs={{0,64},{1,65},{2,66},{3,67},{4,68},{5,69},{6,70},{7,71},{8,72},{9,... | collective-permute-start | bytes 589832 | tf_op jit(solution)/shard_map/ppermute | solution.py:21
  140.8 10.2 %collective-permute-start.13 = (bf16[128,768]{1,0:T(8,128)(2,1)S(1)}, bf16[128,768]{1,0:T(8,128)(2,1)S(1)}, u32[]{:S(2)}, u32[]{:S(2)}) collective-permute-start(bf16[128,768]{1,0:T(8,128)(2,1)S(1)} %fusion.4.refs_0_), channel_id=1, source_target_pairs={{0,16},{16,32},{32,48},{48,0},{1,17},{17,33},{33,49},{49,1},{2,18}... | collective-permute-start | bytes 589832 | tf_op jit(solution)/shard_map/ppermute | solution.py:26
  141.7 11.3 %collective-permute-start.14 = (bf16[128,768]{1,0:T(8,128)(2,1)S(1)}, bf16[128,768]{1,0:T(8,128)(2,1)S(1)}, u32[]{:S(2)}, u32[]{:S(2)}) collective-permute-start(bf16[128,768]{1,0:T(8,128)(2,1)S(1)} %fusion.4.refs_0_), channel_id=1, source_target_pairs={{0,32},{16,48},{32,0},{48,16},{1,33},{17,49},{33,1},{49,17},{2,34}... | collective-permute-start | bytes 589832 | tf_op jit(solution)/shard_map/ppermute | solution.py:26
  144.0 9.0 %collective-permute-start.15 = (bf16[128,768]{1,0:T(8,128)(2,1)S(1)}, bf16[128,768]{1,0:T(8,128)(2,1)S(1)}, u32[]{:S(2)}, u32[]{:S(2)}) collective-permute-start(bf16[128,768]{1,0:T(8,128)(2,1)S(1)} %fusion.4.refs_0_), channel_id=1, source_target_pairs={{0,48},{16,0},{32,16},{48,32},{1,49},{17,1},{33,17},{49,33},{2,50}... | collective-permute-start | bytes 589832 | tf_op jit(solution)/shard_map/ppermute | solution.py:26
  144.5 24.3 %all-to-all-start.3 = ((bf16[4,128,768]{1,2,0:T(8,128)(2,1)}), bf16[4,128,768]{1,2,0:T(8,128)(2,1)}, u32[]{:S(2)}, u32[]{:S(2)}) async-start(bf16[4,128,768]{1,2,0:T(8,128)(2,1)} %fusion), calls=%async_computation.3 | async-start | bytes 1572864 | tf_op jit(solution)/shard_map/all_to_all | solution.py:336
  153.0 3.3 %copy-start.10 = (bf16[128,768]{1,0:T(8,128)(2,1)S(1)}, bf16[128,768]{1,0:T(8,128)(2,1)}, u32[]{:S(2)}) copy-start(bf16[128,768]{1,0:T(8,128)(2,1)} %copy-done.9) | copy-start | bytes 589828
  153.0 3.3 %copy-start.14 = (bf16[128,768]{1,0:T(8,128)(2,1)S(1)}, bf16[128,768]{1,0:T(8,128)(2,1)}, u32[]{:S(2)}) copy-start(bf16[128,768]{1,0:T(8,128)(2,1)} %copy-done.13) | copy-start | bytes 589828
  155.0 2.9 %collective-permute-start.16 = (bf16[2,192,768]{2,1,0:T(8,128)(2,1)S(1)}, bf16[2,192,768]{2,1,0:T(8,128)(2,1)S(1)}, u32[]{:S(2)}, u32[]{:S(2)}) collective-permute-start(bf16[2,192,768]{2,1,0:T(8,128)(2,1)S(1)} %dynamic-slice_bitcast_fusion), channel_id=1, source_target_pairs={{0,4},{4,0},{1,5},{5,1},{2,6},{6,2},{3,7},{7,3},{8,12},{12,8},{9,1... | collective-permute-start | bytes 1769480 | tf_op jit(solution)/shard_map/ppermute | solution.py:26
  158.8 2.3 %copy-start.2 = (bf16[64,48,768]{2,1,0:T(8,128)(2,1)S(1)}, bf16[64,48,768]{2,1,0:T(8,128)(2,1)}, u32[]{:S(2)}) copy-start(bf16[64,48,768]{2,1,0:T(8,128)(2,1)} %all-gather.6.cloned.1.call-done) | copy-start | bytes 14155780
  170.1 18.0 %all-to-all-start.4 = ((bf16[8,48,768]{2,1,0:T(8,128)(2,1)}), bf16[8,48,768]{2,1,0:T(8,128)(2,1)S(1)}, u32[]{:S(2)}, u32[]{:S(2)}) async-start(bf16[8,48,768]{2,1,0:T(8,128)(2,1)} %bitcast.27), calls=%async_computation.4 | async-start | bytes 1179648 | tf_op jit(solution)/shard_map/all_to_all | solution.py:350
  177.7 34.0 %copy-start.6 = (bf16[128,1536]{1,0:T(8,128)(2,1)S(1)}, bf16[128,1536]{1,0:T(8,128)(2,1)}, u32[]{:S(2)}) copy-start(bf16[128,1536]{1,0:T(8,128)(2,1)} %copy-done.5) | copy-start | bytes 1179652
  177.7 34.0 %copy-start.8 = (bf16[128,1536]{1,0:T(8,128)(2,1)S(1)}, bf16[128,1536]{1,0:T(8,128)(2,1)}, u32[]{:S(2)}) copy-start(bf16[128,1536]{1,0:T(8,128)(2,1)} %copy-done.7) | copy-start | bytes 1179652
  177.9 33.6 %collective-permute-start.17 = (bf16[128,768]{1,0:T(8,128)(2,1)S(1)}, bf16[128,768]{1,0:T(8,128)(2,1)S(1)}, u32[]{:S(2)}, u32[]{:S(2)}) collective-permute-start(bf16[128,768]{1,0:T(8,128)(2,1)S(1)} %copy.24), channel_id=1, source_target_pairs={{0,64},{64,128},{128,192},{1,65},{65,129},{129,193},{2,66},{66,130... | collective-permute-start | bytes 589832 | tf_op jit(solution)/shard_map/ppermute | solution.py:21
  179.3 32.1 %collective-permute-start.18 = (bf16[128,768]{1,0:T(8,128)(2,1)S(1)}, bf16[128,768]{1,0:T(8,128)(2,1)S(1)}, u32[]{:S(2)}, u32[]{:S(2)}) collective-permute-start(bf16[128,768]{1,0:T(8,128)(2,1)S(1)} %copy.24), channel_id=1, source_target_pairs={{0,128},{64,192},{192,64},{1,129},{65,193},{193,65},{2,130},{66,19... | collective-permute-start | bytes 589832 | tf_op jit(solution)/shard_map/ppermute | solution.py:21
  184.1 27.4 %collective-permute-start.19 = (bf16[128,768]{1,0:T(8,128)(2,1)S(1)}, bf16[128,768]{1,0:T(8,128)(2,1)S(1)}, u32[]{:S(2)}, u32[]{:S(2)}) collective-permute-start(bf16[128,768]{1,0:T(8,128)(2,1)S(1)} %copy.24), channel_id=1, source_target_pairs={{0,192},{128,64},{192,128},{1,193},{129,65},{193,129},{2,194},{130... | collective-permute-start | bytes 589832 | tf_op jit(solution)/shard_map/ppermute | solution.py:21
  188.2 22.6 %collective-permute-start.20 = (bf16[48,768]{1,0:T(8,128)(2,1)S(1)}, bf16[48,768]{1,0:T(8,128)(2,1)S(1)}, u32[]{:S(2)}, u32[]{:S(2)}) collective-permute-start(bf16[48,768]{1,0:T(8,128)(2,1)S(1)} %reduce_sum.25), channel_id=1, source_target_pairs={{0,0},{16,64},{32,128},{48,192},{64,16},{80,80},{96,144},{112,208}... | collective-permute-start | bytes 221192 | tf_op jit(solution)/shard_map/ppermute | solution.py:352
Sparse Core Ops, SparseCore 0:
  13.6 63.3 all-gather.3
  80.1 50.8 all-gather.5
